TPU v7x, 256 devices: a whole 4x4x8 slice. The times are simulated.
256 devices in a mesh: ctx: 16 (over x, y_lo, core), head: 16 (over y_hi, z).
Axes of the slice: x: 4, y: 4 (y_hi: 2, y_lo: 2; y = y_hi * 2 + y_lo), z: 8, core: 2. Of those that a mesh axis runs over, the one named last changes fastest.
Arguments:
- queries: bfloat16 [5120, 7168], P('ctx', 'head'), may hold values from -40 to 40
- keys: bfloat16 [5120, 7168], P('ctx', 'head'), may hold values from -6.1 to 6.1
- values: bfloat16 [5120, 7168], P('ctx', 'head'), may hold values from -6 to 6
- out_fwd: bfloat16 [5120, 7168], P('ctx', 'head'), may hold values from -6 to 6
- d_out: bfloat16 [5120, 7168], P(('ctx', 'head')), may hold values from -6 to 6
- plan: int32 [32], replicated, may hold values from 0 to 31, as said below
Outputs:
- d_queries: bfloat16 [5120, 7168], P('ctx', 'head')
- d_keys: bfloat16 [5120, 7168], P('ctx', 'head')
- d_values: bfloat16 [5120, 7168], P('ctx', 'head')
Inputs may be any that keep to these rules, and one draw needn't show every extreme that they name: `plan`: a permutation of 0 to 31.
All inputs are finite; a program needn't handle non-finite values.
Results may differ from a plain program's by a relative error of at most 0.009.
Values may be sent and summed in bfloat16 or wider, within the bound.
No kernel may reach another device: no remote copies, remote signals or barrier semaphores. Data moves between devices by JAX's collectives and lax.ppermute only.
A program may use at most 128 MiB of HBM per device.

v0:
```python
import math

import jax
import jax.numpy as jnp
from jax import lax
from jax.sharding import PartitionSpec as P

HD = 112


def combined_all(value, axis, join):
    pieces = jax.tree.map(lambda part: lax.all_gather(part, axis), value)
    head = jax.tree.map(lambda part: part[0], pieces)
    tail = jax.tree.map(lambda part: part[1:], pieces)
    subtotal, _ = lax.scan(lambda subtotal, piece: (join(subtotal, piece), None), head, tail)
    return subtotal


def positions(plan, block):
    starts = plan * block
    return (starts[:, None] + jnp.arange(block, dtype=jnp.int32)[None, :]).reshape(-1)


def scores(query_rows, key_rows, pos_q, pos_k, slopes, scale):
    score = (
        jnp.einsum("qhd,khd->hqk", query_rows, key_rows, preferred_element_type=jnp.float32) * scale
    )
    dist = (pos_q[:, None] - pos_k[None, :]).astype(jnp.float32)
    score = score - slopes[:, None, None] * dist[None]
    visible = (pos_q[:, None] >= pos_k[None, :])[None]
    return (jnp.where(visible, score, -1e30), visible)


def partial_totals(query_rows, key_rows, pos_q, pos_k, slopes, scale):
    score, visible = scores(query_rows, key_rows, pos_q, pos_k, slopes, scale)
    top = jnp.max(score, axis=2)
    total = jnp.sum(jnp.where(visible, jnp.exp(score - top[:, :, None]), 0.0), axis=2)
    return (top, total)


def combine_totals(first, second):
    top = jnp.maximum(first[0], second[0])
    total = first[1] * jnp.exp(first[0] - top) + second[1] * jnp.exp(second[0] - top)
    return (top, total)


def block_grads(
    query_rows, grad_rows, lse_q, delta_q, key_rows, value_rows, pos_q, pos_k, slopes, scale
):
    score, visible = scores(query_rows, key_rows, pos_q, pos_k, slopes, scale)
    prob = jnp.where(visible, jnp.exp(score - lse_q[:, :, None]), 0.0)
    d_value = jnp.einsum(
        "hqk,qhd->khd", prob.astype(jnp.bfloat16), grad_rows, preferred_element_type=jnp.float32
    )
    d_prob = jnp.einsum("qhd,khd->hqk", grad_rows, value_rows, preferred_element_type=jnp.float32)
    d_score = (prob * (d_prob - delta_q[:, :, None])).astype(jnp.bfloat16)
    d_query = (
        jnp.einsum("hqk,khd->qhd", d_score, key_rows, preferred_element_type=jnp.float32) * scale
    )
    d_key = (
        jnp.einsum("hqk,qhd->khd", d_score, query_rows, preferred_element_type=jnp.float32) * scale
    )
    return (d_query, d_key, d_value)


def guarded(work, operands):
    return work(*operands)


def on_device(queries, keys, values, out_fwd, d_out, plan):
    own_rows = queries.shape[0]
    width = queries.shape[1]
    heads_dev = width // HD
    grad_local = lax.all_to_all(d_out, "head", split_axis=1, concat_axis=0, tiled=True)
    ctx_count = lax.axis_size("ctx")
    me_index = lax.axis_index("ctx")
    seq = own_rows * ctx_count
    pos_all = positions(plan, own_rows // 2)
    pos_own = lax.dynamic_slice_in_dim(pos_all, me_index * own_rows, own_rows)
    heads = heads_dev * lax.axis_size("head")
    head_ids = lax.axis_index("head") * heads_dev + jnp.arange(heads_dev, dtype=jnp.int32)
    slopes = jnp.exp2(-8.0 * (head_ids + 1).astype(jnp.float32) / heads)
    scale = 1.0 / math.sqrt(HD)
    group = 1
    while group * 2 <= ctx_count and ctx_count % (group * 2) == 0 and (group * own_rows < 512):
        group = group * 2
    rows = group * own_rows
    nblocks = ctx_count // group
    shape3 = (own_rows, heads_dev, HD)
    key_own = keys.reshape(shape3)
    value_own = values.reshape(shape3)
    delta_own = jnp.sum(
        grad_local.astype(jnp.float32).reshape(shape3)
        * out_fwd.astype(jnp.float32).reshape(shape3),
        axis=2,
    )
    query_all, grad_all = (
        lax.all_gather(queries, "ctx", axis=0, tiled=True),
        lax.all_gather(grad_local, "ctx", axis=0, tiled=True),
    )
    delta_all = lax.all_gather(delta_own, "ctx", axis=0, tiled=True)
    query_blocks = query_all.reshape(nblocks, rows, heads_dev, HD)
    grad_blocks = grad_all.reshape(nblocks, rows, heads_dev, HD)
    pos_blocks = pos_all.reshape(nblocks, rows)
    delta_blocks = jnp.transpose(delta_all.reshape(nblocks, rows, heads_dev), (0, 2, 1))

    def stats_step(item):
        query_rows, pos_q = item
        return guarded(partial_totals, (query_rows, key_own, pos_q, pos_own, slopes, scale))

    tops, totals = lax.map(stats_step, (query_blocks, pos_blocks))
    top, total = combined_all((tops, totals), "ctx", combine_totals)
    lse_blocks = top + jnp.log(total)

    def grad_step(carry, item):
        query_rows, grad_rows, pos_q, lse_q, delta_q = item
        d_query, d_key, d_value = guarded(
            block_grads,
            (
                query_rows,
                grad_rows,
                lse_q,
                delta_q,
                key_own,
                value_own,
                pos_q,
                pos_own,
                slopes,
                scale,
            ),
        )
        return ((carry[0] + d_key, carry[1] + d_value), d_query)

    start = (jnp.zeros(shape3, jnp.float32), jnp.zeros(shape3, jnp.float32))
    (d_key, d_value), query_terms = lax.scan(
        grad_step, start, (query_blocks, grad_blocks, pos_blocks, lse_blocks, delta_blocks)
    )
    d_query = lax.psum_scatter(
        query_terms.reshape(seq, width), "ctx", scatter_dimension=0, tiled=True
    )
    d_key = d_key.reshape(own_rows, width)
    d_value = d_value.reshape(own_rows, width)
    return (d_query.astype(jnp.bfloat16), d_key.astype(jnp.bfloat16), d_value.astype(jnp.bfloat16))


def solution(mesh):
    in_specs = (
        P("ctx", "head"),
        P("ctx", "head"),
        P("ctx", "head"),
        P("ctx", "head"),
        P(("ctx", "head"), None),
        P(),
    )
    out_specs = (P("ctx", "head"), P("ctx", "head"), P("ctx", "head"))
    return jax.shard_map(
        on_device, mesh=mesh, in_specs=in_specs, out_specs=out_specs, check_vma=False
    )
```

profile of v0, /device:TPU:1, one launch (start us, length us, event | category | flops | bytes accessed | tf_op | source)
XLA Modules:
  0.0 432.6 jit_solution(4280606109025059675)
XLA Ops:
  10.2 11.7 %all-to-all-start = ((bf16[20,16,448]{2,0,1:T(8,128)(2,1)}), bf16[20,16,448]{2,0,1:T(8,128)(2,1)S(1)}, u32[]{:S(2)}, u32[]{:S(2)}) async-start(bf16[20,16,448]{2,0,1:T(8,128)(2,1)} %copy.32), calls=%async_computation | async-start | bytes 786432 | tf_op jit(solution)/shard_map/all_to_all | solution.py:74
  24.7 9.5 %all-to-all-done = bf16[20,16,448]{2,0,1:T(8,128)(2,1)S(1)} async-done(((bf16[20,16,448]{2,0,1:T(8,128)(2,1)}), bf16[20,16,448]{2,0,1:T(8,128)(2,1)S(1)}, u32[]{:S(2)}, u32[]{:S(2)}) %all-to-all-start) | async-done | bytes 286752 | tf_op jit(solution)/shard_map/all_to_all | solution.py:74
  35.1 23.2 %all-gather.8.cloned.1.call-done = bf16[5120,448]{1,0:T(8,128)(2,1)} async-done(((bf16[320,448]{1,0:T(8,128)(2,1)}), bf16[5120,448]{1,0:T(8,128)(2,1)}) %all-gather.8.cloned.1.call-update) | async-done | bytes 4587536 | tf_op jit(solution)/shard_map/all_gather | solution.py:98
  58.4 9.3 %reshape.193 = bf16[8,640,4,112]{3,2,1,0:T(4,128)(2,1)} reshape(bf16[5120,448]{1,0:T(8,128)(2,1)} %all-gather.8.cloned.1.call-done) | data formatting | bytes 9175040 | tf_op jit(solution)/shard_map/reshape | solution.py:102
  67.6 8.7 %copy.37 = bf16[8,640,4,112]{1,3,2,0:T(8,128)(2,1)} copy(bf16[8,640,4,112]{3,2,1,0:T(4,128)(2,1)} %reshape.193) | data formatting | bytes 9175040
  76.4 33.2 %while.41 = (s32[]{:T(128)}, f32[8,4,640]{2,1,0:T(4,128)S(1)}, f32[8,4,640]{2,1,0:T(4,128)}, s32[8,640]{1,0:T(8,128)S(1)}, s32[320]{0:T(512)S(1)}, /*index=5*/bf...) while((s32[]{:T(128)}, f32[8,4,640]{2,1,0:T(4,128)S(1)}, ...), condition=%wide.region_3.4_spmd.clone, body=%wide.region_0.3_spmd.clone.sunk | while | flops 193940496 | bytes 10570405 | solution.py:111
  76.7 2.1 fusion.59
  80.9 2.1 fusion.59
  85.0 2.1 fusion.59
  89.2 2.1 fusion.59
  93.3 2.1 fusion.59
  97.5 2.1 fusion.59
  101.6 2.1 fusion.59
  105.8 2.1 fusion.59
  115.8 18.5 %all-gather.2 = f32[16,320,4]{1,2,0:T(4,128)S(1)} all-gather(f32[1,320,4]{1,2,0:T(4,128)S(1)} %copy.35), channel_id=1, replica_groups=mesh['ctx'=16,'head'=16] {'ctx'}, dimensions={0}, use_global_device_ids=true | all-gather | bytes 87040 | tf_op jit(solution)/shard_map/all_gather | solution.py:101
  134.5 9.3 %reshape.194 = bf16[8,640,4,112]{3,2,1,0:T(4,128)(2,1)} reshape(bf16[5120,448]{1,0:T(8,128)(2,1)} %all-gather.10.cloned.1.call-done) | data formatting | bytes 9175040 | tf_op jit(solution)/shard_map/reshape | solution.py:103
  143.8 8.8 %copy.39 = bf16[8,640,4,112]{1,3,2,0:T(8,128)(2,1)} copy(bf16[8,640,4,112]{3,2,1,0:T(4,128)(2,1)} %reshape.194) | data formatting | bytes 9175040
  153.5 29.9 %all-gather.14.cloned.1.call-done = f32[128,4,640]{2,1,0:T(4,128)} async-done(((f32[8,4,640]{2,1,0:T(4,128)}), f32[128,4,640]{2,1,0:T(4,128)}) %all-gather.14.cloned.1.call-update) | async-done | bytes 1310736 | tf_op jit(solution)/shard_map/all_gather | solution.py:12
  184.3 2.5 slice.23
  186.8 15.1 %while.40 = (s32[]{:T(128)}, f32[8,4,640]{2,1,0:T(4,128)S(1)}, f32[8,4,640]{2,1,0:T(4,128)S(1)}, f32[15,8,4,640]{3,2,1,0:T(4,128)S(1)}, f32[15,8,4,640]{3,2,1,0:T(4,128)}, /*index=5*/s32[]{:T(128)}) while((s32[]{:T(128)}, f32[8,4,640]{2,1,0:T(4,128)S(1)}, f32[8,4,640]{2,1,0:T(4,128)S(1)}, f32[15,8,4,640]{3,2,1,0:T(4,128)S(1)}, ...), condition=%wide.region_5.6_spmd, body=%wide.region_4.5_spmd.sunk | while | flops 122882 | bytes 491601 | solution.py:15
  201.9 77.3 %while.42 = (s32[]{:T(128)}, f32[320,4,112]{2,0,1:T(8,128)S(1)}, f32[320,4,112]{2,0,1:T(8,128)S(1)}, f32[8,640,4,112]{1,3,2,0:T(8,128)}, bf16[8,640,4,112]{1,3,2...) while((s32[]{:T(128)}, f32[320,4,112]{2,0,1:T(8,128)S(1)}, ...), condition=%wide.region_8.9_spmd.clone, body=%wide.region_7.8_spmd.clone.sunk | while | flops 927313920 | bytes 23483108 | solution.py:135
  202.3 2.3 exponential_select_fusion.2
  212.0 2.3 exponential_select_fusion.2
  221.6 2.3 exponential_select_fusion.2
  231.3 2.3 exponential_select_fusion.2
  241.0 2.3 exponential_select_fusion.2
  250.6 2.3 exponential_select_fusion.2
  260.3 2.3 exponential_select_fusion.2
  269.9 2.3 exponential_select_fusion.2
  279.2 11.8 %copy.53 = f32[8,640,4,112]{3,2,1,0:T(4,128)} copy(f32[8,640,4,112]{1,3,2,0:T(8,128)} %get-tuple-element.147) | data formatting | bytes 18350080
  291.0 13.0 %reshape.195 = f32[5120,448]{1,0:T(8,128)} reshape(f32[8,640,4,112]{3,2,1,0:T(4,128)} %copy.53) | data formatting | bytes 18350080
  306.5 117.4 %reduce-scatter.4.cloned.1.call-done = f32[320,448]{1,0:T(8,128)} async-done(((f32[5120,448]{1,0:T(8,128)}), f32[320,448]{1,0:T(8,128)}) %reduce-scatter.4.cloned.1.call-update) | async-done | bytes 573456
  (211 shorter events, 108.7 us)
Async XLA Ops:
  7.2 51.2 %all-gather.8.cloned.1.call-start = ((), (), s32[]{:S(2)}) async-start(), calls=%async_computation.2 | async-start | bytes 5570560 | tf_op jit(solution)/shard_map/all_gather | solution.py:98
  10.2 24.0 %all-to-all-start = ((bf16[20,16,448]{2,0,1:T(8,128)(2,1)}), bf16[20,16,448]{2,0,1:T(8,128)(2,1)S(1)}, u32[]{:S(2)}, u32[]{:S(2)}) async-start(bf16[20,16,448]{2,0,1:T(8,128)(2,1)} %copy.32), calls=%async_computation | async-start | bytes 786432 | tf_op jit(solution)/shard_map/all_to_all | solution.py:74
  22.0 112.5 %all-gather.10.cloned.1.call-start = ((), (), s32[]{:S(2)}) async-start(), calls=%async_computation.3 | async-start | bytes 5570560 | tf_op jit(solution)/shard_map/all_gather | solution.py:99
  35.1 117.5 %all-gather.12.cloned.1.call-start = ((), (), s32[]{:S(2)}) async-start(), calls=%async_computation.4 | async-start | bytes 1392640 | tf_op jit(solution)/shard_map/all_gather | solution.py:12
  76.4 34.5 %copy-start = (bf16[320,448]{1,0:T(8,128)(2,1)S(1)}, bf16[320,448]{1,0:T(8,128)(2,1)}, u32[]{:S(2)}) copy-start(bf16[320,448]{1,0:T(8,128)(2,1)} %param.14) | copy-start | bytes 860164
  76.4 35.0 %copy-start.1 = (bf16[320,448]{1,0:T(8,128)(2,1)S(1)}, bf16[320,448]{1,0:T(8,128)(2,1)}, u32[]{:S(2)}) copy-start(bf16[320,448]{1,0:T(8,128)(2,1)} %param.15) | copy-start | bytes 860164
  109.6 0.6 copy-start.2
  110.2 73.2 %all-gather.14.cloned.1.call-start = ((), (), s32[]{:S(2)}) async-start(), calls=%async_computation.5 | async-start | bytes 1392640 | tf_op jit(solution)/shard_map/all_gather | solution.py:12
  110.8 313.1 %reduce-scatter.4.cloned.1.call-start = ((), (), s32[]{:S(2)}) async-start(), calls=%async_computation.6 | async-start | bytes 11141120
  152.6 34.3 %slice-start = ((f32[128,4,640]{2,1,0:T(4,128)}), f32[120,4,640]{2,1,0:T(4,128)S(1)}, s32[]{:S(2)}) async-start(f32[128,4,640]{2,1,0:T(4,128)} %all-gather.12.cloned.1.call-done), calls=%async_computation.7 | async-start | bytes 2457600 | tf_op jit(solution)/shard_map/slice | solution.py:14
Sparse Core Ops, SparseCore 0:
  9.8 48.4 all-gather.7
  60.8 41.7 all-gather.9
  110.3 35.2 all-gather.11
  148.0 35.4 all-gather.13
  304.1 119.7 reduce-scatter.3
where the time goes:
time: 437 us; the launch traced here: 433 us
  waiting for transfers between devices  181 us (41%)
  matrix products  90.5 us (21%)
  local copies, waits for them, and re-layouts  84.2 us (19%)
  other arithmetic  31.4 us (7%)
  blocking collectives  18.5 us (4%)
  between operations  13.9 us (3%)
  starting transfers between devices  12 us (3%)
    unnamed x6, waiting for transfers between devices  119 us
    unnamed x17, local copies, waits for them, and re-layouts  47.1 us
    dot_general x16, matrix products, scores(): jnp.einsum('qhd,khd->hqk', query_rows, key_rows, preferred_element_type=j...  35.5 us
    all_gather x2, waiting for transfers between devices, combined_all(): pieces = jax.tree.map(lambda part: lax.all_gather(part, axis), value)  29.9 us
    all_gather x1, waiting for transfers between devices, on_device(): lax.all_gather(queries, 'ctx', axis=0, tiled=True)  23.2 us
    all_gather x1, blocking collectives, on_device(): delta_all = lax.all_gather(delta_own, 'ctx', axis=0, tiled=True)  18.5 us
    add x15, other arithmetic, combine_totals(): first[1] * jnp.exp(first[0] - top) + second[1] * jnp.exp(second[0] - top)  15 us
    dot_general x8, matrix products, block_grads(): jnp.einsum('hqk,qhd->khd', d_score, query_rows, preferred_element_type=jn...  14.4 us
  transfers between devices with their start and end apart: 6, of which 4 were waited for; matrix products, arithmetic and copies ran while one was open for 19% of the time, Pallas kernels for 0%

commit v1 on v0

v1 whole, which is shorter than its diff:
```python
import functools
import math

import jax
import jax.numpy as jnp
from jax import lax
from jax.experimental import pallas as pl
from jax.experimental.pallas import tpu as pltpu
from jax.sharding import Mesh, PartitionSpec as P

HD = 112
W = 128
NX = 4
BLK = 160
OWN = 2 * BLK
QT = 256
QROWS = NX * OWN
NQT = QROWS // QT
HALF = 16 * BLK
KC = 256
SCALE = 1.0 / math.sqrt(HD)
LOG2E = math.log2(math.e)
CEXP = SCALE * LOG2E
NEG = -1e30
LIMIT = 56 * 1024 * 1024
F32 = jnp.float32
BF16 = jnp.bfloat16

VM = pl.BlockSpec(memory_space=pltpu.VMEM)
SM = pl.BlockSpec(memory_space=pltpu.SMEM)


def call(kernel, outs, scratch, name):
    def run(*args):
        specs = [SM if a.dtype == jnp.int32 or a.size <= 8 else VM for a in args]
        return pl.pallas_call(
            kernel,
            out_shape=[jax.ShapeDtypeStruct(s, d) for s, d in outs],
            in_specs=specs,
            out_specs=[VM] * len(outs),
            scratch_shapes=scratch,
            compiler_params=pltpu.CompilerParams(vmem_limit_bytes=LIMIT),
            name=name,
        )(*args)

    return run


def ctx_of(ids, s, dyl, dc):
    x = lax.rem(ids[0] + (NX - s), NX)
    yl = ids[1] if dyl == 0 else 1 - ids[1]
    c = ids[2] if dc == 0 else 1 - ids[2]
    return x * 4 + yl * 2 + c


def cotangent_pack_kernel(d_ref, out_ref):
    out_ref[:, :, HD:] = jnp.zeros((64, 20, W - HD), BF16)
    for n in range(64):
        out_ref[(n % NX) * 16 + n // NX, :, :HD] = d_ref[:, n * HD : (n + 1) * HD]


def pack_kernel(ids, tables, q_ref, k_ref, v_ref, o_ref, *rest):
    kv = rest[0:4]
    qo = rest[4:8]
    skv, sqo = rest[8], rest[9]
    ctx = ctx_of(ids, 0, 0, 0)
    row = lax.broadcasted_iota(jnp.int32, (OWN, W - HD), 0)
    lane = lax.broadcasted_iota(jnp.int32, (OWN, W - HD), 1)
    first, second = tables[3, 2 * ctx] * BLK, tables[3, 2 * ctx + 1] * BLK
    pos = jnp.where(row < BLK, first + row, second + row - BLK)
    high = (pos // 64) * 64
    low = pos - high
    one = jnp.where(lane < 9, 1, 0)
    kx = jnp.where(lane < 3, high, jnp.where(lane < 6, low, one)).astype(F32).astype(BF16)
    vx = jnp.where(lane < 3, 1.0, 0.0).astype(BF16)
    zx = jnp.zeros((OWN, W - HD), BF16)
    for n in range(NX):
        cols = slice(n * HD, (n + 1) * HD)
        skv[n, :OWN, :HD] = k_ref[:, cols]
        skv[n, :OWN, HD:] = kx
        skv[n, OWN:, :HD] = v_ref[:, cols]
        skv[n, OWN:, HD:] = vx
        sqo[n, :OWN, :HD] = q_ref[:, cols]
        sqo[n, :OWN, HD:] = zx
        sqo[n, OWN:, :HD] = o_ref[:, cols]
        sqo[n, OWN:, HD:] = zx
    for s in range(NX):
        head = lax.rem(ids[0] + s, NX)
        kv[s][...] = skv[head]
        qo[s][...] = sqo[head]


def at(start, size):
    return pl.ds(pl.multiple_of(start, 32), size)


def split3(value):
    a = value.astype(BF16)
    r = value - a.astype(F32)
    b = r.astype(BF16)
    return a, b, (r - b.astype(F32)).astype(BF16)


def sort_keys(ids, tables, pieces, dyl, dst, first):
    for s in range(NX):
        for dc in range(2):
            ctx = ctx_of(ids, s, dyl, dc)
            for h in range(2):
                rank = tables[0, 2 * ctx + h]
                dst[at(rank * BLK, BLK), :] = pieces[s * 2 + dc][
                    first + h * BLK : first + (h + 1) * BLK, :
                ]


def sort_rows(ids, tables, blocks, dst):
    for s in range(NX):
        ctx = ctx_of(ids, s, 0, 0)
        for h in range(2):
            dst[at(tables[1, 2 * ctx + h] * BLK, BLK), :] = blocks(s, h)


def sort_limits(ids, tables, limits):
    for s in range(NX):
        ctx = ctx_of(ids, s, 0, 0)
        for h in range(2):
            r = tables[1, 2 * ctx + h]
            limits[0, r] = tables[0, 2 * ctx + h]
            limits[1, r] = tables[2, 2 * ctx + h]


def tile_limits(limits, i, dyl):
    b0, b1 = (QT * i) // BLK, (QT * i + QT - 1) // BLK
    row = lax.broadcasted_iota(jnp.int32, (1, QT), 1) + QT * i
    lim = jnp.zeros((1, QT), jnp.int32)
    for b in range(b0, b1 + 1):
        inside = jnp.logical_and(row >= b * BLK, row < (b + 1) * BLK)
        if dyl == 0:
            value = limits[0, b] * BLK + (row - b * BLK)
        else:
            value = jnp.broadcast_to(limits[1, b] * BLK - 1, (1, QT))
        lim = jnp.where(inside, value, lim)
    full = lax.div(limits[dyl, b0] * BLK, KC)
    last = limits[dyl, b1] * BLK + (BLK if dyl == 0 else 0)
    return lim, full, lax.div(last + KC - 1, KC)


def stats_kernel(ids, tables, slope, *rest):
    kown, koth = rest[0:8], rest[8:16]
    qo = rest[16:20]
    qs, qt = rest[20:22]
    keys, limits = rest[22:24]
    sort_keys(ids, tables, kown, 0, keys.at[0], 0)
    sort_keys(ids, tables, koth, 1, keys.at[1], 0)
    sort_rows(ids, tables, lambda s, h: qo[s][h * BLK : (h + 1) * BLK, :], qs)
    sort_limits(ids, tables, limits)
    m1, m2, m3 = split3(jnp.full((1, QT), slope[0] / SCALE, F32))
    for i in range(NQT):
        cols = slice(i * QT, (i + 1) * QT)
        qt[:, cols] = qs[cols, :].T
        qt[HD : HD + 16, cols] = jnp.concatenate(
            [m1, m2, m3, m1, m2, m3, jnp.zeros((10, QT), BF16)], axis=0
        )
        qti = qt[:, cols]
        state = (jnp.full((8, QT), NEG, F32), jnp.zeros((8, QT), F32))
        for dyl in range(2):
            lim, full, end = tile_limits(limits, i, dyl)

            def step(j, state, masked, dyl=dyl, lim=lim, qti=qti):
                top, total = state
                s = jnp.dot(keys[dyl, at(j * KC, KC), :], qti, preferred_element_type=F32)
                if masked:
                    index = lax.broadcasted_iota(jnp.int32, (KC, QT), 0) + j * KC
                    s = jnp.where(index <= lim, s, NEG)
                s = s.reshape(KC // 8, 8, QT)
                new = jnp.maximum(top, jnp.max(s, axis=0))
                e = jnp.exp2((s - new[None]) * CEXP)
                total = total * jnp.exp2((top - new) * CEXP) + jnp.sum(e, axis=0)
                return new, total

            state = lax.fori_loop(0, full, functools.partial(step, masked=False), state)
            state = lax.fori_loop(full, end, functools.partial(step, masked=True), state)
        top8, total8 = state
        top = jnp.max(top8, axis=0, keepdims=True)
        total = jnp.sum(total8 * jnp.exp2((top8 - top) * CEXP), axis=0, keepdims=True)
        l1, l2, l3 = split3(-(top + jnp.log(total) * (1.0 / SCALE)))
        qt[HD : HD + 16, cols] = jnp.concatenate(
            [m1, m2, m3, m1, m2, m3, l1, l2, l3, jnp.zeros((7, QT), BF16)], axis=0
        )


def grads_loop(dyl, keys, vals, qs, qt, dos, dot, limits, dkey, dval, dq):
    dkey[...] = jnp.zeros((HALF, W), F32)
    dval[...] = jnp.zeros((HALF, W), F32)
    for i in range(NQT):
        cols = slice(i * QT, (i + 1) * QT)
        lim, full, end = tile_limits(limits, i, dyl)

        def step(j, carry, masked, cols=cols, lim=lim):
            rows = at(j * KC, KC)
            kc = keys[rows, :]
            s = jnp.dot(kc, qt[:, cols], preferred_element_type=F32)
            p = jnp.exp2(s * CEXP)
            if masked:
                index = lax.broadcasted_iota(jnp.int32, (KC, QT), 0) + j * KC
                p = jnp.where(index <= lim, p, 0.0)
            dp = jnp.dot(vals[rows, :], dot[:, cols], preferred_element_type=F32)
            ds = (p * dp).astype(BF16)
            dval[rows, :] += jnp.dot(p.astype(BF16), dos[cols, :], preferred_element_type=F32)
            dkey[rows, :] += jnp.dot(ds, qs[cols, :], preferred_element_type=F32)
            dq[cols, :] += lax.dot_general(
                ds, kc, (((0,), (0,)), ((), ())), preferred_element_type=F32
            )
            return carry

        lax.fori_loop(0, full, functools.partial(step, masked=False), 0)
        lax.fori_loop(full, end, functools.partial(step, masked=True), 0)


def unsort(ids, tables, dyl, dc, dkey, dval, out):
    for s in range(NX):
        ctx = ctx_of(ids, s, dyl, dc)
        for h in range(2):
            rows = at(tables[0, 2 * ctx + h] * BLK, BLK)
            base = s * 2 * OWN + h * BLK
            out[base : base + BLK, :] = (dkey[rows, :] * SCALE).astype(BF16)
            out[base + OWN : base + OWN + BLK, :] = dval[rows, :].astype(BF16)


def grads_other_kernel(ids, tables, *rest):
    kv = rest[0:8]
    qo = rest[8:12]
    dor, qs, qt = rest[12:15]
    dos, dot, dq, keep, send = rest[15:20]
    keys, vals, dkey, dval, flat, outs, limits = rest[20:27]
    sort_keys(ids, tables, kv, 1, keys, 0)
    sort_keys(ids, tables, kv, 1, vals, OWN)
    sort_limits(ids, tables, limits)
    for n in range(64):
        flat[n * 20 : (n + 1) * 20, :] = dor[n]

    def block(s, h):
        x = lax.rem(ids[0] + (NX - s), NX)
        return flat[at(x * OWN + h * BLK, BLK), :]

    sort_rows(ids, tables, block, dos)
    sort_rows(ids, tables, lambda s, h: qo[s][OWN + h * BLK : OWN + (h + 1) * BLK, :], outs)
    for i in range(NQT):
        cols = slice(i * QT, (i + 1) * QT)
        prod = dos[cols, :].astype(F32) * outs[cols, :].astype(F32)
        delta = jnp.sum(prod.T, axis=0, keepdims=True)
        d1, d2, d3 = split3(-delta)
        dot[:, cols] = dos[cols, :].T
        dot[HD : HD + 16, cols] = jnp.concatenate(
            [d1, d2, d3, jnp.zeros((13, QT), BF16)], axis=0
        )
    dq[...] = jnp.zeros((QROWS, W), F32)
    grads_loop(1, keys, vals, qs, qt, dos, dot, limits, dkey, dval, dq)
    unsort(ids, tables, 1, 0, dkey, dval, keep)
    unsort(ids, tables, 1, 1, dkey, dval, send)


def grads_own_kernel(ids, tables, *rest):
    kv = rest[0:8]
    qs, qt, dos, dot, dq_in = rest[8:13]
    dqo = rest[13:17]
    keep, send = rest[17:19]
    keys, vals, dkey, dval, dq, limits = rest[19:25]
    sort_keys(ids, tables, kv, 0, keys, 0)
    sort_keys(ids, tables, kv, 0, vals, OWN)
    sort_limits(ids, tables, limits)
    dq[...] = dq_in[...]
    grads_loop(0, keys, vals, qs, qt, dos, dot, limits, dkey, dval, dq)
    unsort(ids, tables, 0, 0, dkey, dval, keep)
    unsort(ids, tables, 0, 1, dkey, dval, send)
    for s in range(NX):
        ctx = ctx_of(ids, s, 0, 0)
        for h in range(2):
            rows = at(tables[1, 2 * ctx + h] * BLK, BLK)
            dqo[s][h * BLK : (h + 1) * BLK, :] = (dq[rows, :] * SCALE).astype(BF16)


def add_kernel(a, b, out):
    out[...] = (a[...].astype(F32) + b[...].astype(F32)).astype(BF16)


def add3_kernel(a, b, c, *outs):
    for s in range(NX):
        rows = slice(s * 2 * OWN, (s + 1) * 2 * OWN)
        outs[s][...] = (
            a[rows, :].astype(F32) + b[rows, :].astype(F32) + c[rows, :].astype(F32)
        ).astype(BF16)


def unpack_kernel(ids, *rest):
    dq, dkv = rest[0:4], rest[4:8]
    oq, ok, ov = rest[8:11]
    sq, skv = rest[11:13]
    for s in range(NX):
        head = lax.rem(ids[0] + s, NX)
        sq[head] = dq[s][...]
        skv[head] = dkv[s][...]
    for n in range(NX):
        cols = slice(n * HD, (n + 1) * HD)
        oq[:, cols] = sq[n, :, :HD]
        ok[:, cols] = skv[n, :OWN, :HD]
        ov[:, cols] = skv[n, OWN:, :HD]


def shift(value, axis, by):
    n = lax.axis_size(axis)
    return lax.ppermute(value, axis, [(i, (i + by) % n) for i in range(n)])


def plan_tables(plan):
    block = jnp.arange(32, dtype=jnp.int32)
    half = (block >> 2) & 1
    group = (block >> 1) & 3
    before = plan[None, :] < plan[:, None]
    same_half = half[None, :] == half[:, None]
    same_group = group[None, :] == group[:, None]

    def count(m):
        return jnp.sum(jnp.where(jnp.logical_and(before, m), 1, 0), axis=1, dtype=jnp.int32)

    return jnp.stack([count(same_half), count(same_group), count(jnp.logical_not(same_half)), plan])


def on_device(queries, keys, values, out_fwd, d_out, plan):
    piece = ((2 * OWN, W), BF16)
    stack = ((NX * 2 * OWN, W), BF16)
    x = lax.axis_index("x")
    ids = jnp.stack([x, lax.axis_index("yl"), lax.axis_index("c")]).astype(jnp.int32)
    tables = plan_tables(plan)
    head_id = (lax.axis_index("yh") * 8 + lax.axis_index("z")) * NX + x
    slope = jnp.exp2(-8.0 * (head_id + 1).astype(F32) / 64.0).reshape(1)

    (d_pack,) = call(cotangent_pack_kernel, [((64, 20, W), BF16)], [], "cotangent_pack")(d_out)
    d_rows = lax.all_to_all(d_pack, ("x", "yh", "z"), 0, 0)

    packed = call(
        pack_kernel,
        [piece] * 8,
        [pltpu.VMEM((NX, 2 * OWN, W), BF16)] * 2,
        "pack",
    )(ids, tables, queries, keys, values, out_fwd)
    kv, qo = list(packed[:4]), list(packed[4:])
    for s in (1, 3, 2):
        kv[s] = shift(kv[s], "x", s)
    for s in (1, 3, 2):
        qo[s] = shift(qo[s], "x", s)
    kv_y = [shift(a, "yl", 1) for a in kv]
    kv_c = [shift(a, "c", 1) for a in kv]
    kv_yc = [shift(a, "c", 1) for a in kv_y]
    own = [a for s in range(NX) for a in (kv[s], kv_c[s])]
    other = [a for s in range(NX) for a in (kv_y[s], kv_yc[s])]

    limits = pltpu.SMEM((2, 8), jnp.int32)
    qs, qt = call(
        stats_kernel,
        [((QROWS, W), BF16), ((W, QROWS), BF16)],
        [pltpu.VMEM((2, HALF, W), BF16), limits],
        "stats",
    )(ids, tables, slope, *own, *other, *qo)
    accs = [pltpu.VMEM((HALF, W), BF16)] * 2 + [pltpu.VMEM((HALF, W), F32)] * 2
    dos, dot, dq, keep_o, send_o = call(
        grads_other_kernel,
        [((QROWS, W), BF16), ((W, QROWS), BF16), ((QROWS, W), F32), stack, stack],
        accs + [pltpu.VMEM((QROWS, W), BF16)] * 2 + [limits],
        "grads_other",
    )(ids, tables, *other, *qo, d_rows, qs, qt)
    recv_o = shift(send_o, "c", 1)
    (sum_o,) = call(add_kernel, [stack], [], "add_other")(keep_o, recv_o)
    recv_y = shift(sum_o, "yl", 1)

    *dqs, keep, send = call(
        grads_own_kernel,
        [((OWN, W), BF16)] * 4 + [stack, stack],
        accs + [pltpu.VMEM((QROWS, W), F32), limits],
        "grads_own",
    )(ids, tables, *own, qs, qt, dos, dot, dq)
    recv = shift(send, "c", 1)
    dqs = [dqs[0]] + [shift(dqs[s], "x", -s) for s in (1, 2, 3)]
    dkvs = call(add3_kernel, [piece] * 4, [], "add_own")(keep, recv, recv_y)
    dkvs = [dkvs[0]] + [shift(dkvs[s], "x", -s) for s in (1, 2, 3)]
    out = ((OWN, NX * HD), BF16)
    return tuple(
        call(
            unpack_kernel,
            [out] * 3,
            [pltpu.VMEM((NX, OWN, W), BF16), pltpu.VMEM((NX, 2 * OWN, W), BF16)],
            "unpack",
        )(ids, *dqs, *dkvs)
    )


def solution(mesh):
    devices = mesh.devices.reshape(4, 2, 2, 2, 8)
    fine = Mesh(devices, ("x", "yl", "c", "yh", "z"))
    ctx, head = ("x", "yl", "c"), ("yh", "z")
    tile = P(ctx, head)
    return jax.shard_map(
        on_device,
        mesh=fine,
        in_specs=(tile, tile, tile, tile, P(ctx + head, None), P()),
        out_specs=(tile, tile, tile),
        check_vma=False,
    )
```

time: 437 us -> 161 us (0.37)
  waiting for transfers between devices: 181 us -> 37.2 us
  matrix products: 90.5 us -> 0 us
  local copies, waits for them, and re-layouts: 84.2 us -> 4.52 us
  Pallas kernels: 0 us -> 68.3 us
  starting transfers between devices: 12 us -> 47.1 us
  other arithmetic: 31.4 us -> 1.5 us
  blocking collectives: 18.5 us -> 0 us
  between operations: 13.9 us -> 1.01 us
    unnamed x6 -> x0, waiting for transfers between devices: 119 us -> none
    dot_general x48 -> x0, matrix products: 90.5 us -> none  [the longest x16 35.5 us: scores(): jnp.einsum('qhd,khd->hqk', query_rows, key_rows, preferred_element_type=j...]
    pallas_call x0 -> x8, Pallas kernels: none -> 68.3 us  [run(): pl.pallas_call(kernel, out_shape=[jax.ShapeDtypeStruct(s, d) for s, d in...]
    all_gather x4 -> x0, waiting for transfers between devices: 53.2 us -> none  [the longest x2 29.9 us: combined_all(): pieces = jax.tree.map(lambda part: lax.all_gather(part, axis), value)]
    unnamed x17 -> x72, local copies, waits for them, and re-layouts: 47.1 us -> 4.52 us
    ppermute x0 -> x27, waiting for transfers between devices: none -> 37.2 us  [shift(): return lax.ppermute(value, axis, [(i, (i + by) % n) for i in range(n)])]
    ppermute x0 -> x27, starting transfers between devices: none -> 35.1 us  [shift(): return lax.ppermute(value, axis, [(i, (i + by) % n) for i in range(n)])]
    reshape x4 -> x0, local copies, waits for them, and re-layouts: 20 us -> none  [the longest x1 9.32 us: on_device(): grad_blocks = grad_all.reshape(nblocks, rows, heads_dev, HD)]
  transfers between devices with their start and end apart: 6 -> 28, of which waited for: 4 -> 7; matrix products, arithmetic and copies ran while one was open for 19% -> 0% of each run, Pallas kernels for 0% -> 27%
where the time goes in v1:
time: 161 us; the launch traced here: 160 us
  Pallas kernels  68.3 us (42%)
  starting transfers between devices  47.1 us (29%)
  waiting for transfers between devices  37.2 us (23%)
  local copies, waits for them, and re-layouts  4.52 us (3%)
    pallas_call x8, Pallas kernels, run(): pl.pallas_call(kernel, out_shape=[jax.ShapeDtypeStruct(s, d) for s, d in...  68.3 us
    ppermute x27, waiting for transfers between devices, shift(): return lax.ppermute(value, axis, [(i, (i + by) % n) for i in range(n)])  37.2 us
    ppermute x27, starting transfers between devices, shift(): return lax.ppermute(value, axis, [(i, (i + by) % n) for i in range(n)])  35.1 us
    all_to_all x1, starting transfers between devices, on_device(): d_rows = lax.all_to_all(d_pack, ('x', 'yh', 'z'), 0, 0)  12 us
    unnamed x72, local copies, waits for them, and re-layouts  4.52 us
  transfers between devices with their start and end apart: 28, of which 7 were waited for; matrix products, arithmetic and copies ran while one was open for 0% of the time, Pallas kernels for 27%

profile of v1, /device:TPU:1, one launch (start us, length us, event | category | flops | bytes accessed | tf_op | source)
XLA Modules:
  0.0 159.7 jit_solution(7894918342000596193)
XLA Ops:
  2.8 3.2 %pack.1 = (bf16[640,128]{1,0:T(8,128)(2,1)}, bf16[640,128]{1,0:T(8,128)(2,1)}, bf16[640,128]{1,0:T(8,128)(2,1)}, bf16[640,128]{1,0:T(8,128)(2,1)}, bf16[640,128]...) custom-call(s32[3]{0:T(128)} %pad_add_fusion.1.ids, ...), custom_call_target="tpu_custom_call" | custom-call | tf_op jit(solution)/shard_map/pack/pallas_call | solution.py:36
  6.0 2.0 %collective-permute-start.1 = (bf16[640,128]{1,0:T(8,128)(2,1)}, bf16[640,128]{1,0:T(8,128)(2,1)S(1)}, u32[]{:S(2)}, u32[]{:S(2)}) collective-permute-start(bf16[640,128]{1,0:T(8,128)(2,1)} %get-tuple-element.29), channel_id=1, source_target_pairs={{0,64},{64,128},{128,192},{192,0},{1,65},{65,129},{129,193},{193,1... | collective-permute-start | bytes 491528 | tf_op jit(solution)/shard_map/ppermute | solution.py:311
  8.0 2.5 %collective-permute-start.3 = (bf16[640,128]{1,0:T(8,128)(2,1)}, bf16[640,128]{1,0:T(8,128)(2,1)S(1)}, u32[]{:S(2)}, u32[]{:S(2)}) collective-permute-start(bf16[640,128]{1,0:T(8,128)(2,1)} %get-tuple-element.30), channel_id=1, source_target_pairs={{0,128},{64,192},{128,0},{192,64},{1,129},{65,193},{129,1},{193,65... | collective-permute-start | bytes 491528 | tf_op jit(solution)/shard_map/ppermute | solution.py:311
  10.5 1.2 collective-permute-start.5
  11.6 2.0 %cotangent_pack.1 = bf16[64,20,128]{2,1,0:T(8,128)(2,1)} custom-call(bf16[20,7168]{1,0:T(8,128)(2,1)} %d_ref.1), custom_call_target="tpu_custom_call" | custom-call | tf_op jit(solution)/shard_map/cotangent_pack/pallas_call | solution.py:36
  13.6 12.0 %all-to-all-start = ((bf16[64,20,128]{2,1,0:T(8,128)(2,1)}), bf16[64,20,128]{2,1,0:T(8,128)(2,1)S(1)}, u32[]{:S(2)}, u32[]{:S(2)}) async-start(bf16[64,20,128]{2,1,0:T(8,128)(2,1)} %cotangent_pack.1), calls=%async_computation | async-start | bytes 786432 | tf_op jit(solution)/shard_map/all_to_all | solution.py:338
  25.6 1.1 collective-permute-start.15
  26.7 2.6 %collective-permute-start.16 = (bf16[640,128]{1,0:T(8,128)(2,1)S(1)}, bf16[640,128]{1,0:T(8,128)(2,1)S(1)}, u32[]{:S(2)}, u32[]{:S(2)}) collective-permute-start(bf16[640,128]{1,0:T(8,128)(2,1)S(1)} %copy-done.31), channel_id=1, source_target_pairs={{0,128},{64,192},{128,0},{192,64},{1,129},{65,193},{129,1},{193,65... | collective-permute-start | bytes 491528 | tf_op jit(solution)/shard_map/ppermute | solution.py:311
  29.3 1.1 collective-permute-start.17
  31.0 3.2 %collective-permute-start = (bf16[640,128]{1,0:T(8,128)(2,1)S(1)}, bf16[640,128]{1,0:T(8,128)(2,1)S(1)}, u32[]{:S(2)}, u32[]{:S(2)}) collective-permute-start(bf16[640,128]{1,0:T(8,128)(2,1)S(1)} %copy-done.1), channel_id=1, source_target_pairs={{0,16},{16,0},{1,17},{17,1},{2,18},{18,2},{3,19},{19,3},{4,20},{20... | collective-permute-start | bytes 491528 | tf_op jit(solution)/shard_map/ppermute | solution.py:311
  34.2 1.1 collective-permute-start.9
  35.2 4.7 %collective-permute-done.16.rest_18_.rest_10_ = bf16[640,128]{1,0:T(8,128)(2,1)S(1)} collective-permute-done((bf16[640,128]{1,0:T(8,128)(2,1)S(1)}, bf16[640,128]{1,0:T(8,128)(2,1)S(1)}, u32[]{:S(2)}, u32[]{:S(2)}) %collective-permute-start.16) | collective-permute-done | bytes 163872 | tf_op jit(solution)/shard_map/ppermute | solution.py:311
  39.9 2.0 %collective-permute-start.2 = (bf16[640,128]{1,0:T(8,128)(2,1)S(1)}, bf16[640,128]{1,0:T(8,128)(2,1)S(1)}, u32[]{:S(2)}, u32[]{:S(2)}) collective-permute-start(bf16[640,128]{1,0:T(8,128)(2,1)S(1)} %collective-permute-done.1.rest_2_), channel_id=1, source_target_pairs={{0,16},{16,0},{1,17},{17,1},{2,18},{18,2},{3,19},{19,3},{4,20},{20... | collective-permute-start | bytes 491528 | tf_op jit(solution)/shard_map/ppermute | solution.py:311
  42.7 1.1 collective-permute-start.13
  44.3 3.3 %collective-permute-done.11.rest_12_.rest_4_ = bf16[640,128]{1,0:T(8,128)(2,1)S(1)} collective-permute-done((bf16[640,128]{1,0:T(8,128)(2,1)S(1)}, bf16[640,128]{1,0:T(8,128)(2,1)S(1)}, u32[]{:S(2)}, u32[]{:S(2)}) %collective-permute-start.11) | collective-permute-done | bytes 163872 | tf_op jit(solution)/shard_map/ppermute | solution.py:311
  47.7 1.3 collective-permute-start.10
  49.1 2.1 %collective-permute-done.13.rest_14_.rest_6_ = bf16[640,128]{1,0:T(8,128)(2,1)S(1)} collective-permute-done((bf16[640,128]{1,0:T(8,128)(2,1)S(1)}, bf16[640,128]{1,0:T(8,128)(2,1)S(1)}, u32[]{:S(2)}, u32[]{:S(2)}) %collective-permute-start.13) | collective-permute-done | bytes 163872 | tf_op jit(solution)/shard_map/ppermute | solution.py:311
  52.2 0.9 collective-permute-done.14.rest_15_.rest_7_
  53.8 17.7 %stats.1 = (bf16[1280,128]{1,0:T(8,128)(2,1)}, bf16[128,1280]{1,0:T(8,128)(2,1)}) custom-call(s32[3]{0:T(128)} %pad_add_fusion.1.ids, s32[4,32]{1,0:T(4,128)} %pad_add_fusion.tables, f32[1]{0:T(128)} %bitcast.7.slope, bf16[640,128]{1,0:T(8,128)(2,1)} %get-tuple-element.28.rest_0_, bf16[640,128]{1,0:T(8,128)(2,1)} %copy-done.6, bf16[640,128]{1,0:T(8,128)(2,1)} %copy-done.2, ...), custom_call_target="tpu_custom_call" | custom-call | tf_op jit(solution)/shard_map/stats/pallas_call | solution.py:36
  72.2 18.9 %grads_other.1 = (bf16[1280,128]{1,0:T(8,128)(2,1)}, bf16[128,1280]{1,0:T(8,128)(2,1)}, f32[1280,128]{1,0:T(8,128)}, bf16[2560,128]{1,0:T(8,128)(2,1)}, bf16[2560,128]{1,0:T(8,128)(2,1)}) custom-call(s32[3]{0:T(128)} %pad_add_fusion.1.ids, s32[4,32]{1,0:T(4,128)} %pad_add_fusion.tables, bf16[640,128]{1,0:T(8,128)(2,1)} %copy-done.10, ...), custom_call_target="tpu_custom_call" | custom-call | tf_op jit(solution)/shard_map/grads_other/pallas_call | solution.py:36
  91.1 4.4 %collective-permute-start.22 = (bf16[2560,128]{1,0:T(8,128)(2,1)}, bf16[2560,128]{1,0:T(8,128)(2,1)S(1)}, u32[]{:S(2)}, u32[]{:S(2)}) collective-permute-start(bf16[2560,128]{1,0:T(8,128)(2,1)} %get-tuple-element.48), channel_id=1, source_target_pairs={{0,16},{16,0},{1,17},{17,1},{2,18},{18,2},{3,19},{19,3},{4,20},{20... | collective-permute-start | bytes 1966088 | tf_op jit(solution)/shard_map/ppermute | solution.py:311
  95.5 19.0 %grads_own.1 = (bf16[320,128]{1,0:T(8,128)(2,1)}, bf16[320,128]{1,0:T(8,128)(2,1)}, bf16[320,128]{1,0:T(8,128)(2,1)}, bf16[320,128]{1,0:T(8,128)(2,1)}, bf16[256...) custom-call(s32[3]{0:T(128)} %pad_add_fusion.1.ids, s32[4,32]{1,0:T(4,128)} %pad_add_fusion.tables, ...), custom_call_target="tpu_custom_call" | custom-call | tf_op jit(solution)/shard_map/grads_own/pallas_call | solution.py:36
  114.5 2.6 %collective-permute-start.21 = (bf16[2560,128]{1,0:T(8,128)(2,1)}, bf16[2560,128]{1,0:T(8,128)(2,1)S(1)}, u32[]{:S(2)}, u32[]{:S(2)}) collective-permute-start(bf16[2560,128]{1,0:T(8,128)(2,1)} %get-tuple-element.46), channel_id=1, source_target_pairs={{0,16},{16,0},{1,17},{17,1},{2,18},{18,2},{3,19},{19,3},{4,20},{20... | collective-permute-start | bytes 1966088 | tf_op jit(solution)/shard_map/ppermute | solution.py:311
  118.0 2.3 %add_other.1 = bf16[2560,128]{1,0:T(8,128)(2,1)} custom-call(bf16[2560,128]{1,0:T(8,128)(2,1)} %get-tuple-element.47.a, bf16[2560,128]{1,0:T(8,128)(2,1)} %copy-done.20), custom_call_target="tpu_custom_call" | custom-call | tf_op jit(solution)/shard_map/add_other/pallas_call | solution.py:36
  120.3 1.0 collective-permute-start.18
  121.3 15.5 %collective-permute-done.23.c = bf16[2560,128]{1,0:T(8,128)(2,1)S(1)} collective-permute-done((bf16[2560,128]{1,0:T(8,128)(2,1)}, bf16[2560,128]{1,0:T(8,128)(2,1)S(1)}, u32[]{:S(2)}, u32[]{:S(2)}) %collective-permute-start.23) | collective-permute-done | bytes 655392 | tf_op jit(solution)/shard_map/ppermute | solution.py:311
  137.7 2.4 %add_own.1 = (bf16[640,128]{1,0:T(8,128)(2,1)}, bf16[640,128]{1,0:T(8,128)(2,1)}, bf16[640,128]{1,0:T(8,128)(2,1)}, bf16[640,128]{1,0:T(8,128)(2,1)}) custom-call(bf16[2560,128]{1,0:T(8,128)(2,1)} %get-tuple-element.45.a, bf16[2560,128]{1,0:T(8,128)(2,1)} %copy-done.21, bf16[2560,128]{1,0:T(8,128)(2,1)} %copy-done.22), custom_call_target="tpu_custom_call" | custom-call | tf_op jit(solution)/shard_map/add_own/pallas_call | solution.py:36
  140.1 1.0 collective-permute-start.24
  141.8 3.3 %collective-permute-start.19 = (bf16[320,128]{1,0:T(8,128)(2,1)S(1)}, bf16[320,128]{1,0:T(8,128)(2,1)S(1)}, u32[]{:S(2)}, u32[]{:S(2)}) collective-permute-start(bf16[320,128]{1,0:T(8,128)(2,1)S(1)} %copy-done.34), channel_id=1, source_target_pairs={{0,128},{64,192},{128,0},{192,64},{1,129},{65,193},{129,1},{193,65... | collective-permute-start | bytes 245768 | tf_op jit(solution)/shard_map/ppermute | solution.py:311
  145.3 7.2 %collective-permute-done.19.rest_2_ = bf16[320,128]{1,0:T(8,128)(2,1)S(1)} collective-permute-done((bf16[320,128]{1,0:T(8,128)(2,1)S(1)}, bf16[320,128]{1,0:T(8,128)(2,1)S(1)}, u32[]{:S(2)}, u32[]{:S(2)}) %collective-permute-start.19) | collective-permute-done | bytes 81952 | tf_op jit(solution)/shard_map/ppermute | solution.py:311
  152.5 3.5 %collective-permute-done.20.rest_3_ = bf16[320,128]{1,0:T(8,128)(2,1)S(1)} collective-permute-done((bf16[320,128]{1,0:T(8,128)(2,1)S(1)}, bf16[320,128]{1,0:T(8,128)(2,1)S(1)}, u32[]{:S(2)}, u32[]{:S(2)}) %collective-permute-start.20) | collective-permute-done | bytes 81952 | tf_op jit(solution)/shard_map/ppermute | solution.py:311
  156.8 2.8 %unpack.1 = (bf16[320,448]{1,0:T(8,128)(2,1)}, bf16[320,448]{1,0:T(8,128)(2,1)}, bf16[320,448]{1,0:T(8,128)(2,1)}) custom-call(s32[3]{0:T(128)} %pad_add_fusion.1.ids, bf16[320,128]{1,0:T(8,128)(2,1)} %get-tuple-element.41.rest_0_, bf16[320,128]{1,0:T(8,128)(2,1)} %copy-done.26, bf16[320,128]{1,0:T(8,128)(2,1)} %copy-done.27, bf16[320,128]{1,0:T(8,128)(2,1)} %copy-done.28, ...), custom_call_target="tpu_custom_call" | custom-call | tf_op jit(solution)/shard_map/unpack/pallas_call | solution.py:36
  (108 shorter events, 9.6 us)
Async XLA Ops:
  6.0 23.3 %collective-permute-start.1 = (bf16[640,128]{1,0:T(8,128)(2,1)}, bf16[640,128]{1,0:T(8,128)(2,1)S(1)}, u32[]{:S(2)}, u32[]{:S(2)}) collective-permute-start(bf16[640,128]{1,0:T(8,128)(2,1)} %get-tuple-element.29), channel_id=1, source_target_pairs={{0,64},{64,128},{128,192},{192,0},{1,65},{65,129},{129,193},{193,1... | collective-permute-start | bytes 491528 | tf_op jit(solution)/shard_map/ppermute | solution.py:311
  8.0 22.4 %collective-permute-start.3 = (bf16[640,128]{1,0:T(8,128)(2,1)}, bf16[640,128]{1,0:T(8,128)(2,1)S(1)}, u32[]{:S(2)}, u32[]{:S(2)}) collective-permute-start(bf16[640,128]{1,0:T(8,128)(2,1)} %get-tuple-element.30), channel_id=1, source_target_pairs={{0,128},{64,192},{128,0},{192,64},{1,129},{65,193},{129,1},{193,65... | collective-permute-start | bytes 491528 | tf_op jit(solution)/shard_map/ppermute | solution.py:311
  10.5 20.5 %collective-permute-start.5 = (bf16[640,128]{1,0:T(8,128)(2,1)}, bf16[640,128]{1,0:T(8,128)(2,1)S(1)}, u32[]{:S(2)}, u32[]{:S(2)}) collective-permute-start(bf16[640,128]{1,0:T(8,128)(2,1)} %get-tuple-element.31), channel_id=1, source_target_pairs={{0,192},{64,0},{128,64},{192,128},{1,193},{65,1},{129,65},{193,129... | collective-permute-start | bytes 491528 | tf_op jit(solution)/shard_map/ppermute | solution.py:311
  13.6 57.9 %all-to-all-start = ((bf16[64,20,128]{2,1,0:T(8,128)(2,1)}), bf16[64,20,128]{2,1,0:T(8,128)(2,1)S(1)}, u32[]{:S(2)}, u32[]{:S(2)}) async-start(bf16[64,20,128]{2,1,0:T(8,128)(2,1)} %cotangent_pack.1), calls=%async_computation | async-start | bytes 786432 | tf_op jit(solution)/shard_map/all_to_all | solution.py:338
  25.6 8.5 %collective-permute-start.15 = (bf16[640,128]{1,0:T(8,128)(2,1)S(1)}, bf16[640,128]{1,0:T(8,128)(2,1)S(1)}, u32[]{:S(2)}, u32[]{:S(2)}) collective-permute-start(bf16[640,128]{1,0:T(8,128)(2,1)S(1)} %copy-done.32), channel_id=1, source_target_pairs={{0,64},{64,128},{128,192},{192,0},{1,65},{65,129},{129,193},{193,1... | collective-permute-start | bytes 491528 | tf_op jit(solution)/shard_map/ppermute | solution.py:311
  26.7 13.2 %collective-permute-start.16 = (bf16[640,128]{1,0:T(8,128)(2,1)S(1)}, bf16[640,128]{1,0:T(8,128)(2,1)S(1)}, u32[]{:S(2)}, u32[]{:S(2)}) collective-permute-start(bf16[640,128]{1,0:T(8,128)(2,1)S(1)} %copy-done.31), channel_id=1, source_target_pairs={{0,128},{64,192},{128,0},{192,64},{1,129},{65,193},{129,1},{193,65... | collective-permute-start | bytes 491528 | tf_op jit(solution)/shard_map/ppermute | solution.py:311
  29.3 23.8 %copy-start.2 = (bf16[640,128]{1,0:T(8,128)(2,1)}, bf16[640,128]{1,0:T(8,128)(2,1)S(1)}, u32[]{:S(2)}) copy-start(bf16[640,128]{1,0:T(8,128)(2,1)S(1)} %collective-permute-done.1.rest_2_) | copy-start | bytes 491524
  29.3 12.6 %collective-permute-start.17 = (bf16[640,128]{1,0:T(8,128)(2,1)S(1)}, bf16[640,128]{1,0:T(8,128)(2,1)S(1)}, u32[]{:S(2)}, u32[]{:S(2)}) collective-permute-start(bf16[640,128]{1,0:T(8,128)(2,1)S(1)} %copy-done.30), channel_id=1, source_target_pairs={{0,192},{64,0},{128,64},{192,128},{1,193},{65,1},{129,65},{193,129... | collective-permute-start | bytes 491528 | tf_op jit(solution)/shard_map/ppermute | solution.py:311
  30.5 22.6 %copy-start.3 = (bf16[640,128]{1,0:T(8,128)(2,1)}, bf16[640,128]{1,0:T(8,128)(2,1)S(1)}, u32[]{:S(2)}) copy-start(bf16[640,128]{1,0:T(8,128)(2,1)S(1)} %collective-permute-done.3.rest_4_) | copy-start | bytes 491524
  30.5 11.9 %collective-permute-start.7 = (bf16[640,128]{1,0:T(8,128)(2,1)S(1)}, bf16[640,128]{1,0:T(8,128)(2,1)S(1)}, u32[]{:S(2)}, u32[]{:S(2)}) collective-permute-start(bf16[640,128]{1,0:T(8,128)(2,1)S(1)} %copy-done.1), channel_id=1, source_target_pairs={{0,32},{32,0},{1,33},{33,1},{2,34},{34,2},{3,35},{35,3},{4,36},{36... | collective-permute-start | bytes 491528 | tf_op jit(solution)/shard_map/ppermute | solution.py:311
  31.0 22.2 %copy-start.4 = (bf16[640,128]{1,0:T(8,128)(2,1)}, bf16[640,128]{1,0:T(8,128)(2,1)S(1)}, u32[]{:S(2)}) copy-start(bf16[640,128]{1,0:T(8,128)(2,1)S(1)} %collective-permute-done.5.rest_6_) | copy-start | bytes 491524
  31.0 11.8 %collective-permute-start = (bf16[640,128]{1,0:T(8,128)(2,1)S(1)}, bf16[640,128]{1,0:T(8,128)(2,1)S(1)}, u32[]{:S(2)}, u32[]{:S(2)}) collective-permute-start(bf16[640,128]{1,0:T(8,128)(2,1)S(1)} %copy-done.1), channel_id=1, source_target_pairs={{0,16},{16,0},{1,17},{17,1},{2,18},{18,2},{3,19},{19,3},{4,20},{20... | collective-permute-start | bytes 491528 | tf_op jit(solution)/shard_map/ppermute | solution.py:311
  34.2 19.0 %copy-start.5 = (bf16[640,128]{1,0:T(8,128)(2,1)}, bf16[640,128]{1,0:T(8,128)(2,1)S(1)}, u32[]{:S(2)}) copy-start(bf16[640,128]{1,0:T(8,128)(2,1)S(1)} %collective-permute-done.15.rest_17_.rest_9_) | copy-start | bytes 491524
  34.2 9.6 %collective-permute-start.9 = (bf16[640,128]{1,0:T(8,128)(2,1)S(1)}, bf16[640,128]{1,0:T(8,128)(2,1)S(1)}, u32[]{:S(2)}, u32[]{:S(2)}) collective-permute-start(bf16[640,128]{1,0:T(8,128)(2,1)S(1)} %collective-permute-done.1.rest_2_), channel_id=1, source_target_pairs={{0,32},{32,0},{1,33},{33,1},{2,34},{34,2},{3,35},{35,3},{4,36},{36... | collective-permute-start | bytes 491528 | tf_op jit(solution)/shard_map/ppermute | solution.py:311
  39.9 4.3 %collective-permute-start.2 = (bf16[640,128]{1,0:T(8,128)(2,1)S(1)}, bf16[640,128]{1,0:T(8,128)(2,1)S(1)}, u32[]{:S(2)}, u32[]{:S(2)}) collective-permute-start(bf16[640,128]{1,0:T(8,128)(2,1)S(1)} %collective-permute-done.1.rest_2_), channel_id=1, source_target_pairs={{0,16},{16,0},{1,17},{17,1},{2,18},{18,2},{3,19},{19,3},{4,20},{20... | collective-permute-start | bytes 491528 | tf_op jit(solution)/shard_map/ppermute | solution.py:311
  41.9 5.8 %collective-permute-start.11 = (bf16[640,128]{1,0:T(8,128)(2,1)S(1)}, bf16[640,128]{1,0:T(8,128)(2,1)S(1)}, u32[]{:S(2)}, u32[]{:S(2)}) collective-permute-start(bf16[640,128]{1,0:T(8,128)(2,1)S(1)} %collective-permute-done.3.rest_4_), channel_id=1, source_target_pairs={{0,32},{32,0},{1,33},{33,1},{2,34},{34,2},{3,35},{35,3},{4,36},{36... | collective-permute-start | bytes 491528 | tf_op jit(solution)/shard_map/ppermute | solution.py:311
  42.3 6.7 %collective-permute-start.4 = (bf16[640,128]{1,0:T(8,128)(2,1)S(1)}, bf16[640,128]{1,0:T(8,128)(2,1)S(1)}, u32[]{:S(2)}, u32[]{:S(2)}) collective-permute-start(bf16[640,128]{1,0:T(8,128)(2,1)S(1)} %collective-permute-done.3.rest_4_), channel_id=1, source_target_pairs={{0,16},{16,0},{1,17},{17,1},{2,18},{18,2},{3,19},{19,3},{4,20},{20... | collective-permute-start | bytes 491528 | tf_op jit(solution)/shard_map/ppermute | solution.py:311
  42.7 8.5 %collective-permute-start.13 = (bf16[640,128]{1,0:T(8,128)(2,1)S(1)}, bf16[640,128]{1,0:T(8,128)(2,1)S(1)}, u32[]{:S(2)}, u32[]{:S(2)}) collective-permute-start(bf16[640,128]{1,0:T(8,128)(2,1)S(1)} %collective-permute-done.5.rest_6_), channel_id=1, source_target_pairs={{0,32},{32,0},{1,33},{33,1},{2,34},{34,2},{3,35},{35,3},{4,36},{36... | collective-permute-start | bytes 491528 | tf_op jit(solution)/shard_map/ppermute | solution.py:311
  43.8 8.3 %collective-permute-start.6 = (bf16[640,128]{1,0:T(8,128)(2,1)S(1)}, bf16[640,128]{1,0:T(8,128)(2,1)S(1)}, u32[]{:S(2)}, u32[]{:S(2)}) collective-permute-start(bf16[640,128]{1,0:T(8,128)(2,1)S(1)} %collective-permute-done.5.rest_6_), channel_id=1, source_target_pairs={{0,16},{16,0},{1,17},{17,1},{2,18},{18,2},{3,19},{19,3},{4,20},{20... | collective-permute-start | bytes 491528 | tf_op jit(solution)/shard_map/ppermute | solution.py:311
  44.2 7.9 %collective-permute-start.8 = (bf16[640,128]{1,0:T(8,128)(2,1)S(1)}, bf16[640,128]{1,0:T(8,128)(2,1)S(1)}, u32[]{:S(2)}, u32[]{:S(2)}) collective-permute-start(bf16[640,128]{1,0:T(8,128)(2,1)S(1)} %collective-permute-done.7.rest_8_.rest_0_), channel_id=1, source_target_pairs={{0,16},{16,0},{1,17},{17,1},{2,18},{18,2},{3,19},{19,3},{4,20},{20... | collective-permute-start | bytes 491528 | tf_op jit(solution)/shard_map/ppermute | solution.py:311
  47.7 4.5 %collective-permute-start.10 = (bf16[640,128]{1,0:T(8,128)(2,1)S(1)}, bf16[640,128]{1,0:T(8,128)(2,1)S(1)}, u32[]{:S(2)}, u32[]{:S(2)}) collective-permute-start(bf16[640,128]{1,0:T(8,128)(2,1)S(1)} %collective-permute-done.9.rest_10_.rest_2_), channel_id=1, source_target_pairs={{0,16},{16,0},{1,17},{17,1},{2,18},{18,2},{3,19},{19,3},{4,20},{20... | collective-permute-start | bytes 491528 | tf_op jit(solution)/shard_map/ppermute | solution.py:311
  49.0 3.1 %collective-permute-start.12 = (bf16[640,128]{1,0:T(8,128)(2,1)S(1)}, bf16[640,128]{1,0:T(8,128)(2,1)S(1)}, u32[]{:S(2)}, u32[]{:S(2)}) collective-permute-start(bf16[640,128]{1,0:T(8,128)(2,1)S(1)} %collective-permute-done.11.rest_12_.rest_4_), channel_id=1, source_target_pairs={{0,16},{16,0},{1,17},{17,1},{2,18},{18,2},{3,19},{19,3},{4,20},{20... | collective-permute-start | bytes 491528 | tf_op jit(solution)/shard_map/ppermute | solution.py:311
  51.2 1.9 %collective-permute-start.14 = (bf16[640,128]{1,0:T(8,128)(2,1)S(1)}, bf16[640,128]{1,0:T(8,128)(2,1)S(1)}, u32[]{:S(2)}, u32[]{:S(2)}) collective-permute-start(bf16[640,128]{1,0:T(8,128)(2,1)S(1)} %collective-permute-done.13.rest_14_.rest_6_), channel_id=1, source_target_pairs={{0,16},{16,0},{1,17},{17,1},{2,18},{18,2},{3,19},{19,3},{4,20},{20... | collective-permute-start | bytes 491528 | tf_op jit(solution)/shard_map/ppermute | solution.py:311
  91.1 26.0 %collective-permute-start.22 = (bf16[2560,128]{1,0:T(8,128)(2,1)}, bf16[2560,128]{1,0:T(8,128)(2,1)S(1)}, u32[]{:S(2)}, u32[]{:S(2)}) collective-permute-start(bf16[2560,128]{1,0:T(8,128)(2,1)} %get-tuple-element.48), channel_id=1, source_target_pairs={{0,16},{16,0},{1,17},{17,1},{2,18},{18,2},{3,19},{19,3},{4,20},{20... | collective-permute-start | bytes 1966088 | tf_op jit(solution)/shard_map/ppermute | solution.py:311
  114.5 6.8 %collective-permute-start.21 = (bf16[2560,128]{1,0:T(8,128)(2,1)}, bf16[2560,128]{1,0:T(8,128)(2,1)S(1)}, u32[]{:S(2)}, u32[]{:S(2)}) collective-permute-start(bf16[2560,128]{1,0:T(8,128)(2,1)} %get-tuple-element.46), channel_id=1, source_target_pairs={{0,16},{16,0},{1,17},{17,1},{2,18},{18,2},{3,19},{19,3},{4,20},{20... | collective-permute-start | bytes 1966088 | tf_op jit(solution)/shard_map/ppermute | solution.py:311
  120.3 16.6 %collective-permute-start.23 = (bf16[2560,128]{1,0:T(8,128)(2,1)}, bf16[2560,128]{1,0:T(8,128)(2,1)S(1)}, u32[]{:S(2)}, u32[]{:S(2)}) collective-permute-start(bf16[2560,128]{1,0:T(8,128)(2,1)} %add_other.1), channel_id=1, source_target_pairs={{0,32},{32,0},{1,33},{33,1},{2,34},{34,2},{3,35},{35,3},{4,36},{36... | collective-permute-start | bytes 1966088 | tf_op jit(solution)/shard_map/ppermute | solution.py:311
  120.3 24.9 %collective-permute-start.18 = (bf16[320,128]{1,0:T(8,128)(2,1)S(1)}, bf16[320,128]{1,0:T(8,128)(2,1)S(1)}, u32[]{:S(2)}, u32[]{:S(2)}) collective-permute-start(bf16[320,128]{1,0:T(8,128)(2,1)S(1)} %copy-done.35), channel_id=1, source_target_pairs={{0,192},{64,0},{128,64},{192,128},{1,193},{65,1},{129,65},{193,129... | collective-permute-start | bytes 245768 | tf_op jit(solution)/shard_map/ppermute | solution.py:311
  140.1 15.9 %collective-permute-start.24 = (bf16[640,128]{1,0:T(8,128)(2,1)}, bf16[640,128]{1,0:T(8,128)(2,1)S(1)}, u32[]{:S(2)}, u32[]{:S(2)}) collective-permute-start(bf16[640,128]{1,0:T(8,128)(2,1)} %get-tuple-element.50), channel_id=1, source_target_pairs={{0,192},{64,0},{128,64},{192,128},{1,193},{65,1},{129,65},{193,129... | collective-permute-start | bytes 491528 | tf_op jit(solution)/shard_map/ppermute | solution.py:311
  141.2 14.8 %collective-permute-start.25 = (bf16[640,128]{1,0:T(8,128)(2,1)}, bf16[640,128]{1,0:T(8,128)(2,1)S(1)}, u32[]{:S(2)}, u32[]{:S(2)}) collective-permute-start(bf16[640,128]{1,0:T(8,128)(2,1)} %get-tuple-element.51), channel_id=1, source_target_pairs={{0,128},{64,192},{128,0},{192,64},{1,129},{65,193},{129,1},{193,65... | collective-permute-start | bytes 491528 | tf_op jit(solution)/shard_map/ppermute | solution.py:311
  141.8 14.2 %collective-permute-start.26 = (bf16[640,128]{1,0:T(8,128)(2,1)}, bf16[640,128]{1,0:T(8,128)(2,1)S(1)}, u32[]{:S(2)}, u32[]{:S(2)}) collective-permute-start(bf16[640,128]{1,0:T(8,128)(2,1)} %get-tuple-element.52), channel_id=1, source_target_pairs={{0,64},{64,128},{128,192},{192,0},{1,65},{65,129},{129,193},{193,1... | collective-permute-start | bytes 491528 | tf_op jit(solution)/shard_map/ppermute | solution.py:311
  141.8 10.6 %collective-permute-start.19 = (bf16[320,128]{1,0:T(8,128)(2,1)S(1)}, bf16[320,128]{1,0:T(8,128)(2,1)S(1)}, u32[]{:S(2)}, u32[]{:S(2)}) collective-permute-start(bf16[320,128]{1,0:T(8,128)(2,1)S(1)} %copy-done.34), channel_id=1, source_target_pairs={{0,128},{64,192},{128,0},{192,64},{1,129},{65,193},{129,1},{193,65... | collective-permute-start | bytes 245768 | tf_op jit(solution)/shard_map/ppermute | solution.py:311
  145.2 10.8 %collective-permute-start.20 = (bf16[320,128]{1,0:T(8,128)(2,1)S(1)}, bf16[320,128]{1,0:T(8,128)(2,1)S(1)}, u32[]{:S(2)}, u32[]{:S(2)}) collective-permute-start(bf16[320,128]{1,0:T(8,128)(2,1)S(1)} %copy-done.33), channel_id=1, source_target_pairs={{0,64},{64,128},{128,192},{192,0},{1,65},{65,129},{129,193},{193,1... | collective-permute-start | bytes 245768 | tf_op jit(solution)/shard_map/ppermute | solution.py:311
  (32 other events, 188.2 us)

commit v2 on v1

v2 whole, which is shorter than its diff:
```python
import functools
import math

import jax
import jax.numpy as jnp
from jax import lax
from jax.experimental import pallas as pl
from jax.experimental.pallas import tpu as pltpu
from jax.sharding import Mesh, PartitionSpec as P

HD = 112
W = 128
NX = 4
BLK = 160
OWN = 2 * BLK
QT = 256
QROWS = NX * OWN
NQT = QROWS // QT
HALF = 16 * BLK
SKC = 512
SPER = 4
GKC = 640
GPER = 2
DROWS = QROWS + QT
SCALE = 1.0 / math.sqrt(HD)
LOG2E = math.log2(math.e)
CEXP = SCALE * LOG2E
NEG = -1e30
LIMIT = 56 * 1024 * 1024
F32 = jnp.float32
BF16 = jnp.bfloat16

VM = pl.BlockSpec(memory_space=pltpu.VMEM)
SM = pl.BlockSpec(memory_space=pltpu.SMEM)


def call(kernel, outs, scratch, name, after=0):
    def run(*args):
        specs = [SM if a.dtype == jnp.int32 or a.size <= 8 else VM for a in args]
        if after:
            specs[-after:] = [pl.BlockSpec(memory_space=pl.ANY)] * after
        return pl.pallas_call(
            kernel,
            out_shape=[jax.ShapeDtypeStruct(s, d) for s, d in outs],
            in_specs=specs,
            out_specs=[VM] * len(outs),
            scratch_shapes=scratch,
            compiler_params=pltpu.CompilerParams(vmem_limit_bytes=LIMIT),
            name=name,
        )(*args)

    return run


def ctx_of(ids, s, dyl, dc):
    x = lax.rem(ids[0] + (NX - s), NX)
    yl = ids[1] if dyl == 0 else 1 - ids[1]
    c = ids[2] if dc == 0 else 1 - ids[2]
    return x * 4 + yl * 2 + c


def cotangent_pack_kernel(d_ref, out_ref):
    out_ref[:, :, HD:] = jnp.zeros((64, 20, W - HD), BF16)
    for n in range(64):
        out_ref[(n % NX) * 16 + n // NX, :, :HD] = d_ref[:, n * HD : (n + 1) * HD]


def here():
    return lax.axis_index("x"), lax.axis_index("yl"), lax.axis_index("c")


def key_columns(plan):
    ctx = ctx_of(here(), 0, 0, 0)
    row = lax.broadcasted_iota(jnp.int32, (OWN, W - HD), 0)
    lane = lax.broadcasted_iota(jnp.int32, (OWN, W - HD), 1)
    first, second = plan[2 * ctx] * BLK, plan[2 * ctx + 1] * BLK
    pos = jnp.where(row < BLK, first + row, second + row - BLK)
    high = (pos // 64) * 64
    one = jnp.where(lane < 9, 1, 0)
    return jnp.where(lane < 3, high, jnp.where(lane < 6, pos - high, one)).astype(F32).astype(BF16)


def pack_kernel(extras, plan, a_ref, b_ref, *rest):
    outs, buf = rest[-5:-1], rest[-1]
    if extras == "kv":
        lane = lax.broadcasted_iota(jnp.int32, (OWN, W - HD), 1)
        wide = (key_columns(plan), jnp.where(lane < 3, 1.0, 0.0).astype(BF16))
    else:
        wide = (jnp.zeros((OWN, W - HD), BF16),) * 2
    for n in range(NX):
        for i, ref in enumerate((a_ref, b_ref)):
            rows = slice(i * OWN, (i + 1) * OWN)
            buf[n, rows, :HD] = ref[:, n * HD : (n + 1) * HD]
            buf[n, rows, HD:] = wide[i]
    x = lax.axis_index("x")
    for s in range(NX):
        outs[s][...] = buf[lax.rem(x + s, NX)]


def at(start, size):
    return pl.ds(pl.multiple_of(start, 32), size)


def split3(value):
    a = value.astype(BF16)
    r = value - a.astype(F32)
    b = r.astype(BF16)
    return a, b, (r - b.astype(F32)).astype(BF16)


def sort_keys(ids, tables, row, dyl, pieces, first, swapped, second, dst):
    for s in range(NX):
        for dc in range(2):
            ctx = ctx_of(ids, s, dyl, dc)
            for h in range(2):
                src, base = (pieces[s], first) if dc == 0 else (swapped, 2 * s * OWN + second)
                base = base + h * BLK
                dst[at(tables[row, 2 * ctx + h] * BLK, BLK), :] = src[base : base + BLK, :]


def sort_rows(ids, tables, blocks, dst):
    for s in range(NX):
        ctx = ctx_of(ids, s, 0, 0)
        for h in range(2):
            dst[at(tables[1, 2 * ctx + h] * BLK, BLK), :] = blocks(s, h)


def sort_limits(ids, tables, limits):
    for s in range(NX):
        ctx = ctx_of(ids, s, 0, 0)
        for h in range(2):
            r = tables[1, 2 * ctx + h]
            limits[0, r] = tables[0, 2 * ctx + h]
            limits[1, r] = tables[2, 2 * ctx + h]
            limits[2, r] = tables[3, 2 * ctx + h]


def tile_limits(limits, i, dyl):
    b0, b1 = (QT * i) // BLK, (QT * i + QT - 1) // BLK
    row = lax.broadcasted_iota(jnp.int32, (1, QT), 1) + QT * i
    lim = jnp.zeros((1, QT), jnp.int32)
    for b in range(b0, b1 + 1):
        inside = jnp.logical_and(row >= b * BLK, row < (b + 1) * BLK)
        if dyl == 1:
            value = jnp.broadcast_to(limits[1, b] * BLK - 1, (1, QT))
        else:
            value = limits[dyl, b] * BLK + (row - b * BLK)
        lim = jnp.where(inside, value, lim)
    return lim, limits[dyl, b1] * BLK + (0 if dyl == 1 else BLK)


def list_work(limits, dyl, size, per, work, lims):
    count = jnp.int32(0)
    for i in range(NQT):
        lim, last = tile_limits(limits, i, dyl)
        lims[i] = lim
        n = lax.div(last + size - 1, size)

        def put(k, carry, i=i, count=count):
            work[0, count + k] = i
            work[1, count + k] = k
            return carry

        lax.fori_loop(0, n, put, 0)
        count = count + n
    lims[NQT] = jnp.full((1, QT), -1, jnp.int32)
    for u in range(per - 1):
        work[0, count + u] = NQT
        work[1, count + u] = 0
    return lax.div(count + per - 1, per)


def stats_kernel(tables, slope, *rest):
    ids = here()
    qo, kv, kv_y, kv_c, kv_yc = rest[0:4], rest[4:8], rest[8:12], rest[12], rest[13]
    qs, qt = rest[14:16]
    keys, limits, work, lims, tops, totals = rest[16:22]
    sort_keys(ids, tables, 3, 0, kv, 0, kv_c, 0, keys)
    sort_keys(ids, tables, 3, 1, kv_y, 0, kv_yc, 0, keys)
    sort_rows(ids, tables, lambda s, h: qo[s][h * BLK : (h + 1) * BLK, :], qs)
    qs[QROWS:, :] = jnp.zeros((QT, W), BF16)
    sort_limits(ids, tables, limits)
    m1, m2, m3 = split3(jnp.full((1, QT), slope[0] / SCALE, F32))
    for i in range(NQT):
        qt[i] = qs[i * QT : (i + 1) * QT, :].T
        qt[i, HD : HD + 16, :] = jnp.concatenate(
            [m1, m2, m3, m1, m2, m3, jnp.zeros((10, QT), BF16)], axis=0
        )
    qt[NQT] = jnp.zeros((W, QT), BF16)
    steps = list_work(limits, 2, SKC, SPER, work, lims)
    tops[...] = jnp.full(tops.shape, NEG, F32)
    totals[...] = jnp.zeros(totals.shape, F32)

    def step(j, carry):
        for u in range(SPER):
            item = j * SPER + u
            tile, chunk = work[0, item], work[1, item]
            s = jnp.dot(keys[at(chunk * SKC, SKC), :], qt[tile], preferred_element_type=F32)
            index = lax.broadcasted_iota(jnp.int32, (SKC, QT), 0)
            s = jnp.where(index <= lims[tile] - chunk * SKC, s, NEG)
            s = s.reshape(SKC // 8, 8, QT)
            top = jnp.max(s, axis=0)
            tops[tile, chunk] = top
            totals[tile, chunk] = jnp.sum(jnp.exp2((s - top[None]) * CEXP), axis=0)
        return carry

    lax.fori_loop(0, steps, step, 0)
    for i in range(NQT):
        top = jnp.max(jnp.max(tops[i], axis=0), axis=0, keepdims=True)
        total8 = jnp.sum(totals[i] * jnp.exp2((tops[i] - top) * CEXP), axis=0)
        total = jnp.sum(total8, axis=0, keepdims=True)
        l1, l2, l3 = split3(-(top + jnp.log(total) * (1.0 / SCALE)))
        qt[i, HD : HD + 16, :] = jnp.concatenate(
            [m1, m2, m3, m1, m2, m3, l1, l2, l3, jnp.zeros((7, QT), BF16)], axis=0
        )


def grads_loop(dyl, keys, vals, qs, qt, dos, dot, limits, dkey, dval, dq, work, lims):
    dkey[...] = jnp.zeros((HALF, W), F32)
    dval[...] = jnp.zeros((HALF, W), F32)
    steps = list_work(limits, dyl, GKC, GPER, work, lims)

    def step(j, carry):
        parts = []
        for u in range(GPER):
            item = j * GPER + u
            tile, chunk = work[0, item], work[1, item]
            rows = at(chunk * GKC, GKC)
            cols = at(tile * QT, QT)
            kc = keys[rows, :]
            s = jnp.dot(kc, qt[tile], preferred_element_type=F32)
            index = lax.broadcasted_iota(jnp.int32, (GKC, QT), 0)
            p = jnp.where(index <= lims[tile] - chunk * GKC, jnp.exp2(s * CEXP), 0.0)
            dp = jnp.dot(vals[rows, :], dot[tile], preferred_element_type=F32)
            ds = (p * dp).astype(BF16)
            dv = jnp.dot(p.astype(BF16), dos[cols, :], preferred_element_type=F32)
            dk = jnp.dot(ds, qs[cols, :], preferred_element_type=F32)
            d = lax.dot_general(ds, kc, (((0,), (0,)), ((), ())), preferred_element_type=F32)
            parts.append((rows, cols, dv, dk, d))
        for rows, cols, dv, dk, d in parts:
            dval[rows, :] += dv
            dkey[rows, :] += dk
            dq[cols, :] += d
        return carry

    lax.fori_loop(0, steps, step, 0)


def unsort(ids, tables, dyl, dc, dkey, dval, out):
    for s in range(NX):
        ctx = ctx_of(ids, s, dyl, dc)
        for h in range(2):
            rows = at(tables[0, 2 * ctx + h] * BLK, BLK)
            base = s * 2 * OWN + h * BLK
            out[base : base + BLK, :] = (dkey[rows, :] * SCALE).astype(BF16)
            out[base + OWN : base + OWN + BLK, :] = dval[rows, :].astype(BF16)


def grads_other_kernel(tables, *rest):
    ids = here()
    qo, kv_y, kv_yc = rest[0:4], rest[4:8], rest[8]
    dor, qs, qt = rest[9:12]
    dos, dot, dq, keep, send = rest[12:17]
    keys, vals, dkey, dval, work, lims, flat, outs, limits = rest[17:26]
    sort_keys(ids, tables, 0, 1, kv_y, 0, kv_yc, 0, keys)
    sort_keys(ids, tables, 0, 1, kv_y, OWN, kv_yc, OWN, vals)
    sort_limits(ids, tables, limits)
    for n in range(64):
        flat[n * 20 : (n + 1) * 20, :] = dor[n]

    def block(s, h):
        x = lax.rem(ids[0] + (NX - s), NX)
        return flat[at(x * OWN + h * BLK, BLK), :]

    sort_rows(ids, tables, block, dos)
    sort_rows(ids, tables, lambda s, h: qo[s][OWN + h * BLK : OWN + (h + 1) * BLK, :], outs)
    for i in range(NQT):
        cols = slice(i * QT, (i + 1) * QT)
        prod = dos[cols, :].astype(F32) * outs[cols, :].astype(F32)
        delta = jnp.sum(prod.T, axis=0, keepdims=True)
        d1, d2, d3 = split3(-delta)
        dot[i] = dos[cols, :].T
        dot[i, HD : HD + 16, :] = jnp.concatenate(
            [d1, d2, d3, jnp.zeros((13, QT), BF16)], axis=0
        )
    dot[NQT] = jnp.zeros((W, QT), BF16)
    dos[QROWS:, :] = jnp.zeros((QT, W), BF16)
    dq[...] = jnp.zeros((DROWS, W), F32)
    grads_loop(1, keys, vals, qs, qt, dos, dot, limits, dkey, dval, dq, work, lims)
    unsort(ids, tables, 1, 0, dkey, dval, keep)
    unsort(ids, tables, 1, 1, dkey, dval, send)


def grads_own_kernel(tables, *rest):
    ids = here()
    kv, kv_c = rest[0:4], rest[4]
    qs, qt, dos, dot, dq_in = rest[5:10]
    dqo, keep, send = rest[10:13]
    keys, vals, dkey, dval, work, lims, dq, limits = rest[13:21]
    sort_keys(ids, tables, 0, 0, kv, 0, kv_c, 0, keys)
    sort_keys(ids, tables, 0, 0, kv, OWN, kv_c, OWN, vals)
    sort_limits(ids, tables, limits)
    dq[...] = dq_in[...]
    grads_loop(0, keys, vals, qs, qt, dos, dot, limits, dkey, dval, dq, work, lims)
    unsort(ids, tables, 0, 0, dkey, dval, keep)
    unsort(ids, tables, 0, 1, dkey, dval, send)
    for s in range(NX):
        ctx = ctx_of(ids, s, 0, 0)
        for h in range(2):
            rows = at(tables[1, 2 * ctx + h] * BLK, BLK)
            base = s * OWN + h * BLK
            dqo[base : base + BLK, :] = (dq[rows, :] * SCALE).astype(BF16)


def add_kernel(a, b, out):
    out[...] = (a[...].astype(F32) + b[...].astype(F32)).astype(BF16)


def add_own_kernel(a, b, c, dq, *outs):
    for s in range(NX):
        rows = slice(s * 2 * OWN, (s + 1) * 2 * OWN)
        outs[s][:OWN, :] = dq[s * OWN : (s + 1) * OWN, :]
        total = a[rows, :].astype(F32) + b[rows, :].astype(F32) + c[rows, :].astype(F32)
        outs[s][OWN:, :] = total.astype(BF16)


def unpack_kernel(*rest):
    pieces, outs, buf = rest[0:4], rest[4:7], rest[7]
    x = lax.axis_index("x")
    for s in range(NX):
        buf[lax.rem(x + s, NX)] = pieces[s][...]
    for n in range(NX):
        for i in range(3):
            outs[i][:, n * HD : (n + 1) * HD] = buf[n, i * OWN : (i + 1) * OWN, :HD]


def shift(value, by, flip=False):
    pairs = []
    for x in range(NX):
        for yl in range(2):
            pairs.append((2 * x + yl, 2 * ((x + by) % NX) + (1 - yl if flip else yl)))
    return lax.ppermute(value, ("x", "yl"), pairs)


def swap_core(value):
    return lax.ppermute(value, "c", [(0, 1), (1, 0)])


def worklist(size, keys, per):
    items = NQT * (keys // size) + per
    return [pltpu.SMEM((2, items), jnp.int32), pltpu.VMEM((NQT + 1, 1, QT), jnp.int32)]


def plan_tables(plan):
    block = jnp.arange(32, dtype=jnp.int32)
    half = (block >> 2) & 1
    group = (block >> 1) & 3
    before = plan[None, :] < plan[:, None]
    same_half = half[None, :] == half[:, None]
    same_group = group[None, :] == group[:, None]

    def count(m):
        return jnp.sum(jnp.where(jnp.logical_and(before, m), 1, 0), axis=1, dtype=jnp.int32)

    return jnp.stack([count(same_half), count(same_group), count(jnp.logical_not(same_half)), plan])


def on_device(queries, keys, values, out_fwd, d_out, plan):
    piece = ((2 * OWN, W), BF16)
    stack = ((NX * 2 * OWN, W), BF16)
    x = lax.axis_index("x")
    tables = plan_tables(plan)
    head_id = (lax.axis_index("yh") * 8 + lax.axis_index("z")) * NX + x
    slope = jnp.exp2(-8.0 * (head_id + 1).astype(F32) / 64.0).reshape(1)

    buf = [pltpu.VMEM((NX, 2 * OWN, W), BF16)]
    kv = call(functools.partial(pack_kernel, "kv"), [piece] * 4, buf, "pack_kv")(plan, keys, values)
    kv, d_out = lax.optimization_barrier((kv, d_out))
    (d_pack,) = call(cotangent_pack_kernel, [((64, 20, W), BF16)], [], "cotangent_pack")(d_out)
    d_rows = lax.all_to_all(d_pack, ("x", "yh", "z"), 0, 0)
    kv = [kv[0]] + [shift(kv[s], s) for s in (1, 2, 3)]
    qo = call(functools.partial(pack_kernel, "qo"), [piece] * 4, buf, "pack_qo", 4)(
        plan, queries, out_fwd, *kv[1:], tables
    )
    kv_y = [shift(a, 0, True) for a in kv]
    qo = [qo[0]] + [shift(qo[s], s) for s in (1, 2, 3)]
    kv_y, qo, d_rows = lax.optimization_barrier((kv_y, qo, d_rows))
    kv_c = swap_core(jnp.concatenate(kv))
    kv_yc = swap_core(jnp.concatenate(kv_y))

    limits = pltpu.SMEM((3, 8), jnp.int32)
    qs, qt = call(
        stats_kernel,
        [((DROWS, W), BF16), ((NQT + 1, W, QT), BF16)],
        [pltpu.VMEM((2 * HALF, W), BF16), limits]
        + worklist(SKC, 2 * HALF, SPER)
        + [pltpu.VMEM((NQT + 1, 2 * HALF // SKC, 8, QT), F32)] * 2,
        "stats",
    )(tables, slope, *qo, *kv, *kv_y, kv_c, kv_yc)
    accs = [pltpu.VMEM((HALF, W), BF16)] * 2 + [pltpu.VMEM((HALF, W), F32)] * 2
    accs = accs + worklist(GKC, HALF, GPER)
    dos, dot, dq, keep, send = call(
        grads_other_kernel,
        [((DROWS, W), BF16), ((NQT + 1, W, QT), BF16), ((DROWS, W), F32), stack, stack],
        accs + [pltpu.VMEM((QROWS, W), BF16)] * 2 + [limits],
        "grads_other",
    )(tables, *qo, *kv_y, kv_yc, d_rows, qs, qt)
    (dkv_y,) = call(add_kernel, [stack], [], "add_other")(keep, swap_core(send))
    dq, dkv_y = lax.optimization_barrier((dq, dkv_y))
    dkv_y = shift(dkv_y, 0, True)

    dq, keep, send = call(
        grads_own_kernel,
        [((QROWS, W), BF16), stack, stack],
        accs + [pltpu.VMEM((DROWS, W), F32), limits],
        "grads_own",
    )(tables, *kv, kv_c, qs, qt, dos, dot, dq)
    send, dkv_y = lax.optimization_barrier((send, dkv_y))
    grads = call(add_own_kernel, [((3 * OWN, W), BF16)] * 4, [], "add_own")(
        keep, swap_core(send), dkv_y, dq
    )
    grads = [grads[0]] + [shift(grads[s], -s) for s in (1, 2, 3)]
    return tuple(
        call(
            unpack_kernel,
            [((OWN, NX * HD), BF16)] * 3,
            [pltpu.VMEM((NX, 3 * OWN, W), BF16)],
            "unpack",
        )(*grads)
    )


def solution(mesh):
    devices = mesh.devices.reshape(4, 2, 2, 2, 8)
    fine = Mesh(devices, ("x", "yl", "c", "yh", "z"))
    ctx, head = ("x", "yl", "c"), ("yh", "z")
    tile = P(ctx, head)
    return jax.shard_map(
        on_device,
        mesh=fine,
        in_specs=(tile, tile, tile, tile, P(ctx + head, None), P()),
        out_specs=(tile, tile, tile),
        check_vma=False,
    )
```

time: 161 us -> 119 us (0.74); the launches traced: 160 us -> 120 us
  Pallas kernels: 68.3 us -> 52.4 us
  starting transfers between devices: 47.1 us -> 33.7 us
  waiting for transfers between devices: 37.2 us -> 24.5 us
  other arithmetic: 1.5 us -> 3.79 us
    pallas_call x8 -> x9, Pallas kernels: 68.3 us -> 52.4 us  [run(): pl.pallas_call(kernel, out_shape=[jax.ShapeDtypeStruct(s, d) for s, d in...]
    ppermute x27 -> x18, starting transfers between devices: 35.1 us -> 22.1 us  [the longest x14 15.4 us: shift(): return lax.ppermute(value, ('x', 'yl'), pairs)]
    ppermute x27 -> x18, waiting for transfers between devices: 37.2 us -> 24.5 us  [the longest x14 18.4 us: shift(): return lax.ppermute(value, ('x', 'yl'), pairs)]
    concatenate x0 -> x2, other arithmetic: none -> 2.96 us  [the longest x1 1.97 us: on_device(): kv_c = swap_core(jnp.concatenate(kv))]
    unnamed x72 -> x42, local copies, waits for them, and re-layouts: 4.52 us -> 4.57 us
  transfers between devices with their start and end apart: 28 -> 19, of which waited for: 7 -> 8; matrix products, arithmetic and copies ran while one was open for 0% -> 3% of each run, Pallas kernels for 27% -> 14%
where the time goes in v2:
time: 119 us; the launch traced here: 120 us
  Pallas kernels  52.4 us (44%)
  starting transfers between devices  33.7 us (28%)
  waiting for transfers between devices  24.5 us (21%)
  local copies, waits for them, and re-layouts  4.57 us (4%)
  other arithmetic  3.79 us (3%)
    pallas_call x9, Pallas kernels, run(): pl.pallas_call(kernel, out_shape=[jax.ShapeDtypeStruct(s, d) for s, d in...  52.4 us
    ppermute x14, waiting for transfers between devices, shift(): return lax.ppermute(value, ('x', 'yl'), pairs)  18.4 us
    ppermute x14, starting transfers between devices, shift(): return lax.ppermute(value, ('x', 'yl'), pairs)  15.4 us
    all_to_all x1, starting transfers between devices, on_device(): d_rows = lax.all_to_all(d_pack, ('x', 'yh', 'z'), 0, 0)  11.6 us
    ppermute x4, starting transfers between devices, swap_core(): return lax.ppermute(value, 'c', [(0, 1), (1, 0)])  6.68 us
    ppermute x4, waiting for transfers between devices, swap_core(): return lax.ppermute(value, 'c', [(0, 1), (1, 0)])  6.11 us
    unnamed x42, local copies, waits for them, and re-layouts  4.57 us
  transfers between devices with their start and end apart: 19, of which 8 were waited for; matrix products, arithmetic and copies ran while one was open for 3% of the time, Pallas kernels for 14%

profile of v2, /device:TPU:1, one launch (start us, length us, event | category | flops | bytes accessed | tf_op | source)
XLA Modules:
  0.0 119.8 jit_solution(3469807986779668245)
XLA Ops:
  0.6 2.5 %pack_kv.1 = (bf16[640,128]{1,0:T(8,128)(2,1)}, bf16[640,128]{1,0:T(8,128)(2,1)}, bf16[640,128]{1,0:T(8,128)(2,1)}, bf16[640,128]{1,0:T(8,128)(2,1)}) custom-call(s32[32]{0:T(128)} %plan.3, bf16[320,448]{1,0:T(8,128)(2,1)} %a_ref.2, bf16[320,448]{1,0:T(8,128)(2,1)} %b_ref.2), custom_call_target="tpu_custom_call" | custom-call | tf_op jit(solution)/shard_map/pack_kv/pallas_call | solution.py:42
  3.2 2.0 %collective-permute-start = (bf16[640,128]{1,0:T(8,128)(2,1)}, bf16[640,128]{1,0:T(8,128)(2,1)S(1)}, u32[]{:S(2)}, u32[]{:S(2)}) collective-permute-start(bf16[640,128]{1,0:T(8,128)(2,1)} %get-tuple-element.48), channel_id=1, source_target_pairs={{0,64},{32,96},{64,128},{96,160},{128,192},{160,224},{192,0},{224,... | collective-permute-start | bytes 491528 | tf_op jit(solution)/shard_map/ppermute | solution.py:342
  5.2 2.5 %collective-permute-start.1 = (bf16[640,128]{1,0:T(8,128)(2,1)}, bf16[640,128]{1,0:T(8,128)(2,1)S(1)}, u32[]{:S(2)}, u32[]{:S(2)}) collective-permute-start(bf16[640,128]{1,0:T(8,128)(2,1)} %get-tuple-element.49), channel_id=1, source_target_pairs={{0,128},{32,160},{64,192},{96,224},{128,0},{160,32},{192,64},{224,... | collective-permute-start | bytes 491528 | tf_op jit(solution)/shard_map/ppermute | solution.py:342
  7.7 1.2 collective-permute-start.2
  8.8 1.3 %collective-permute-start.4 = (bf16[640,128]{1,0:T(8,128)(2,1)}, bf16[640,128]{1,0:T(8,128)(2,1)S(1)}, u32[]{:S(2)}, u32[]{:S(2)}) collective-permute-start(bf16[640,128]{1,0:T(8,128)(2,1)} %get-tuple-element.47.rest_4_.rest_0_), channel_id=1, source_target_pairs={{0,32},{32,0},{64,96},{96,64},{128,160},{160,128},{192,224},{224,1... | collective-permute-start | bytes 491528 | tf_op jit(solution)/shard_map/ppermute | solution.py:342
  10.1 2.0 %cotangent_pack.1 = bf16[64,20,128]{2,1,0:T(8,128)(2,1)} custom-call(bf16[20,7168]{1,0:T(8,128)(2,1)} %d_ref), custom_call_target="tpu_custom_call" | custom-call | tf_op jit(solution)/shard_map/cotangent_pack/pallas_call | solution.py:42
  12.1 11.6 %all-to-all-start = ((bf16[64,20,128]{2,1,0:T(8,128)(2,1)}), bf16[64,20,128]{2,1,0:T(8,128)(2,1)S(1)}, u32[]{:S(2)}, u32[]{:S(2)}) async-start(bf16[64,20,128]{2,1,0:T(8,128)(2,1)} %cotangent_pack.1), calls=%async_computation | async-start | bytes 786432 | tf_op jit(solution)/shard_map/all_to_all | solution.py:380
  26.0 2.4 %pack_qo.1 = (bf16[640,128]{1,0:T(8,128)(2,1)}, bf16[640,128]{1,0:T(8,128)(2,1)}, bf16[640,128]{1,0:T(8,128)(2,1)}, bf16[640,128]{1,0:T(8,128)(2,1)}) custom-call(s32[32]{0:T(128)} %plan.3, bf16[320,448]{1,0:T(8,128)(2,1)} %a_ref.3, bf16[320,448]{1,0:T(8,128)(2,1)} %b_ref.3, bf16[640,128]{1,0:T(8,128)(2,1)} %copy-done, bf16[640,128]{1,0:T(8,128)(2,1)} %copy-done.1, ...), custom_call_target="tpu_custom_call" | custom-call | tf_op jit(solution)/shard_map/pack_qo/pallas_call | solution.py:42
  28.4 1.0 collective-permute-start.8
  29.4 2.6 %collective-permute-start.9 = (bf16[640,128]{1,0:T(8,128)(2,1)}, bf16[640,128]{1,0:T(8,128)(2,1)S(1)}, u32[]{:S(2)}, u32[]{:S(2)}) collective-permute-start(bf16[640,128]{1,0:T(8,128)(2,1)} %get-tuple-element.53), channel_id=1, source_target_pairs={{0,128},{32,160},{64,192},{96,224},{128,0},{160,32},{192,64},{224,... | collective-permute-start | bytes 491528 | tf_op jit(solution)/shard_map/ppermute | solution.py:342
  32.0 1.1 collective-permute-start.10
  33.0 1.4 %collective-permute-start.6 = (bf16[640,128]{1,0:T(8,128)(2,1)}, bf16[640,128]{1,0:T(8,128)(2,1)S(1)}, u32[]{:S(2)}, u32[]{:S(2)}) collective-permute-start(bf16[640,128]{1,0:T(8,128)(2,1)} %copy-done.1), channel_id=1, source_target_pairs={{0,32},{32,0},{64,96},{96,64},{128,160},{160,128},{192,224},{224,1... | collective-permute-start | bytes 491528 | tf_op jit(solution)/shard_map/ppermute | solution.py:342
  34.6 2.0 %pad_maximum_fusion = bf16[2560,128]{1,0:T(8,128)(2,1)} fusion(bf16[640,128]{1,0:T(8,128)(2,1)} %copy-done.2, bf16[640,128]{1,0:T(8,128)(2,1)} %copy-done.1, bf16[640,128]{1,0:T(8,128)(2,1)} %copy-done, bf16[640,128]{1,0:T(8,128)(2,1)S(1)} %copy-done.6), kind=kLoop, calls=%fused_computation | loop fusion | flops 2621440 | bytes 1310720 | tf_op jit(solution)/shard_map/concatenate | solution.py:388
  36.6 1.5 %collective-permute-done.6.rest_10_.rest_6_ = bf16[640,128]{1,0:T(8,128)(2,1)S(1)} collective-permute-done((bf16[640,128]{1,0:T(8,128)(2,1)}, bf16[640,128]{1,0:T(8,128)(2,1)S(1)}, u32[]{:S(2)}, u32[]{:S(2)}) %collective-permute-start.6) | collective-permute-done | bytes 163872 | tf_op jit(solution)/shard_map/ppermute | solution.py:342
  38.1 3.9 %collective-permute-start.3 = (bf16[2560,128]{1,0:T(8,128)(2,1)}, bf16[2560,128]{1,0:T(8,128)(2,1)S(1)}, u32[]{:S(2)}, u32[]{:S(2)}) collective-permute-start(bf16[2560,128]{1,0:T(8,128)(2,1)} %pad_maximum_fusion), channel_id=1, source_target_pairs={{0,16},{16,0},{1,17},{17,1},{2,18},{18,2},{3,19},{19,3},{4,20},{20... | collective-permute-start | bytes 1966088 | tf_op jit(solution)/shard_map/ppermute | solution.py:346
  42.0 1.0 pad_maximum_fusion.1
  43.0 1.8 %collective-permute-start.11 = (bf16[2560,128]{1,0:T(8,128)(2,1)}, bf16[2560,128]{1,0:T(8,128)(2,1)S(1)}, u32[]{:S(2)}, u32[]{:S(2)}) collective-permute-start(bf16[2560,128]{1,0:T(8,128)(2,1)} %pad_maximum_fusion.1), channel_id=1, source_target_pairs={{0,16},{16,0},{1,17},{17,1},{2,18},{18,2},{3,19},{19,3},{4,20},{20... | collective-permute-start | bytes 1966088 | tf_op jit(solution)/shard_map/ppermute | solution.py:346
  44.9 1.9 %collective-permute-done.11.rest_13_.rest_8_ = bf16[2560,128]{1,0:T(8,128)(2,1)S(1)} collective-permute-done((bf16[2560,128]{1,0:T(8,128)(2,1)}, bf16[2560,128]{1,0:T(8,128)(2,1)S(1)}, u32[]{:S(2)}, u32[]{:S(2)}) %collective-permute-start.11) | collective-permute-done | bytes 655392 | tf_op jit(solution)/shard_map/ppermute | solution.py:346
  47.6 11.0 %stats.1 = (bf16[1536,128]{1,0:T(8,128)(2,1)}, bf16[6,128,256]{2,1,0:T(8,128)(2,1)}) custom-call(s32[4,32]{1,0:T(4,128)} %pad_add_fusion.rest_3_.tables, f32[1]{0:T(128)} %bitcast.4.slope, bf16[640,128]{1,0:T(8,128)(2,1)} %get-tuple-element.56.rest_0_, bf16[640,128]{1,0:T(8,128)(2,1)} %copy-done.11, bf16[640,128]{1,0:T(8,128)(2,1)} %copy-done.12, ...), custom_call_target="tpu_custom_call" | custom-call | tf_op jit(solution)/shard_map/stats/pallas_call | solution.py:42
  58.6 14.3 %grads_other.1 = (bf16[1536,128]{1,0:T(8,128)(2,1)}, bf16[6,128,256]{2,1,0:T(8,128)(2,1)}, f32[1536,128]{1,0:T(8,128)}, bf16[2560,128]{1,0:T(8,128)(2,1)}, bf16[2560,128]{1,0:T(8,128)(2,1)}) custom-call(s32[4,32]{1,0:T(4,128)} %pad_add_fusion.rest_3_.tables, bf16[640,128]{1,0:T(8,128)(2,1)} %get-tuple-element.56.rest_0_, bf16[640,128]{1,0:T(8,128)(2,1)} %copy-done.11, ...), custom_call_target="tpu_custom_call" | custom-call | tf_op jit(solution)/shard_map/grads_other/pallas_call | solution.py:42
  72.9 2.3 %collective-permute-done.12.b = bf16[2560,128]{1,0:T(8,128)(2,1)S(1)} collective-permute-done((bf16[2560,128]{1,0:T(8,128)(2,1)}, bf16[2560,128]{1,0:T(8,128)(2,1)S(1)}, u32[]{:S(2)}, u32[]{:S(2)}) %collective-permute-start.12) | collective-permute-done | bytes 655392 | tf_op jit(solution)/shard_map/ppermute | solution.py:346
  76.1 2.3 %add_other.1 = bf16[2560,128]{1,0:T(8,128)(2,1)} custom-call(bf16[2560,128]{1,0:T(8,128)(2,1)} %get-tuple-element.70.a, bf16[2560,128]{1,0:T(8,128)(2,1)} %copy-done.16), custom_call_target="tpu_custom_call" | custom-call | tf_op jit(solution)/shard_map/add_other/pallas_call | solution.py:42
  78.4 12.5 %grads_own.1 = (bf16[1280,128]{1,0:T(8,128)(2,1)}, bf16[2560,128]{1,0:T(8,128)(2,1)}, bf16[2560,128]{1,0:T(8,128)(2,1)}) custom-call(s32[4,32]{1,0:T(4,128)} %pad_add_fusion.rest_3_.tables, bf16[640,128]{1,0:T(8,128)(2,1)} %get-tuple-element.47.rest_4_.rest_0_, bf16[640,128]{1,0:T(8,128)(2,1)} %copy-done, bf16[640,128]{1,0:T(8,128)(2,1)} %copy-done.1, ...), custom_call_target="tpu_custom_call" | custom-call | tf_op jit(solution)/shard_map/grads_own/pallas_call | solution.py:42
  90.9 3.9 %collective-permute-done.13.c = bf16[2560,128]{1,0:T(8,128)(2,1)S(1)} collective-permute-done((bf16[2560,128]{1,0:T(8,128)(2,1)}, bf16[2560,128]{1,0:T(8,128)(2,1)S(1)}, u32[]{:S(2)}, u32[]{:S(2)}) %collective-permute-start.13) | collective-permute-done | bytes 655392 | tf_op jit(solution)/shard_map/ppermute | solution.py:342
  94.8 1.0 collective-permute-start.14
  95.7 1.9 %collective-permute-done.14.b = bf16[2560,128]{1,0:T(8,128)(2,1)S(1)} collective-permute-done((bf16[2560,128]{1,0:T(8,128)(2,1)}, bf16[2560,128]{1,0:T(8,128)(2,1)S(1)}, u32[]{:S(2)}, u32[]{:S(2)}) %collective-permute-start.14) | collective-permute-done | bytes 655392 | tf_op jit(solution)/shard_map/ppermute | solution.py:346
  98.5 2.6 %add_own.1 = (bf16[960,128]{1,0:T(8,128)(2,1)}, bf16[960,128]{1,0:T(8,128)(2,1)}, bf16[960,128]{1,0:T(8,128)(2,1)}, bf16[960,128]{1,0:T(8,128)(2,1)}) custom-call(bf16[2560,128]{1,0:T(8,128)(2,1)} %get-tuple-element.73.a, bf16[2560,128]{1,0:T(8,128)(2,1)} %copy-done.15, bf16[2560,128]{1,0:T(8,128)(2,1)} %copy-done.14, bf16[1280,128]{1,0:T(8,128)(2,1)} %get-tuple-element.78.dq), custom_call_target="tpu_custom_call" | custom-call | tf_op jit(solution)/shard_map/add_own/pallas_call | solution.py:42
  101.4 1.9 %collective-permute-start.16 = (bf16[960,128]{1,0:T(8,128)(2,1)}, bf16[960,128]{1,0:T(8,128)(2,1)S(1)}, u32[]{:S(2)}, u32[]{:S(2)}) collective-permute-start(bf16[960,128]{1,0:T(8,128)(2,1)} %get-tuple-element.81), channel_id=1, source_target_pairs={{0,128},{32,160},{64,192},{96,224},{128,0},{160,32},{192,64},{224,... | collective-permute-start | bytes 737288 | tf_op jit(solution)/shard_map/ppermute | solution.py:342
  103.3 5.2 %collective-permute-done.15.rest_1_ = bf16[960,128]{1,0:T(8,128)(2,1)S(1)} collective-permute-done((bf16[960,128]{1,0:T(8,128)(2,1)}, bf16[960,128]{1,0:T(8,128)(2,1)S(1)}, u32[]{:S(2)}, u32[]{:S(2)}) %collective-permute-start.15) | collective-permute-done | bytes 245792 | tf_op jit(solution)/shard_map/ppermute | solution.py:342
  108.5 1.5 %collective-permute-done.16.rest_2_ = bf16[960,128]{1,0:T(8,128)(2,1)S(1)} collective-permute-done((bf16[960,128]{1,0:T(8,128)(2,1)}, bf16[960,128]{1,0:T(8,128)(2,1)S(1)}, u32[]{:S(2)}, u32[]{:S(2)}) %collective-permute-start.16) | collective-permute-done | bytes 245792 | tf_op jit(solution)/shard_map/ppermute | solution.py:342
  110.0 6.3 %collective-permute-done.17.rest_3_ = bf16[960,128]{1,0:T(8,128)(2,1)S(1)} collective-permute-done((bf16[960,128]{1,0:T(8,128)(2,1)}, bf16[960,128]{1,0:T(8,128)(2,1)S(1)}, u32[]{:S(2)}, u32[]{:S(2)}) %collective-permute-start.17) | collective-permute-done | bytes 245792 | tf_op jit(solution)/shard_map/ppermute | solution.py:342
  117.0 2.9 %unpack.1 = (bf16[320,448]{1,0:T(8,128)(2,1)}, bf16[320,448]{1,0:T(8,128)(2,1)}, bf16[320,448]{1,0:T(8,128)(2,1)}) custom-call(bf16[960,128]{1,0:T(8,128)(2,1)} %get-tuple-element.79.rest_0_, bf16[960,128]{1,0:T(8,128)(2,1)} %copy-done.17, bf16[960,128]{1,0:T(8,128)(2,1)} %copy-done.18, bf16[960,128]{1,0:T(8,128)(2,1)} %copy-done.19), custom_call_target="tpu_custom_call" | custom-call | tf_op jit(solution)/shard_map/unpack/pallas_call | solution.py:42
  (62 shorter events, 5.9 us)
Async XLA Ops:
  3.2 20.6 %copy-start.20 = (s32[32]{0:T(128)S(1)}, s32[32]{0:T(128)}, u32[]{:S(2)}) copy-start(s32[32]{0:T(128)} %plan.3) | copy-start | bytes 388
  3.2 20.5 %collective-permute-start = (bf16[640,128]{1,0:T(8,128)(2,1)}, bf16[640,128]{1,0:T(8,128)(2,1)S(1)}, u32[]{:S(2)}, u32[]{:S(2)}) collective-permute-start(bf16[640,128]{1,0:T(8,128)(2,1)} %get-tuple-element.48), channel_id=1, source_target_pairs={{0,64},{32,96},{64,128},{96,160},{128,192},{160,224},{192,0},{224,... | collective-permute-start | bytes 491528 | tf_op jit(solution)/shard_map/ppermute | solution.py:342
  5.2 19.4 %collective-permute-start.1 = (bf16[640,128]{1,0:T(8,128)(2,1)}, bf16[640,128]{1,0:T(8,128)(2,1)S(1)}, u32[]{:S(2)}, u32[]{:S(2)}) collective-permute-start(bf16[640,128]{1,0:T(8,128)(2,1)} %get-tuple-element.49), channel_id=1, source_target_pairs={{0,128},{32,160},{64,192},{96,224},{128,0},{160,32},{192,64},{224,... | collective-permute-start | bytes 491528 | tf_op jit(solution)/shard_map/ppermute | solution.py:342
  7.7 17.0 %collective-permute-start.2 = (bf16[640,128]{1,0:T(8,128)(2,1)}, bf16[640,128]{1,0:T(8,128)(2,1)S(1)}, u32[]{:S(2)}, u32[]{:S(2)}) collective-permute-start(bf16[640,128]{1,0:T(8,128)(2,1)} %get-tuple-element.50), channel_id=1, source_target_pairs={{0,192},{32,224},{64,0},{96,32},{128,64},{160,96},{192,128},{224,1... | collective-permute-start | bytes 491528 | tf_op jit(solution)/shard_map/ppermute | solution.py:342
  8.8 24.2 %collective-permute-start.4 = (bf16[640,128]{1,0:T(8,128)(2,1)}, bf16[640,128]{1,0:T(8,128)(2,1)S(1)}, u32[]{:S(2)}, u32[]{:S(2)}) collective-permute-start(bf16[640,128]{1,0:T(8,128)(2,1)} %get-tuple-element.47.rest_4_.rest_0_), channel_id=1, source_target_pairs={{0,32},{32,0},{64,96},{96,64},{128,160},{160,128},{192,224},{224,1... | collective-permute-start | bytes 491528 | tf_op jit(solution)/shard_map/ppermute | solution.py:342
  12.1 29.9 %all-to-all-start = ((bf16[64,20,128]{2,1,0:T(8,128)(2,1)}), bf16[64,20,128]{2,1,0:T(8,128)(2,1)S(1)}, u32[]{:S(2)}, u32[]{:S(2)}) async-start(bf16[64,20,128]{2,1,0:T(8,128)(2,1)} %cotangent_pack.1), calls=%async_computation | async-start | bytes 786432 | tf_op jit(solution)/shard_map/all_to_all | solution.py:380
  23.7 10.9 %copy-start.6 = (bf16[640,128]{1,0:T(8,128)(2,1)S(1)}, bf16[640,128]{1,0:T(8,128)(2,1)}, u32[]{:S(2)}) copy-start(bf16[640,128]{1,0:T(8,128)(2,1)} %get-tuple-element.47.rest_4_.rest_0_) | copy-start | bytes 491524
  23.7 10.8 %collective-permute-start.5 = (bf16[640,128]{1,0:T(8,128)(2,1)S(1)}, bf16[640,128]{1,0:T(8,128)(2,1)S(1)}, u32[]{:S(2)}, u32[]{:S(2)}) collective-permute-start(bf16[640,128]{1,0:T(8,128)(2,1)S(1)} %collective-permute-done.rest_0_.rest_5_.rest_1_), channel_id=1, source_target_pairs={{0,32},{32,0},{64,96},{96,64},{128,160},{160,128},{192,224},{224,1... | collective-permute-start | bytes 491528 | tf_op jit(solution)/shard_map/ppermute | solution.py:342
  28.4 13.6 %collective-permute-start.8 = (bf16[640,128]{1,0:T(8,128)(2,1)}, bf16[640,128]{1,0:T(8,128)(2,1)S(1)}, u32[]{:S(2)}, u32[]{:S(2)}) collective-permute-start(bf16[640,128]{1,0:T(8,128)(2,1)} %get-tuple-element.52), channel_id=1, source_target_pairs={{0,64},{32,96},{64,128},{96,160},{128,192},{160,224},{192,0},{224,... | collective-permute-start | bytes 491528 | tf_op jit(solution)/shard_map/ppermute | solution.py:342
  29.4 12.6 %collective-permute-start.9 = (bf16[640,128]{1,0:T(8,128)(2,1)}, bf16[640,128]{1,0:T(8,128)(2,1)S(1)}, u32[]{:S(2)}, u32[]{:S(2)}) collective-permute-start(bf16[640,128]{1,0:T(8,128)(2,1)} %get-tuple-element.53), channel_id=1, source_target_pairs={{0,128},{32,160},{64,192},{96,224},{128,0},{160,32},{192,64},{224,... | collective-permute-start | bytes 491528 | tf_op jit(solution)/shard_map/ppermute | solution.py:342
  32.0 10.0 %collective-permute-start.10 = (bf16[640,128]{1,0:T(8,128)(2,1)}, bf16[640,128]{1,0:T(8,128)(2,1)S(1)}, u32[]{:S(2)}, u32[]{:S(2)}) collective-permute-start(bf16[640,128]{1,0:T(8,128)(2,1)} %get-tuple-element.54), channel_id=1, source_target_pairs={{0,192},{32,224},{64,0},{96,32},{128,64},{160,96},{192,128},{224,1... | collective-permute-start | bytes 491528 | tf_op jit(solution)/shard_map/ppermute | solution.py:342
  33.0 10.0 %copy-start.7 = (bf16[640,128]{1,0:T(8,128)(2,1)}, bf16[640,128]{1,0:T(8,128)(2,1)S(1)}, u32[]{:S(2)}) copy-start(bf16[640,128]{1,0:T(8,128)(2,1)S(1)} %collective-permute-done.4.rest_8_.rest_4_) | copy-start | bytes 491524
  33.0 5.0 %collective-permute-start.6 = (bf16[640,128]{1,0:T(8,128)(2,1)}, bf16[640,128]{1,0:T(8,128)(2,1)S(1)}, u32[]{:S(2)}, u32[]{:S(2)}) collective-permute-start(bf16[640,128]{1,0:T(8,128)(2,1)} %copy-done.1), channel_id=1, source_target_pairs={{0,32},{32,0},{64,96},{96,64},{128,160},{160,128},{192,224},{224,1... | collective-permute-start | bytes 491528 | tf_op jit(solution)/shard_map/ppermute | solution.py:342
  34.5 8.5 %copy-start.8 = (bf16[640,128]{1,0:T(8,128)(2,1)}, bf16[640,128]{1,0:T(8,128)(2,1)S(1)}, u32[]{:S(2)}) copy-start(bf16[640,128]{1,0:T(8,128)(2,1)S(1)} %collective-permute-done.5.rest_9_.rest_5_) | copy-start | bytes 491524
  34.5 7.5 %collective-permute-start.7 = (bf16[640,128]{1,0:T(8,128)(2,1)}, bf16[640,128]{1,0:T(8,128)(2,1)S(1)}, u32[]{:S(2)}, u32[]{:S(2)}) collective-permute-start(bf16[640,128]{1,0:T(8,128)(2,1)} %copy-done.2), channel_id=1, source_target_pairs={{0,32},{32,0},{64,96},{96,64},{128,160},{160,128},{192,224},{224,1... | collective-permute-start | bytes 491528 | tf_op jit(solution)/shard_map/ppermute | solution.py:342
  38.1 8.7 %copy-start.9 = (bf16[640,128]{1,0:T(8,128)(2,1)}, bf16[640,128]{1,0:T(8,128)(2,1)S(1)}, u32[]{:S(2)}) copy-start(bf16[640,128]{1,0:T(8,128)(2,1)S(1)} %collective-permute-done.6.rest_10_.rest_6_) | copy-start | bytes 491524
  38.1 6.9 %collective-permute-start.3 = (bf16[2560,128]{1,0:T(8,128)(2,1)}, bf16[2560,128]{1,0:T(8,128)(2,1)S(1)}, u32[]{:S(2)}, u32[]{:S(2)}) collective-permute-start(bf16[2560,128]{1,0:T(8,128)(2,1)} %pad_maximum_fusion), channel_id=1, source_target_pairs={{0,16},{16,0},{1,17},{17,1},{2,18},{18,2},{3,19},{19,3},{4,20},{20... | collective-permute-start | bytes 1966088 | tf_op jit(solution)/shard_map/ppermute | solution.py:346
  42.0 4.8 %copy-start.10 = (bf16[640,128]{1,0:T(8,128)(2,1)}, bf16[640,128]{1,0:T(8,128)(2,1)S(1)}, u32[]{:S(2)}) copy-start(bf16[640,128]{1,0:T(8,128)(2,1)S(1)} %collective-permute-done.7.rest_11_.rest_7_) | copy-start | bytes 491524
  42.0 4.8 %copy-start.11 = (bf16[640,128]{1,0:T(8,128)(2,1)}, bf16[640,128]{1,0:T(8,128)(2,1)S(1)}, u32[]{:S(2)}) copy-start(bf16[640,128]{1,0:T(8,128)(2,1)S(1)} %collective-permute-done.8.rest_1_) | copy-start | bytes 491524
  42.0 4.8 %copy-start.12 = (bf16[640,128]{1,0:T(8,128)(2,1)}, bf16[640,128]{1,0:T(8,128)(2,1)S(1)}, u32[]{:S(2)}) copy-start(bf16[640,128]{1,0:T(8,128)(2,1)S(1)} %collective-permute-done.9.rest_2_) | copy-start | bytes 491524
  42.0 4.8 %copy-start.13 = (bf16[640,128]{1,0:T(8,128)(2,1)}, bf16[640,128]{1,0:T(8,128)(2,1)S(1)}, u32[]{:S(2)}) copy-start(bf16[640,128]{1,0:T(8,128)(2,1)S(1)} %collective-permute-done.10.rest_3_) | copy-start | bytes 491524
  42.0 16.6 %copy-start.5 = (bf16[64,20,128]{2,1,0:T(8,128)(2,1)}, bf16[64,20,128]{2,1,0:T(8,128)(2,1)S(1)}, u32[]{:S(2)}) copy-start(bf16[64,20,128]{2,1,0:T(8,128)(2,1)S(1)} %all-to-all-done.rest_9_) | copy-start | bytes 983044
  43.0 3.7 %collective-permute-start.11 = (bf16[2560,128]{1,0:T(8,128)(2,1)}, bf16[2560,128]{1,0:T(8,128)(2,1)S(1)}, u32[]{:S(2)}, u32[]{:S(2)}) collective-permute-start(bf16[2560,128]{1,0:T(8,128)(2,1)} %pad_maximum_fusion.1), channel_id=1, source_target_pairs={{0,16},{16,0},{1,17},{17,1},{2,18},{18,2},{3,19},{19,3},{4,20},{20... | collective-permute-start | bytes 1966088 | tf_op jit(solution)/shard_map/ppermute | solution.py:346
  72.9 2.3 %collective-permute-start.12 = (bf16[2560,128]{1,0:T(8,128)(2,1)}, bf16[2560,128]{1,0:T(8,128)(2,1)S(1)}, u32[]{:S(2)}, u32[]{:S(2)}) collective-permute-start(bf16[2560,128]{1,0:T(8,128)(2,1)} %get-tuple-element.71), channel_id=1, source_target_pairs={{0,16},{16,0},{1,17},{17,1},{2,18},{18,2},{3,19},{19,3},{4,20},{20... | collective-permute-start | bytes 1966088 | tf_op jit(solution)/shard_map/ppermute | solution.py:346
  78.4 16.4 %collective-permute-start.13 = (bf16[2560,128]{1,0:T(8,128)(2,1)}, bf16[2560,128]{1,0:T(8,128)(2,1)S(1)}, u32[]{:S(2)}, u32[]{:S(2)}) collective-permute-start(bf16[2560,128]{1,0:T(8,128)(2,1)} %add_other.1), channel_id=1, source_target_pairs={{0,32},{32,0},{64,96},{96,64},{128,160},{160,128},{192,224},{224,1... | collective-permute-start | bytes 1966088 | tf_op jit(solution)/shard_map/ppermute | solution.py:342
  94.8 2.9 %copy-start.14 = (bf16[2560,128]{1,0:T(8,128)(2,1)}, bf16[2560,128]{1,0:T(8,128)(2,1)S(1)}, u32[]{:S(2)}) copy-start(bf16[2560,128]{1,0:T(8,128)(2,1)S(1)} %collective-permute-done.13.c) | copy-start | bytes 1966084
  94.8 2.9 %collective-permute-start.14 = (bf16[2560,128]{1,0:T(8,128)(2,1)}, bf16[2560,128]{1,0:T(8,128)(2,1)S(1)}, u32[]{:S(2)}, u32[]{:S(2)}) collective-permute-start(bf16[2560,128]{1,0:T(8,128)(2,1)} %get-tuple-element.76), channel_id=1, source_target_pairs={{0,16},{16,0},{1,17},{17,1},{2,18},{18,2},{3,19},{19,3},{4,20},{20... | collective-permute-start | bytes 1966088 | tf_op jit(solution)/shard_map/ppermute | solution.py:346
  101.1 7.4 %collective-permute-start.15 = (bf16[960,128]{1,0:T(8,128)(2,1)}, bf16[960,128]{1,0:T(8,128)(2,1)S(1)}, u32[]{:S(2)}, u32[]{:S(2)}) collective-permute-start(bf16[960,128]{1,0:T(8,128)(2,1)} %get-tuple-element.80), channel_id=1, source_target_pairs={{0,192},{32,224},{64,0},{96,32},{128,64},{160,96},{192,128},{224,1... | collective-permute-start | bytes 737288 | tf_op jit(solution)/shard_map/ppermute | solution.py:342
  101.4 8.6 %collective-permute-start.16 = (bf16[960,128]{1,0:T(8,128)(2,1)}, bf16[960,128]{1,0:T(8,128)(2,1)S(1)}, u32[]{:S(2)}, u32[]{:S(2)}) collective-permute-start(bf16[960,128]{1,0:T(8,128)(2,1)} %get-tuple-element.81), channel_id=1, source_target_pairs={{0,128},{32,160},{64,192},{96,224},{128,0},{160,32},{192,64},{224,... | collective-permute-start | bytes 737288 | tf_op jit(solution)/shard_map/ppermute | solution.py:342
  103.3 13.0 %collective-permute-start.17 = (bf16[960,128]{1,0:T(8,128)(2,1)}, bf16[960,128]{1,0:T(8,128)(2,1)S(1)}, u32[]{:S(2)}, u32[]{:S(2)}) collective-permute-start(bf16[960,128]{1,0:T(8,128)(2,1)} %get-tuple-element.82), channel_id=1, source_target_pairs={{0,64},{32,96},{64,128},{96,160},{128,192},{160,224},{192,0},{224,... | collective-permute-start | bytes 737288 | tf_op jit(solution)/shard_map/ppermute | solution.py:342
  108.5 7.8 %copy-start.17 = (bf16[960,128]{1,0:T(8,128)(2,1)}, bf16[960,128]{1,0:T(8,128)(2,1)S(1)}, u32[]{:S(2)}) copy-start(bf16[960,128]{1,0:T(8,128)(2,1)S(1)} %collective-permute-done.15.rest_1_) | copy-start | bytes 737284
  110.0 6.3 %copy-start.18 = (bf16[960,128]{1,0:T(8,128)(2,1)}, bf16[960,128]{1,0:T(8,128)(2,1)S(1)}, u32[]{:S(2)}) copy-start(bf16[960,128]{1,0:T(8,128)(2,1)S(1)} %collective-permute-done.16.rest_2_) | copy-start | bytes 737284
  (8 other events, 7.4 us)

commit v3 on v2

--- a/solution.py
+++ b/solution.py
@@ -18,9 +18,9 @@
 NQT = QROWS // QT
 HALF = 16 * BLK
 SKC = 512
-SPER = 4
-GKC = 640
-GPER = 2
+SPER = 5
+GKC = 320
+GPER = 6
 DROWS = QROWS + QT
 SCALE = 1.0 / math.sqrt(HD)
 LOG2E = math.log2(math.e)
@@ -108,14 +108,15 @@
     return a, b, (r - b.astype(F32)).astype(BF16)
 
 
-def sort_keys(ids, tables, row, dyl, pieces, first, swapped, second, dst):
+def sort_keys(ids, tables, row, dyl, first, pieces, swapped, dst):
     for s in range(NX):
         for dc in range(2):
             ctx = ctx_of(ids, s, dyl, dc)
+            near, far = (pieces, swapped)[dc]
+            src, base = (near, 0) if s == 0 else (far, 2 * (s - 1) * OWN)
             for h in range(2):
-                src, base = (pieces[s], first) if dc == 0 else (swapped, 2 * s * OWN + second)
-                base = base + h * BLK
-                dst[at(tables[row, 2 * ctx + h] * BLK, BLK), :] = src[base : base + BLK, :]
+                begin = base + first + h * BLK
+                dst[at(tables[row, 2 * ctx + h] * BLK, BLK), :] = src[begin : begin + BLK, :]
 
 
 def sort_rows(ids, tables, blocks, dst):
@@ -172,11 +173,11 @@
 
 def stats_kernel(tables, slope, *rest):
     ids = here()
-    qo, kv, kv_y, kv_c, kv_yc = rest[0:4], rest[4:8], rest[8:12], rest[12], rest[13]
-    qs, qt = rest[14:16]
-    keys, limits, work, lims, tops, totals = rest[16:22]
-    sort_keys(ids, tables, 3, 0, kv, 0, kv_c, 0, keys)
-    sort_keys(ids, tables, 3, 1, kv_y, 0, kv_yc, 0, keys)
+    qo, kv, kv_c, kv_y, kv_yc = rest[0:4], rest[4:6], rest[6:8], rest[8:10], rest[10:12]
+    qs, qt = rest[12:14]
+    keys, limits, work, lims, tops, totals = rest[14:20]
+    sort_keys(ids, tables, 3, 0, 0, kv, kv_c, keys)
+    sort_keys(ids, tables, 3, 1, 0, kv_y, kv_yc, keys)
     sort_rows(ids, tables, lambda s, h: qo[s][h * BLK : (h + 1) * BLK, :], qs)
     qs[QROWS:, :] = jnp.zeros((QT, W), BF16)
     sort_limits(ids, tables, limits)
@@ -221,7 +222,7 @@
     steps = list_work(limits, dyl, GKC, GPER, work, lims)
 
     def step(j, carry):
-        parts = []
+        items = []
         for u in range(GPER):
             item = j * GPER + u
             tile, chunk = work[0, item], work[1, item]
@@ -229,9 +230,12 @@
             cols = at(tile * QT, QT)
             kc = keys[rows, :]
             s = jnp.dot(kc, qt[tile], preferred_element_type=F32)
+            dp = jnp.dot(vals[rows, :], dot[tile], preferred_element_type=F32)
+            items.append((tile, chunk, rows, cols, kc, s, dp))
+        parts = []
+        for tile, chunk, rows, cols, kc, s, dp in items:
             index = lax.broadcasted_iota(jnp.int32, (GKC, QT), 0)
             p = jnp.where(index <= lims[tile] - chunk * GKC, jnp.exp2(s * CEXP), 0.0)
-            dp = jnp.dot(vals[rows, :], dot[tile], preferred_element_type=F32)
             ds = (p * dp).astype(BF16)
             dv = jnp.dot(p.astype(BF16), dos[cols, :], preferred_element_type=F32)
             dk = jnp.dot(ds, qs[cols, :], preferred_element_type=F32)
@@ -258,12 +262,12 @@
 
 def grads_other_kernel(tables, *rest):
     ids = here()
-    qo, kv_y, kv_yc = rest[0:4], rest[4:8], rest[8]
-    dor, qs, qt = rest[9:12]
-    dos, dot, dq, keep, send = rest[12:17]
-    keys, vals, dkey, dval, work, lims, flat, outs, limits = rest[17:26]
-    sort_keys(ids, tables, 0, 1, kv_y, 0, kv_yc, 0, keys)
-    sort_keys(ids, tables, 0, 1, kv_y, OWN, kv_yc, OWN, vals)
+    qo, kv_y, kv_yc = rest[0:4], rest[4:6], rest[6:8]
+    dor, qs, qt = rest[8:11]
+    dos, dot, dq, keep, send = rest[11:16]
+    keys, vals, dkey, dval, work, lims, flat, outs, limits = rest[16:25]
+    sort_keys(ids, tables, 0, 1, 0, kv_y, kv_yc, keys)
+    sort_keys(ids, tables, 0, 1, OWN, kv_y, kv_yc, vals)
     sort_limits(ids, tables, limits)
     for n in range(64):
         flat[n * 20 : (n + 1) * 20, :] = dor[n]
@@ -293,12 +297,12 @@
 
 def grads_own_kernel(tables, *rest):
     ids = here()
-    kv, kv_c = rest[0:4], rest[4]
-    qs, qt, dos, dot, dq_in = rest[5:10]
-    dqo, keep, send = rest[10:13]
-    keys, vals, dkey, dval, work, lims, dq, limits = rest[13:21]
-    sort_keys(ids, tables, 0, 0, kv, 0, kv_c, 0, keys)
-    sort_keys(ids, tables, 0, 0, kv, OWN, kv_c, OWN, vals)
+    kv, kv_c = rest[0:2], rest[2:4]
+    qs, qt, dos, dot, dq_in = rest[4:9]
+    dqo, keep, send = rest[9:13], rest[13], rest[14]
+    keys, vals, dkey, dval, work, lims, dq, limits = rest[15:23]
+    sort_keys(ids, tables, 0, 0, 0, kv, kv_c, keys)
+    sort_keys(ids, tables, 0, 0, OWN, kv, kv_c, vals)
     sort_limits(ids, tables, limits)
     dq[...] = dq_in[...]
     grads_loop(0, keys, vals, qs, qt, dos, dot, limits, dkey, dval, dq, work, lims)
@@ -308,27 +312,27 @@
         ctx = ctx_of(ids, s, 0, 0)
         for h in range(2):
             rows = at(tables[1, 2 * ctx + h] * BLK, BLK)
-            base = s * OWN + h * BLK
-            dqo[base : base + BLK, :] = (dq[rows, :] * SCALE).astype(BF16)
+            dqo[s][h * BLK : (h + 1) * BLK, :] = (dq[rows, :] * SCALE).astype(BF16)
 
 
 def add_kernel(a, b, out):
     out[...] = (a[...].astype(F32) + b[...].astype(F32)).astype(BF16)
 
 
-def add_own_kernel(a, b, c, dq, *outs):
+def add_own_kernel(a, b, c, *outs):
     for s in range(NX):
         rows = slice(s * 2 * OWN, (s + 1) * 2 * OWN)
-        outs[s][:OWN, :] = dq[s * OWN : (s + 1) * OWN, :]
         total = a[rows, :].astype(F32) + b[rows, :].astype(F32) + c[rows, :].astype(F32)
-        outs[s][OWN:, :] = total.astype(BF16)
+        outs[s][...] = total.astype(BF16)
 
 
 def unpack_kernel(*rest):
-    pieces, outs, buf = rest[0:4], rest[4:7], rest[7]
+    dqs, dkvs, outs, buf = rest[0:4], rest[4:8], rest[8:11], rest[11]
     x = lax.axis_index("x")
     for s in range(NX):
-        buf[lax.rem(x + s, NX)] = pieces[s][...]
+        head = lax.rem(x + s, NX)
+        buf[head, :OWN, :] = dqs[s][...]
+        buf[head, OWN:, :] = dkvs[s][...]
     for n in range(NX):
         for i in range(3):
             outs[i][:, n * HD : (n + 1) * HD] = buf[n, i * OWN : (i + 1) * OWN, :HD]
@@ -378,15 +382,15 @@
     kv, d_out = lax.optimization_barrier((kv, d_out))
     (d_pack,) = call(cotangent_pack_kernel, [((64, 20, W), BF16)], [], "cotangent_pack")(d_out)
     d_rows = lax.all_to_all(d_pack, ("x", "yh", "z"), 0, 0)
-    kv = [kv[0]] + [shift(kv[s], s) for s in (1, 2, 3)]
-    qo = call(functools.partial(pack_kernel, "qo"), [piece] * 4, buf, "pack_qo", 4)(
-        plan, queries, out_fwd, *kv[1:], tables
+    kv = [kv[0], jnp.concatenate([shift(kv[s], s) for s in (1, 2, 3)])]
+    kv_y = [shift(a, 0, True) for a in kv]
+    kv_c = [swap_core(a) for a in kv]
+    qo = call(functools.partial(pack_kernel, "qo"), [piece] * 4, buf, "pack_qo", 2)(
+        plan, queries, out_fwd, kv[1], tables
     )
-    kv_y = [shift(a, 0, True) for a in kv]
     qo = [qo[0]] + [shift(qo[s], s) for s in (1, 2, 3)]
     kv_y, qo, d_rows = lax.optimization_barrier((kv_y, qo, d_rows))
-    kv_c = swap_core(jnp.concatenate(kv))
-    kv_yc = swap_core(jnp.concatenate(kv_y))
+    kv_yc = [swap_core(a) for a in kv_y]
 
     limits = pltpu.SMEM((3, 8), jnp.int32)
     qs, qt = call(
@@ -396,7 +400,7 @@
         + worklist(SKC, 2 * HALF, SPER)
         + [pltpu.VMEM((NQT + 1, 2 * HALF // SKC, 8, QT), F32)] * 2,
         "stats",
-    )(tables, slope, *qo, *kv, *kv_y, kv_c, kv_yc)
+    )(tables, slope, *qo, *kv, *kv_c, *kv_y, *kv_yc)
     accs = [pltpu.VMEM((HALF, W), BF16)] * 2 + [pltpu.VMEM((HALF, W), F32)] * 2
     accs = accs + worklist(GKC, HALF, GPER)
     dos, dot, dq, keep, send = call(
@@ -404,29 +408,29 @@
         [((DROWS, W), BF16), ((NQT + 1, W, QT), BF16), ((DROWS, W), F32), stack, stack],
         accs + [pltpu.VMEM((QROWS, W), BF16)] * 2 + [limits],
         "grads_other",
-    )(tables, *qo, *kv_y, kv_yc, d_rows, qs, qt)
+    )(tables, *qo, *kv_y, *kv_yc, d_rows, qs, qt)
     (dkv_y,) = call(add_kernel, [stack], [], "add_other")(keep, swap_core(send))
     dq, dkv_y = lax.optimization_barrier((dq, dkv_y))
     dkv_y = shift(dkv_y, 0, True)
 
-    dq, keep, send = call(
+    *dqs, keep, send = call(
         grads_own_kernel,
-        [((QROWS, W), BF16), stack, stack],
+        [((OWN, W), BF16)] * 4 + [stack, stack],
         accs + [pltpu.VMEM((DROWS, W), F32), limits],
         "grads_own",
-    )(tables, *kv, kv_c, qs, qt, dos, dot, dq)
-    send, dkv_y = lax.optimization_barrier((send, dkv_y))
-    grads = call(add_own_kernel, [((3 * OWN, W), BF16)] * 4, [], "add_own")(
-        keep, swap_core(send), dkv_y, dq
-    )
-    grads = [grads[0]] + [shift(grads[s], -s) for s in (1, 2, 3)]
+    )(tables, *kv, *kv_c, qs, qt, dos, dot, dq)
+    dqs[1], dqs[2], dkv_y = lax.optimization_barrier((dqs[1], dqs[2], dkv_y))
+    swapped = swap_core(send)
+    dqs = [dqs[0]] + [shift(dqs[s], -s) for s in (1, 2, 3)]
+    dkvs = call(add_own_kernel, [piece] * 4, [], "add_own")(keep, swapped, dkv_y)
+    dkvs = [dkvs[0]] + [shift(dkvs[s], -s) for s in (1, 2, 3)]
     return tuple(
         call(
             unpack_kernel,
             [((OWN, NX * HD), BF16)] * 3,
             [pltpu.VMEM((NX, 3 * OWN, W), BF16)],
             "unpack",
-        )(*grads)
+        )(*dqs, *dkvs)
     )
 
 

time: 119 us -> 112 us (0.941)
  starting transfers between devices: 33.7 us -> 41.2 us
  waiting for transfers between devices: 24.5 us -> 18.1 us
  Pallas kernels: 52.4 us -> 47.6 us
  other arithmetic: 3.79 us -> 0.82 us
    ppermute x14 -> x15, starting transfers between devices: 15.4 us -> 23.4 us  [shift(): return lax.ppermute(value, ('x', 'yl'), pairs)]
    pallas_call x9, Pallas kernels: 52.4 us -> 47.6 us  [run(): pl.pallas_call(kernel, out_shape=[jax.ShapeDtypeStruct(s, d) for s, d in...]
    ppermute x14 -> x15, waiting for transfers between devices: 18.4 us -> 14.4 us  [shift(): return lax.ppermute(value, ('x', 'yl'), pairs)]
    concatenate x2 -> x0, other arithmetic: 2.96 us -> none  [the longest x1 1.97 us: on_device(): kv_c = swap_core(jnp.concatenate(kv))]
    ppermute x4 -> x6, waiting for transfers between devices: 6.11 us -> 3.7 us  [swap_core(): return lax.ppermute(value, 'c', [(0, 1), (1, 0)])]
    ppermute x4 -> x6, starting transfers between devices: 6.68 us -> 6.18 us  [swap_core(): return lax.ppermute(value, 'c', [(0, 1), (1, 0)])]
    unnamed x42 -> x50, local copies, waits for them, and re-layouts: 4.57 us -> 4.15 us
  transfers between devices with their start and end apart: 19 -> 22, of which waited for: 8 -> 8; matrix products, arithmetic and copies ran while one was open for 3% -> 1% of each run, Pallas kernels for 14% -> 17%
where the time goes in v3:
time: 112 us; the launch traced here: 113 us
  Pallas kernels  47.6 us (42%)
  starting transfers between devices  41.2 us (37%)
  waiting for transfers between devices  18.1 us (16%)
  local copies, waits for them, and re-layouts  4.17 us (4%)
    pallas_call x9, Pallas kernels, run(): pl.pallas_call(kernel, out_shape=[jax.ShapeDtypeStruct(s, d) for s, d in...  47.6 us
    ppermute x15, starting transfers between devices, shift(): return lax.ppermute(value, ('x', 'yl'), pairs)  23.4 us
    ppermute x15, waiting for transfers between devices, shift(): return lax.ppermute(value, ('x', 'yl'), pairs)  14.4 us
    all_to_all x1, starting transfers between devices, on_device(): d_rows = lax.all_to_all(d_pack, ('x', 'yh', 'z'), 0, 0)  11.6 us
    ppermute x6, starting transfers between devices, swap_core(): return lax.ppermute(value, 'c', [(0, 1), (1, 0)])  6.18 us
    unnamed x50, local copies, waits for them, and re-layouts  4.15 us
    ppermute x6, waiting for transfers between devices, swap_core(): return lax.ppermute(value, 'c', [(0, 1), (1, 0)])  3.7 us
  transfers between devices with their start and end apart: 22, of which 8 were waited for; matrix products, arithmetic and copies ran while one was open for 1% of the time, Pallas kernels for 17%

profile of v3, /device:TPU:1, one launch (start us, length us, event | category | flops | bytes accessed | tf_op | source)
XLA Modules:
  0.0 112.7 jit_solution(7387469139812377921)
XLA Ops:
  0.6 2.6 %pack_kv.1 = (bf16[640,128]{1,0:T(8,128)(2,1)}, bf16[640,128]{1,0:T(8,128)(2,1)}, bf16[640,128]{1,0:T(8,128)(2,1)}, bf16[640,128]{1,0:T(8,128)(2,1)}) custom-call(s32[32]{0:T(128)} %plan.3, bf16[320,448]{1,0:T(8,128)(2,1)} %a_ref.2, bf16[320,448]{1,0:T(8,128)(2,1)} %b_ref.2), custom_call_target="tpu_custom_call" | custom-call | tf_op jit(solution)/shard_map/pack_kv/pallas_call | solution.py:42
  3.2 2.0 %collective-permute-start = (bf16[640,128]{1,0:T(8,128)(2,1)}, bf16[640,128]{1,0:T(8,128)(2,1)S(1)}, u32[]{:S(2)}, u32[]{:S(2)}) collective-permute-start(bf16[640,128]{1,0:T(8,128)(2,1)} %get-tuple-element.50), channel_id=1, source_target_pairs={{0,64},{32,96},{64,128},{96,160},{128,192},{160,224},{192,0},{224,... | collective-permute-start | bytes 491528 | tf_op jit(solution)/shard_map/ppermute | solution.py:346
  5.2 2.5 %collective-permute-start.1 = (bf16[640,128]{1,0:T(8,128)(2,1)}, bf16[640,128]{1,0:T(8,128)(2,1)S(1)}, u32[]{:S(2)}, u32[]{:S(2)}) collective-permute-start(bf16[640,128]{1,0:T(8,128)(2,1)} %get-tuple-element.51), channel_id=1, source_target_pairs={{0,128},{32,160},{64,192},{96,224},{128,0},{160,32},{192,64},{224,... | collective-permute-start | bytes 491528 | tf_op jit(solution)/shard_map/ppermute | solution.py:346
  7.7 1.2 %collective-permute-start.2 = (bf16[640,128]{1,0:T(8,128)(2,1)}, bf16[640,128]{1,0:T(8,128)(2,1)S(1)}, u32[]{:S(2)}, u32[]{:S(2)}) collective-permute-start(bf16[640,128]{1,0:T(8,128)(2,1)} %get-tuple-element.52), channel_id=1, source_target_pairs={{0,192},{32,224},{64,0},{96,32},{128,64},{160,96},{192,128},{224,1... | collective-permute-start | bytes 491528 | tf_op jit(solution)/shard_map/ppermute | solution.py:346
  8.8 1.3 %collective-permute-start.5 = (bf16[640,128]{1,0:T(8,128)(2,1)}, bf16[640,128]{1,0:T(8,128)(2,1)S(1)}, u32[]{:S(2)}, u32[]{:S(2)}) collective-permute-start(bf16[640,128]{1,0:T(8,128)(2,1)} %get-tuple-element.49.rest_4_.rest_0_), channel_id=1, source_target_pairs={{0,32},{32,0},{64,96},{96,64},{128,160},{160,128},{192,224},{224,1... | collective-permute-start | bytes 491528 | tf_op jit(solution)/shard_map/ppermute | solution.py:346
  10.1 2.0 %cotangent_pack.1 = bf16[64,20,128]{2,1,0:T(8,128)(2,1)} custom-call(bf16[20,7168]{1,0:T(8,128)(2,1)} %d_ref), custom_call_target="tpu_custom_call" | custom-call | tf_op jit(solution)/shard_map/cotangent_pack/pallas_call | solution.py:42
  12.1 11.6 %all-to-all-start = ((bf16[64,20,128]{2,1,0:T(8,128)(2,1)}), bf16[64,20,128]{2,1,0:T(8,128)(2,1)S(1)}, u32[]{:S(2)}, u32[]{:S(2)}) async-start(bf16[64,20,128]{2,1,0:T(8,128)(2,1)} %cotangent_pack.1), calls=%async_computation | async-start | bytes 786432 | tf_op jit(solution)/shard_map/all_to_all | solution.py:384
  25.4 2.4 %pack_qo.1 = (bf16[640,128]{1,0:T(8,128)(2,1)}, bf16[640,128]{1,0:T(8,128)(2,1)}, bf16[640,128]{1,0:T(8,128)(2,1)}, bf16[640,128]{1,0:T(8,128)(2,1)}) custom-call(s32[32]{0:T(128)} %plan.3, bf16[320,448]{1,0:T(8,128)(2,1)} %a_ref.3, bf16[320,448]{1,0:T(8,128)(2,1)} %b_ref.3, bf16[1920,128]{1,0:T(8,128)(2,1)} %copy-done, s32[4,32]{1,0:T(4,128)} %pad_add_fusion.rest_1_.tables), custom_call_target="tpu_custom_call" | custom-call | tf_op jit(solution)/shard_map/pack_qo/pallas_call | solution.py:42
  27.8 1.0 collective-permute-start.7
  28.9 2.6 %collective-permute-start.8 = (bf16[640,128]{1,0:T(8,128)(2,1)}, bf16[640,128]{1,0:T(8,128)(2,1)S(1)}, u32[]{:S(2)}, u32[]{:S(2)}) collective-permute-start(bf16[640,128]{1,0:T(8,128)(2,1)} %get-tuple-element.55), channel_id=1, source_target_pairs={{0,128},{32,160},{64,192},{96,224},{128,0},{160,32},{192,64},{224,... | collective-permute-start | bytes 491528 | tf_op jit(solution)/shard_map/ppermute | solution.py:346
  31.5 1.1 collective-permute-start.9
  32.5 3.3 %collective-permute-start.4 = (bf16[1920,128]{1,0:T(8,128)(2,1)}, bf16[1920,128]{1,0:T(8,128)(2,1)S(1)}, u32[]{:S(2)}, u32[]{:S(2)}) collective-permute-start(bf16[1920,128]{1,0:T(8,128)(2,1)} %copy-done), channel_id=1, source_target_pairs={{0,16},{16,0},{1,17},{17,1},{2,18},{18,2},{3,19},{19,3},{4,20},{20... | collective-permute-start | bytes 1474568 | tf_op jit(solution)/shard_map/ppermute | solution.py:350
  35.8 4.8 %collective-permute-done.8.rest_2_ = bf16[640,128]{1,0:T(8,128)(2,1)S(1)} collective-permute-done((bf16[640,128]{1,0:T(8,128)(2,1)}, bf16[640,128]{1,0:T(8,128)(2,1)S(1)}, u32[]{:S(2)}, u32[]{:S(2)}) %collective-permute-start.8) | collective-permute-done | bytes 163872 | tf_op jit(solution)/shard_map/ppermute | solution.py:346
  40.7 2.0 %collective-permute-start.11 = (bf16[1920,128]{1,0:T(8,128)(2,1)S(1)}, bf16[1920,128]{1,0:T(8,128)(2,1)S(1)}, u32[]{:S(2)}, u32[]{:S(2)}) collective-permute-start(bf16[1920,128]{1,0:T(8,128)(2,1)S(1)} %collective-permute-done.6.rest_9_.rest_5_), channel_id=1, source_target_pairs={{0,16},{16,0},{1,17},{17,1},{2,18},{18,2},{3,19},{19,3},{4,20},{20... | collective-permute-start | bytes 1474568 | tf_op jit(solution)/shard_map/ppermute | solution.py:350
  43.2 1.2 %collective-permute-done.3.rest_6_.rest_2_ = bf16[640,128]{1,0:T(8,128)(2,1)S(1)} collective-permute-done((bf16[640,128]{1,0:T(8,128)(2,1)S(1)}, bf16[640,128]{1,0:T(8,128)(2,1)S(1)}, u32[]{:S(2)}, u32[]{:S(2)}) %collective-permute-start.3) | collective-permute-done | bytes 163872 | tf_op jit(solution)/shard_map/ppermute | solution.py:350
  45.4 10.1 %stats.1 = (bf16[1536,128]{1,0:T(8,128)(2,1)}, bf16[6,128,256]{2,1,0:T(8,128)(2,1)}) custom-call(s32[4,32]{1,0:T(4,128)} %pad_add_fusion.rest_1_.tables, f32[1]{0:T(128)} %bitcast.4.slope, bf16[640,128]{1,0:T(8,128)(2,1)} %get-tuple-element.58.rest_0_, bf16[640,128]{1,0:T(8,128)(2,1)} %copy-done.8, bf16[640,128]{1,0:T(8,128)(2,1)} %copy-done.9, ...), custom_call_target="tpu_custom_call" | custom-call | tf_op jit(solution)/shard_map/stats/pallas_call | solution.py:42
  55.5 11.0 %grads_other.1 = (bf16[1536,128]{1,0:T(8,128)(2,1)}, bf16[6,128,256]{2,1,0:T(8,128)(2,1)}, f32[1536,128]{1,0:T(8,128)}, bf16[2560,128]{1,0:T(8,128)(2,1)}, bf16[2560,128]{1,0:T(8,128)(2,1)}) custom-call(s32[4,32]{1,0:T(4,128)} %pad_add_fusion.rest_1_.tables, bf16[640,128]{1,0:T(8,128)(2,1)} %get-tuple-element.58.rest_0_, bf16[640,128]{1,0:T(8,128)(2,1)} %copy-done.8, ...), custom_call_target="tpu_custom_call" | custom-call | tf_op jit(solution)/shard_map/grads_other/pallas_call | solution.py:42
  66.6 2.3 %collective-permute-done.12.b = bf16[2560,128]{1,0:T(8,128)(2,1)S(1)} collective-permute-done((bf16[2560,128]{1,0:T(8,128)(2,1)}, bf16[2560,128]{1,0:T(8,128)(2,1)S(1)}, u32[]{:S(2)}, u32[]{:S(2)}) %collective-permute-start.12) | collective-permute-done | bytes 655392 | tf_op jit(solution)/shard_map/ppermute | solution.py:350
  68.9 0.8 copy-done.14
  69.7 2.3 %add_other.1 = bf16[2560,128]{1,0:T(8,128)(2,1)} custom-call(bf16[2560,128]{1,0:T(8,128)(2,1)} %get-tuple-element.70.a, bf16[2560,128]{1,0:T(8,128)(2,1)} %copy-done.14), custom_call_target="tpu_custom_call" | custom-call | tf_op jit(solution)/shard_map/add_other/pallas_call | solution.py:42
  72.0 4.8 %collective-permute-start.13 = (bf16[2560,128]{1,0:T(8,128)(2,1)}, bf16[2560,128]{1,0:T(8,128)(2,1)S(1)}, u32[]{:S(2)}, u32[]{:S(2)}) collective-permute-start(bf16[2560,128]{1,0:T(8,128)(2,1)} %add_other.1), channel_id=1, source_target_pairs={{0,32},{32,0},{64,96},{96,64},{128,160},{160,128},{192,224},{224,1... | collective-permute-start | bytes 1966088 | tf_op jit(solution)/shard_map/ppermute | solution.py:346
  76.8 12.0 %grads_own.1 = (bf16[320,128]{1,0:T(8,128)(2,1)}, bf16[320,128]{1,0:T(8,128)(2,1)}, bf16[320,128]{1,0:T(8,128)(2,1)}, bf16[320,128]{1,0:T(8,128)(2,1)}, bf16[256...) custom-call(s32[4,32]{1,0:T(4,128)} %pad_add_fusion.rest_1_.tables, bf16[640,128]{1,0:T(8,128)(2,1)} %get-tuple-element.49.rest_4_.rest_0_, ...), custom_call_target="tpu_custom_call" | custom-call | tf_op jit(solution)/shard_map/grads_own/pallas_call | solution.py:42
  90.0 2.0 %collective-permute-done.13.c = bf16[2560,128]{1,0:T(8,128)(2,1)S(1)} collective-permute-done((bf16[2560,128]{1,0:T(8,128)(2,1)}, bf16[2560,128]{1,0:T(8,128)(2,1)S(1)}, u32[]{:S(2)}, u32[]{:S(2)}) %collective-permute-start.13) | collective-permute-done | bytes 655392 | tf_op jit(solution)/shard_map/ppermute | solution.py:346
  92.0 0.8 copy-done.12
  93.1 2.4 %add_own.1 = (bf16[640,128]{1,0:T(8,128)(2,1)}, bf16[640,128]{1,0:T(8,128)(2,1)}, bf16[640,128]{1,0:T(8,128)(2,1)}, bf16[640,128]{1,0:T(8,128)(2,1)}) custom-call(bf16[2560,128]{1,0:T(8,128)(2,1)} %get-tuple-element.80.a, bf16[2560,128]{1,0:T(8,128)(2,1)} %copy-done.13, bf16[2560,128]{1,0:T(8,128)(2,1)} %copy-done.12), custom_call_target="tpu_custom_call" | custom-call | tf_op jit(solution)/shard_map/add_own/pallas_call | solution.py:42
  95.5 1.6 %collective-permute-start.18 = (bf16[640,128]{1,0:T(8,128)(2,1)}, bf16[640,128]{1,0:T(8,128)(2,1)S(1)}, u32[]{:S(2)}, u32[]{:S(2)}) collective-permute-start(bf16[640,128]{1,0:T(8,128)(2,1)} %get-tuple-element.84), channel_id=1, source_target_pairs={{0,192},{32,224},{64,0},{96,32},{128,64},{160,96},{192,128},{224,1... | collective-permute-start | bytes 491528 | tf_op jit(solution)/shard_map/ppermute | solution.py:346
  97.1 1.0 collective-permute-start.19
  98.2 2.5 %collective-permute-start.14 = (bf16[320,128]{1,0:T(8,128)(2,1)S(1)}, bf16[320,128]{1,0:T(8,128)(2,1)S(1)}, u32[]{:S(2)}, u32[]{:S(2)}) collective-permute-start(bf16[320,128]{1,0:T(8,128)(2,1)S(1)} %copy-done.23), channel_id=1, source_target_pairs={{0,192},{32,224},{64,0},{96,32},{128,64},{160,96},{192,128},{224,1... | collective-permute-start | bytes 245768 | tf_op jit(solution)/shard_map/ppermute | solution.py:346
  100.8 0.9 collective-permute-start.15
  101.6 4.6 %collective-permute-done.14.rest_1_ = bf16[320,128]{1,0:T(8,128)(2,1)S(1)} collective-permute-done((bf16[320,128]{1,0:T(8,128)(2,1)S(1)}, bf16[320,128]{1,0:T(8,128)(2,1)S(1)}, u32[]{:S(2)}, u32[]{:S(2)}) %collective-permute-start.14) | collective-permute-done | bytes 81952 | tf_op jit(solution)/shard_map/ppermute | solution.py:346
  106.3 2.2 %collective-permute-done.15.rest_2_ = bf16[320,128]{1,0:T(8,128)(2,1)S(1)} collective-permute-done((bf16[320,128]{1,0:T(8,128)(2,1)S(1)}, bf16[320,128]{1,0:T(8,128)(2,1)S(1)}, u32[]{:S(2)}, u32[]{:S(2)}) %collective-permute-start.15) | collective-permute-done | bytes 81952 | tf_op jit(solution)/shard_map/ppermute | solution.py:346
  109.9 2.8 %unpack.1 = (bf16[320,448]{1,0:T(8,128)(2,1)}, bf16[320,448]{1,0:T(8,128)(2,1)}, bf16[320,448]{1,0:T(8,128)(2,1)}) custom-call(bf16[320,128]{1,0:T(8,128)(2,1)} %get-tuple-element.73.rest_0_, bf16[320,128]{1,0:T(8,128)(2,1)} %copy-done.19, bf16[320,128]{1,0:T(8,128)(2,1)} %copy-done.20, bf16[320,128]{1,0:T(8,128)(2,1)} %copy-done.18, ...), custom_call_target="tpu_custom_call" | custom-call | tf_op jit(solution)/shard_map/unpack/pallas_call | solution.py:42
  (75 shorter events, 6.3 us)
Async XLA Ops:
  3.2 20.5 %collective-permute-start = (bf16[640,128]{1,0:T(8,128)(2,1)}, bf16[640,128]{1,0:T(8,128)(2,1)S(1)}, u32[]{:S(2)}, u32[]{:S(2)}) collective-permute-start(bf16[640,128]{1,0:T(8,128)(2,1)} %get-tuple-element.50), channel_id=1, source_target_pairs={{0,64},{32,96},{64,128},{96,160},{128,192},{160,224},{192,0},{224,... | collective-permute-start | bytes 491528 | tf_op jit(solution)/shard_map/ppermute | solution.py:346
  5.2 18.5 %collective-permute-start.1 = (bf16[640,128]{1,0:T(8,128)(2,1)}, bf16[640,128]{1,0:T(8,128)(2,1)S(1)}, u32[]{:S(2)}, u32[]{:S(2)}) collective-permute-start(bf16[640,128]{1,0:T(8,128)(2,1)} %get-tuple-element.51), channel_id=1, source_target_pairs={{0,128},{32,160},{64,192},{96,224},{128,0},{160,32},{192,64},{224,... | collective-permute-start | bytes 491528 | tf_op jit(solution)/shard_map/ppermute | solution.py:346
  7.7 16.1 %collective-permute-start.2 = (bf16[640,128]{1,0:T(8,128)(2,1)}, bf16[640,128]{1,0:T(8,128)(2,1)S(1)}, u32[]{:S(2)}, u32[]{:S(2)}) collective-permute-start(bf16[640,128]{1,0:T(8,128)(2,1)} %get-tuple-element.52), channel_id=1, source_target_pairs={{0,192},{32,224},{64,0},{96,32},{128,64},{160,96},{192,128},{224,1... | collective-permute-start | bytes 491528 | tf_op jit(solution)/shard_map/ppermute | solution.py:346
  8.8 23.7 %collective-permute-start.5 = (bf16[640,128]{1,0:T(8,128)(2,1)}, bf16[640,128]{1,0:T(8,128)(2,1)S(1)}, u32[]{:S(2)}, u32[]{:S(2)}) collective-permute-start(bf16[640,128]{1,0:T(8,128)(2,1)} %get-tuple-element.49.rest_4_.rest_0_), channel_id=1, source_target_pairs={{0,32},{32,0},{64,96},{96,64},{128,160},{160,128},{192,224},{224,1... | collective-permute-start | bytes 491528 | tf_op jit(solution)/shard_map/ppermute | solution.py:346
  12.1 28.5 %all-to-all-start = ((bf16[64,20,128]{2,1,0:T(8,128)(2,1)}), bf16[64,20,128]{2,1,0:T(8,128)(2,1)S(1)}, u32[]{:S(2)}, u32[]{:S(2)}) async-start(bf16[64,20,128]{2,1,0:T(8,128)(2,1)} %cotangent_pack.1), calls=%async_computation | async-start | bytes 786432 | tf_op jit(solution)/shard_map/all_to_all | solution.py:384
  23.8 16.9 %collective-permute-start.6 = (bf16[1920,128]{1,0:T(8,128)(2,1)S(1)}, bf16[1920,128]{1,0:T(8,128)(2,1)S(1)}, u32[]{:S(2)}, u32[]{:S(2)}) collective-permute-start(bf16[1920,128]{1,0:T(8,128)(2,1)S(1)} %constant_dynamic-update-slice_fusion.rest_0_.rest_5_.rest_1_), channel_id=1, source_target_pairs={{0,32},{32,0},{64,96},{96,64},{128,160},{160,128},{192,224},{224,1... | collective-permute-start | bytes 1474568 | tf_op jit(solution)/shard_map/ppermute | solution.py:346
  25.4 17.2 %copy-start.5 = (bf16[640,128]{1,0:T(8,128)(2,1)S(1)}, bf16[640,128]{1,0:T(8,128)(2,1)}, u32[]{:S(2)}) copy-start(bf16[640,128]{1,0:T(8,128)(2,1)} %get-tuple-element.49.rest_4_.rest_0_) | copy-start | bytes 491524
  27.8 8.0 %collective-permute-start.7 = (bf16[640,128]{1,0:T(8,128)(2,1)}, bf16[640,128]{1,0:T(8,128)(2,1)S(1)}, u32[]{:S(2)}, u32[]{:S(2)}) collective-permute-start(bf16[640,128]{1,0:T(8,128)(2,1)} %get-tuple-element.54), channel_id=1, source_target_pairs={{0,64},{32,96},{64,128},{96,160},{128,192},{160,224},{192,0},{224,... | collective-permute-start | bytes 491528 | tf_op jit(solution)/shard_map/ppermute | solution.py:346
  28.9 11.8 %collective-permute-start.8 = (bf16[640,128]{1,0:T(8,128)(2,1)}, bf16[640,128]{1,0:T(8,128)(2,1)S(1)}, u32[]{:S(2)}, u32[]{:S(2)}) collective-permute-start(bf16[640,128]{1,0:T(8,128)(2,1)} %get-tuple-element.55), channel_id=1, source_target_pairs={{0,128},{32,160},{64,192},{96,224},{128,0},{160,32},{192,64},{224,... | collective-permute-start | bytes 491528 | tf_op jit(solution)/shard_map/ppermute | solution.py:346
  31.5 9.2 %collective-permute-start.9 = (bf16[640,128]{1,0:T(8,128)(2,1)}, bf16[640,128]{1,0:T(8,128)(2,1)S(1)}, u32[]{:S(2)}, u32[]{:S(2)}) collective-permute-start(bf16[640,128]{1,0:T(8,128)(2,1)} %get-tuple-element.56), channel_id=1, source_target_pairs={{0,192},{32,224},{64,0},{96,32},{128,64},{160,96},{192,128},{224,1... | collective-permute-start | bytes 491528 | tf_op jit(solution)/shard_map/ppermute | solution.py:346
  32.5 12.1 %copy-start.7 = (bf16[640,128]{1,0:T(8,128)(2,1)}, bf16[640,128]{1,0:T(8,128)(2,1)S(1)}, u32[]{:S(2)}) copy-start(bf16[640,128]{1,0:T(8,128)(2,1)S(1)} %collective-permute-done.5.rest_8_.rest_4_) | copy-start | bytes 491524
  32.5 11.8 %collective-permute-start.4 = (bf16[1920,128]{1,0:T(8,128)(2,1)}, bf16[1920,128]{1,0:T(8,128)(2,1)S(1)}, u32[]{:S(2)}, u32[]{:S(2)}) collective-permute-start(bf16[1920,128]{1,0:T(8,128)(2,1)} %copy-done), channel_id=1, source_target_pairs={{0,16},{16,0},{1,17},{17,1},{2,18},{18,2},{3,19},{19,3},{4,20},{20... | collective-permute-start | bytes 1474568 | tf_op jit(solution)/shard_map/ppermute | solution.py:350
  35.8 8.8 %copy-start.8 = (bf16[640,128]{1,0:T(8,128)(2,1)}, bf16[640,128]{1,0:T(8,128)(2,1)S(1)}, u32[]{:S(2)}) copy-start(bf16[640,128]{1,0:T(8,128)(2,1)S(1)} %collective-permute-done.7.rest_1_) | copy-start | bytes 491524
  40.6 4.0 %copy-start.9 = (bf16[640,128]{1,0:T(8,128)(2,1)}, bf16[640,128]{1,0:T(8,128)(2,1)S(1)}, u32[]{:S(2)}) copy-start(bf16[640,128]{1,0:T(8,128)(2,1)S(1)} %collective-permute-done.8.rest_2_) | copy-start | bytes 491524
  40.6 4.0 %copy-start.10 = (bf16[640,128]{1,0:T(8,128)(2,1)}, bf16[640,128]{1,0:T(8,128)(2,1)S(1)}, u32[]{:S(2)}) copy-start(bf16[640,128]{1,0:T(8,128)(2,1)S(1)} %collective-permute-done.9.rest_3_) | copy-start | bytes 491524
  40.6 14.9 %copy-start.4 = (bf16[64,20,128]{2,1,0:T(8,128)(2,1)}, bf16[64,20,128]{2,1,0:T(8,128)(2,1)S(1)}, u32[]{:S(2)}) copy-start(bf16[64,20,128]{2,1,0:T(8,128)(2,1)S(1)} %all-to-all-done.rest_8_) | copy-start | bytes 983044
  40.7 4.0 %copy-start.2 = (bf16[1920,128]{1,0:T(8,128)(2,1)}, bf16[1920,128]{1,0:T(8,128)(2,1)S(1)}, u32[]{:S(2)}) copy-start(bf16[1920,128]{1,0:T(8,128)(2,1)S(1)} %collective-permute-done.6.rest_9_.rest_5_) | copy-start | bytes 1474564
  40.7 3.9 %collective-permute-start.11 = (bf16[1920,128]{1,0:T(8,128)(2,1)S(1)}, bf16[1920,128]{1,0:T(8,128)(2,1)S(1)}, u32[]{:S(2)}, u32[]{:S(2)}) collective-permute-start(bf16[1920,128]{1,0:T(8,128)(2,1)S(1)} %collective-permute-done.6.rest_9_.rest_5_), channel_id=1, source_target_pairs={{0,16},{16,0},{1,17},{17,1},{2,18},{18,2},{3,19},{19,3},{4,20},{20... | collective-permute-start | bytes 1474568 | tf_op jit(solution)/shard_map/ppermute | solution.py:350
  42.6 1.7 %collective-permute-start.3 = (bf16[640,128]{1,0:T(8,128)(2,1)S(1)}, bf16[640,128]{1,0:T(8,128)(2,1)S(1)}, u32[]{:S(2)}, u32[]{:S(2)}) collective-permute-start(bf16[640,128]{1,0:T(8,128)(2,1)S(1)} %copy-done.5), channel_id=1, source_target_pairs={{0,16},{16,0},{1,17},{17,1},{2,18},{18,2},{3,19},{19,3},{4,20},{20... | collective-permute-start | bytes 491528 | tf_op jit(solution)/shard_map/ppermute | solution.py:350
  42.7 1.8 %collective-permute-start.10 = (bf16[640,128]{1,0:T(8,128)(2,1)S(1)}, bf16[640,128]{1,0:T(8,128)(2,1)S(1)}, u32[]{:S(2)}, u32[]{:S(2)}) collective-permute-start(bf16[640,128]{1,0:T(8,128)(2,1)S(1)} %collective-permute-done.5.rest_8_.rest_4_), channel_id=1, source_target_pairs={{0,16},{16,0},{1,17},{17,1},{2,18},{18,2},{3,19},{19,3},{4,20},{20... | collective-permute-start | bytes 491528 | tf_op jit(solution)/shard_map/ppermute | solution.py:350
  66.6 2.3 %collective-permute-start.12 = (bf16[2560,128]{1,0:T(8,128)(2,1)}, bf16[2560,128]{1,0:T(8,128)(2,1)S(1)}, u32[]{:S(2)}, u32[]{:S(2)}) collective-permute-start(bf16[2560,128]{1,0:T(8,128)(2,1)} %get-tuple-element.71), channel_id=1, source_target_pairs={{0,16},{16,0},{1,17},{17,1},{2,18},{18,2},{3,19},{19,3},{4,20},{20... | collective-permute-start | bytes 1966088 | tf_op jit(solution)/shard_map/ppermute | solution.py:350
  72.0 19.9 %collective-permute-start.13 = (bf16[2560,128]{1,0:T(8,128)(2,1)}, bf16[2560,128]{1,0:T(8,128)(2,1)S(1)}, u32[]{:S(2)}, u32[]{:S(2)}) collective-permute-start(bf16[2560,128]{1,0:T(8,128)(2,1)} %add_other.1), channel_id=1, source_target_pairs={{0,32},{32,0},{64,96},{96,64},{128,160},{160,128},{192,224},{224,1... | collective-permute-start | bytes 1966088 | tf_op jit(solution)/shard_map/ppermute | solution.py:346
  88.7 3.2 %collective-permute-start.17 = (bf16[2560,128]{1,0:T(8,128)(2,1)}, bf16[2560,128]{1,0:T(8,128)(2,1)S(1)}, u32[]{:S(2)}, u32[]{:S(2)}) collective-permute-start(bf16[2560,128]{1,0:T(8,128)(2,1)} %get-tuple-element.81), channel_id=1, source_target_pairs={{0,16},{16,0},{1,17},{17,1},{2,18},{18,2},{3,19},{19,3},{4,20},{20... | collective-permute-start | bytes 1966088 | tf_op jit(solution)/shard_map/ppermute | solution.py:350
  89.2 11.6 %collective-permute-start.16 = (bf16[320,128]{1,0:T(8,128)(2,1)}, bf16[320,128]{1,0:T(8,128)(2,1)S(1)}, u32[]{:S(2)}, u32[]{:S(2)}) collective-permute-start(bf16[320,128]{1,0:T(8,128)(2,1)} %get-tuple-element.79), channel_id=1, source_target_pairs={{0,64},{32,96},{64,128},{96,160},{128,192},{160,224},{192,0},{224,... | collective-permute-start | bytes 245768 | tf_op jit(solution)/shard_map/ppermute | solution.py:346
  93.0 5.2 %copy-start.23 = (bf16[320,128]{1,0:T(8,128)(2,1)S(1)}, bf16[320,128]{1,0:T(8,128)(2,1)}, u32[]{:S(2)}) copy-start(bf16[320,128]{1,0:T(8,128)(2,1)} %get-tuple-element.77) | copy-start | bytes 245764
  93.1 7.7 %copy-start.22 = (bf16[320,128]{1,0:T(8,128)(2,1)S(1)}, bf16[320,128]{1,0:T(8,128)(2,1)}, u32[]{:S(2)}) copy-start(bf16[320,128]{1,0:T(8,128)(2,1)} %get-tuple-element.78) | copy-start | bytes 245764
  95.5 13.0 %collective-permute-start.18 = (bf16[640,128]{1,0:T(8,128)(2,1)}, bf16[640,128]{1,0:T(8,128)(2,1)S(1)}, u32[]{:S(2)}, u32[]{:S(2)}) collective-permute-start(bf16[640,128]{1,0:T(8,128)(2,1)} %get-tuple-element.84), channel_id=1, source_target_pairs={{0,192},{32,224},{64,0},{96,32},{128,64},{160,96},{192,128},{224,1... | collective-permute-start | bytes 491528 | tf_op jit(solution)/shard_map/ppermute | solution.py:346
  97.1 11.4 %collective-permute-start.19 = (bf16[640,128]{1,0:T(8,128)(2,1)}, bf16[640,128]{1,0:T(8,128)(2,1)S(1)}, u32[]{:S(2)}, u32[]{:S(2)}) collective-permute-start(bf16[640,128]{1,0:T(8,128)(2,1)} %get-tuple-element.85), channel_id=1, source_target_pairs={{0,128},{32,160},{64,192},{96,224},{128,0},{160,32},{192,64},{224,... | collective-permute-start | bytes 491528 | tf_op jit(solution)/shard_map/ppermute | solution.py:346
  98.1 11.1 %collective-permute-start.20 = (bf16[640,128]{1,0:T(8,128)(2,1)}, bf16[640,128]{1,0:T(8,128)(2,1)S(1)}, u32[]{:S(2)}, u32[]{:S(2)}) collective-permute-start(bf16[640,128]{1,0:T(8,128)(2,1)} %get-tuple-element.86), channel_id=1, source_target_pairs={{0,64},{32,96},{64,128},{96,160},{128,192},{160,224},{192,0},{224,... | collective-permute-start | bytes 491528 | tf_op jit(solution)/shard_map/ppermute | solution.py:346
  98.2 8.0 %collective-permute-start.14 = (bf16[320,128]{1,0:T(8,128)(2,1)S(1)}, bf16[320,128]{1,0:T(8,128)(2,1)S(1)}, u32[]{:S(2)}, u32[]{:S(2)}) collective-permute-start(bf16[320,128]{1,0:T(8,128)(2,1)S(1)} %copy-done.23), channel_id=1, source_target_pairs={{0,192},{32,224},{64,0},{96,32},{128,64},{160,96},{192,128},{224,1... | collective-permute-start | bytes 245768 | tf_op jit(solution)/shard_map/ppermute | solution.py:346
  100.8 8.5 %copy-start.18 = (bf16[320,128]{1,0:T(8,128)(2,1)}, bf16[320,128]{1,0:T(8,128)(2,1)S(1)}, u32[]{:S(2)}) copy-start(bf16[320,128]{1,0:T(8,128)(2,1)S(1)} %collective-permute-done.16.rest_3_) | copy-start | bytes 245764
  100.8 7.7 %collective-permute-start.15 = (bf16[320,128]{1,0:T(8,128)(2,1)S(1)}, bf16[320,128]{1,0:T(8,128)(2,1)S(1)}, u32[]{:S(2)}, u32[]{:S(2)}) collective-permute-start(bf16[320,128]{1,0:T(8,128)(2,1)S(1)} %copy-done.22), channel_id=1, source_target_pairs={{0,128},{32,160},{64,192},{96,224},{128,0},{160,32},{192,64},{224,... | collective-permute-start | bytes 245768 | tf_op jit(solution)/shard_map/ppermute | solution.py:346
  (14 other events, 13.9 us)

commit v4 on v3

--- a/solution.py
+++ b/solution.py
@@ -26,7 +26,7 @@
 LOG2E = math.log2(math.e)
 CEXP = SCALE * LOG2E
 NEG = -1e30
-LIMIT = 56 * 1024 * 1024
+LIMIT = 24 * 1024 * 1024
 F32 = jnp.float32
 BF16 = jnp.bfloat16
 

time: 112 us -> 97.2 us (0.87); the launches traced: 113 us -> 96.1 us
  Pallas kernels: 47.6 us -> 30.3 us
  waiting for transfers between devices: 18.1 us -> 20.3 us
    pallas_call x9, Pallas kernels: 47.6 us -> 30.3 us  [run(): pl.pallas_call(kernel, out_shape=[jax.ShapeDtypeStruct(s, d) for s, d in...]
    ppermute x15, waiting for transfers between devices: 14.4 us -> 17 us  [shift(): return lax.ppermute(value, ('x', 'yl'), pairs)]
    ppermute x15, starting transfers between devices: 23.4 us -> 21.4 us  [shift(): return lax.ppermute(value, ('x', 'yl'), pairs)]
    ppermute x6, starting transfers between devices: 6.18 us -> 8.03 us  [swap_core(): return lax.ppermute(value, 'c', [(0, 1), (1, 0)])]
    unnamed x50 -> x16, local copies, waits for them, and re-layouts: 4.15 us -> 3.34 us
  transfers between devices with their start and end apart: 22 -> 22, of which waited for: 8 -> 10; matrix products, arithmetic and copies ran while one was open for 1% -> 0% of each run, Pallas kernels for 17% -> 12%
where the time goes in v4:
time: 97.2 us; the launch traced here: 96.1 us
  starting transfers between devices  41 us (42%)
  Pallas kernels  30.3 us (31%)
  waiting for transfers between devices  20.3 us (21%)
  local copies, waits for them, and re-layouts  3.37 us (3%)
    pallas_call x9, Pallas kernels, run(): pl.pallas_call(kernel, out_shape=[jax.ShapeDtypeStruct(s, d) for s, d in...  30.3 us
    ppermute x15, starting transfers between devices, shift(): return lax.ppermute(value, ('x', 'yl'), pairs)  21.4 us
    ppermute x15, waiting for transfers between devices, shift(): return lax.ppermute(value, ('x', 'yl'), pairs)  17 us
    all_to_all x1, starting transfers between devices, on_device(): d_rows = lax.all_to_all(d_pack, ('x', 'yh', 'z'), 0, 0)  11.6 us
    ppermute x6, starting transfers between devices, swap_core(): return lax.ppermute(value, 'c', [(0, 1), (1, 0)])  8.03 us
    unnamed x16, local copies, waits for them, and re-layouts  3.34 us
    ppermute x6, waiting for transfers between devices, swap_core(): return lax.ppermute(value, 'c', [(0, 1), (1, 0)])  3.26 us
  transfers between devices with their start and end apart: 22, of which 10 were waited for; matrix products, arithmetic and copies ran while one was open for 0% of the time, Pallas kernels for 12%

profile of v4, /device:TPU:1, one launch (start us, length us, event | category | flops | bytes accessed | tf_op | source)
XLA Modules:
  0.0 96.1 jit_solution(11497405282972797950)
XLA Ops:
  0.7 1.0 %copy-done.1 = bf16[320,448]{1,0:T(8,128)(2,1)S(1)} copy-done((bf16[320,448]{1,0:T(8,128)(2,1)S(1)}, bf16[320,448]{1,0:T(8,128)(2,1)}, u32[]{:S(2)}) %copy-start.1) | copy-done | bytes 286744
  1.7 1.0 %copy-done.2 = bf16[320,448]{1,0:T(8,128)(2,1)S(1)} copy-done((bf16[320,448]{1,0:T(8,128)(2,1)S(1)}, bf16[320,448]{1,0:T(8,128)(2,1)}, u32[]{:S(2)}) %copy-start.2) | copy-done | bytes 286744
  2.6 0.7 copy-done.5
  3.3 1.2 %pack_kv.1 = (bf16[640,128]{1,0:T(8,128)(2,1)S(1)}, bf16[640,128]{1,0:T(8,128)(2,1)S(1)}, bf16[640,128]{1,0:T(8,128)(2,1)S(1)}, bf16[640,128]{1,0:T(8,128)(2,1)S(1)}) custom-call(s32[32]{0:T(128)S(1)} %copy-done.5, bf16[320,448]{1,0:T(8,128)(2,1)S(1)} %copy-done.1, bf16[320,448]{1,0:T(8,128)(2,1)S(1)} %copy-done.2), custom_call_target="tpu_custom_call" | custom-call | tf_op jit(solution)/shard_map/pack_kv/pallas_call | solution.py:42
  4.5 2.1 %collective-permute-start = (bf16[640,128]{1,0:T(8,128)(2,1)S(1)}, bf16[640,128]{1,0:T(8,128)(2,1)S(1)}, u32[]{:S(2)}, u32[]{:S(2)}) collective-permute-start(bf16[640,128]{1,0:T(8,128)(2,1)S(1)} %get-tuple-element.50), channel_id=1, source_target_pairs={{0,64},{32,96},{64,128},{96,160},{128,192},{160,224},{192,0},{224,... | collective-permute-start | bytes 491528 | tf_op jit(solution)/shard_map/ppermute | solution.py:346
  6.6 2.5 %collective-permute-start.1 = (bf16[640,128]{1,0:T(8,128)(2,1)S(1)}, bf16[640,128]{1,0:T(8,128)(2,1)S(1)}, u32[]{:S(2)}, u32[]{:S(2)}) collective-permute-start(bf16[640,128]{1,0:T(8,128)(2,1)S(1)} %get-tuple-element.51), channel_id=1, source_target_pairs={{0,128},{32,160},{64,192},{96,224},{128,0},{160,32},{192,64},{224,... | collective-permute-start | bytes 491528 | tf_op jit(solution)/shard_map/ppermute | solution.py:346
  9.0 1.2 %collective-permute-start.2 = (bf16[640,128]{1,0:T(8,128)(2,1)S(1)}, bf16[640,128]{1,0:T(8,128)(2,1)S(1)}, u32[]{:S(2)}, u32[]{:S(2)}) collective-permute-start(bf16[640,128]{1,0:T(8,128)(2,1)S(1)} %get-tuple-element.52), channel_id=1, source_target_pairs={{0,192},{32,224},{64,0},{96,32},{128,64},{160,96},{192,128},{224,1... | collective-permute-start | bytes 491528 | tf_op jit(solution)/shard_map/ppermute | solution.py:346
  10.2 1.3 %collective-permute-start.5 = (bf16[640,128]{1,0:T(8,128)(2,1)S(1)}, bf16[640,128]{1,0:T(8,128)(2,1)S(1)}, u32[]{:S(2)}, u32[]{:S(2)}) collective-permute-start(bf16[640,128]{1,0:T(8,128)(2,1)S(1)} %get-tuple-element.49.rest_4_.rest_0_), channel_id=1, source_target_pairs={{0,32},{32,0},{64,96},{96,64},{128,160},{160,128},{192,224},{224,1... | collective-permute-start | bytes 491528 | tf_op jit(solution)/shard_map/ppermute | solution.py:346
  11.5 1.0 %cotangent_pack.1 = bf16[64,20,128]{2,1,0:T(8,128)(2,1)} custom-call(bf16[20,7168]{1,0:T(8,128)(2,1)S(1)} %copy-done), custom_call_target="tpu_custom_call" | custom-call | tf_op jit(solution)/shard_map/cotangent_pack/pallas_call | solution.py:42
  12.5 11.6 %all-to-all-start = ((bf16[64,20,128]{2,1,0:T(8,128)(2,1)}), bf16[64,20,128]{2,1,0:T(8,128)(2,1)S(1)}, u32[]{:S(2)}, u32[]{:S(2)}) async-start(bf16[64,20,128]{2,1,0:T(8,128)(2,1)} %cotangent_pack.1), calls=%async_computation | async-start | bytes 786432 | tf_op jit(solution)/shard_map/all_to_all | solution.py:384
  25.3 1.0 %pack_qo.1 = (bf16[640,128]{1,0:T(8,128)(2,1)S(1)}, bf16[640,128]{1,0:T(8,128)(2,1)S(1)}, bf16[640,128]{1,0:T(8,128)(2,1)S(1)}, bf16[640,128]{1,0:T(8,128)(2,1)S(1)}) custom-call(s32[32]{0:T(128)S(1)} %copy-done.6, bf16[320,448]{1,0:T(8,128)(2,1)S(1)} %copy-done.3, bf16[320,448]{1,0:T(8,128)(2,1)S(1)} %copy-done.4, ...), custom_call_target="tpu_custom_call" | custom-call | tf_op jit(solution)/shard_map/pack_qo/pallas_call | solution.py:42
  26.3 1.1 %collective-permute-start.7 = (bf16[640,128]{1,0:T(8,128)(2,1)S(1)}, bf16[640,128]{1,0:T(8,128)(2,1)S(1)}, u32[]{:S(2)}, u32[]{:S(2)}) collective-permute-start(bf16[640,128]{1,0:T(8,128)(2,1)S(1)} %get-tuple-element.54), channel_id=1, source_target_pairs={{0,64},{32,96},{64,128},{96,160},{128,192},{160,224},{192,0},{224,... | collective-permute-start | bytes 491528 | tf_op jit(solution)/shard_map/ppermute | solution.py:346
  27.4 2.6 %collective-permute-start.8 = (bf16[640,128]{1,0:T(8,128)(2,1)S(1)}, bf16[640,128]{1,0:T(8,128)(2,1)S(1)}, u32[]{:S(2)}, u32[]{:S(2)}) collective-permute-start(bf16[640,128]{1,0:T(8,128)(2,1)S(1)} %get-tuple-element.55), channel_id=1, source_target_pairs={{0,128},{32,160},{64,192},{96,224},{128,0},{160,32},{192,64},{224,... | collective-permute-start | bytes 491528 | tf_op jit(solution)/shard_map/ppermute | solution.py:346
  30.0 1.1 %collective-permute-start.9 = (bf16[640,128]{1,0:T(8,128)(2,1)S(1)}, bf16[640,128]{1,0:T(8,128)(2,1)S(1)}, u32[]{:S(2)}, u32[]{:S(2)}) collective-permute-start(bf16[640,128]{1,0:T(8,128)(2,1)S(1)} %get-tuple-element.56), channel_id=1, source_target_pairs={{0,192},{32,224},{64,0},{96,32},{128,64},{160,96},{192,128},{224,1... | collective-permute-start | bytes 491528 | tf_op jit(solution)/shard_map/ppermute | solution.py:346
  31.1 3.3 %collective-permute-start.4 = (bf16[1920,128]{1,0:T(8,128)(2,1)S(1)}, bf16[1920,128]{1,0:T(8,128)(2,1)S(1)}, u32[]{:S(2)}, u32[]{:S(2)}) collective-permute-start(bf16[1920,128]{1,0:T(8,128)(2,1)S(1)} %constant_dynamic-update-slice_fusion.rest_0_.rest_5_.rest_1_), channel_id=1, source_target_pairs={{0,16},{16,0},{1,17},{17,1},{2,18},{18,2},{3,19},{19,3},{4,20},{20... | collective-permute-start | bytes 1474568 | tf_op jit(solution)/shard_map/ppermute | solution.py:350
  34.9 4.4 %collective-permute-done.8.rest_2_ = bf16[640,128]{1,0:T(8,128)(2,1)S(1)} collective-permute-done((bf16[640,128]{1,0:T(8,128)(2,1)S(1)}, bf16[640,128]{1,0:T(8,128)(2,1)S(1)}, u32[]{:S(2)}, u32[]{:S(2)}) %collective-permute-start.8) | collective-permute-done | bytes 163872 | tf_op jit(solution)/shard_map/ppermute | solution.py:346
  39.6 3.0 %collective-permute-start.11 = (bf16[1920,128]{1,0:T(8,128)(2,1)S(1)}, bf16[1920,128]{1,0:T(8,128)(2,1)S(1)}, u32[]{:S(2)}, u32[]{:S(2)}) collective-permute-start(bf16[1920,128]{1,0:T(8,128)(2,1)S(1)} %collective-permute-done.6.rest_9_.rest_5_), channel_id=1, source_target_pairs={{0,16},{16,0},{1,17},{17,1},{2,18},{18,2},{3,19},{19,3},{4,20},{20... | collective-permute-start | bytes 1474568 | tf_op jit(solution)/shard_map/ppermute | solution.py:350
  43.2 1.4 %collective-permute-done.3.rest_6_.rest_2_ = bf16[640,128]{1,0:T(8,128)(2,1)S(1)} collective-permute-done((bf16[640,128]{1,0:T(8,128)(2,1)S(1)}, bf16[640,128]{1,0:T(8,128)(2,1)S(1)}, u32[]{:S(2)}, u32[]{:S(2)}) %collective-permute-start.3) | collective-permute-done | bytes 163872 | tf_op jit(solution)/shard_map/ppermute | solution.py:350
  44.7 7.4 %stats.1 = (bf16[1536,128]{1,0:T(8,128)(2,1)S(1)}, bf16[6,128,256]{2,1,0:T(8,128)(2,1)S(1)}) custom-call(s32[4,32]{1,0:T(4,128)S(1)} %pad_add_fusion.rest_1_.tables, f32[1]{0:T(128)} %bitcast.4.slope, bf16[640,128]{1,0:T(8,128)(2,1)S(1)} %get-tuple-element.58.rest_0_, bf16[640,128]{1,0:T(8,128)(2,1)S(1)} %collective-permute-done.7.rest_1_, ...), custom_call_target="tpu_custom_call" | custom-call | tf_op jit(solution)/shard_map/stats/pallas_call | solution.py:42
  52.2 8.4 %grads_other.1 = (bf16[1536,128]{1,0:T(8,128)(2,1)S(1)}, bf16[6,128,256]{2,1,0:T(8,128)(2,1)S(1)}, f32[1536,128]{1,0:T(8,128)S(1)}, bf16[2560,128]{1,0:T(8,128)(2,1)S(1)}, bf16[2560,128]{1,0:T(8,128)(2,1)S(1)}) custom-call(s32[4,32]{1,0:T(4,128)S(1)} %pad_add_fusion.rest_1_.tables, bf16[640,128]{1,0:T(8,128)(2,1)S(1)} %get-tuple-element.58.rest_0_, ...), custom_call_target="tpu_custom_call" | custom-call | tf_op jit(solution)/shard_map/grads_other/pallas_call | solution.py:42
  61.0 1.7 %collective-permute-done.12.b = bf16[2560,128]{1,0:T(8,128)(2,1)S(1)} collective-permute-done((bf16[2560,128]{1,0:T(8,128)(2,1)S(1)}, bf16[2560,128]{1,0:T(8,128)(2,1)S(1)}, u32[]{:S(2)}, u32[]{:S(2)}) %collective-permute-start.12) | collective-permute-done | bytes 655392 | tf_op jit(solution)/shard_map/ppermute | solution.py:350
  62.9 2.5 %collective-permute-start.13 = (bf16[2560,128]{1,0:T(8,128)(2,1)S(1)}, bf16[2560,128]{1,0:T(8,128)(2,1)S(1)}, u32[]{:S(2)}, u32[]{:S(2)}) collective-permute-start(bf16[2560,128]{1,0:T(8,128)(2,1)S(1)} %add_other.1), channel_id=1, source_target_pairs={{0,32},{32,0},{64,96},{96,64},{128,160},{160,128},{192,224},{224,1... | collective-permute-start | bytes 1966088 | tf_op jit(solution)/shard_map/ppermute | solution.py:346
  65.5 9.3 %grads_own.1 = (bf16[320,128]{1,0:T(8,128)(2,1)S(1)}, bf16[320,128]{1,0:T(8,128)(2,1)S(1)}, bf16[320,128]{1,0:T(8,128)(2,1)S(1)}, bf16[320,128]{1,0:T(8,128)(2,1...) custom-call(s32[4,32]{1,0:T(4,128)S(1)} %pad_add_fusion.rest_1_.tables, ...), custom_call_target="tpu_custom_call" | custom-call | tf_op jit(solution)/shard_map/grads_own/pallas_call | solution.py:42
  74.7 0.7 collective-permute-start.17
  76.1 4.2 %collective-permute-done.13.c = bf16[2560,128]{1,0:T(8,128)(2,1)S(1)} collective-permute-done((bf16[2560,128]{1,0:T(8,128)(2,1)S(1)}, bf16[2560,128]{1,0:T(8,128)(2,1)S(1)}, u32[]{:S(2)}, u32[]{:S(2)}) %collective-permute-start.13) | collective-permute-done | bytes 655392 | tf_op jit(solution)/shard_map/ppermute | solution.py:346
  80.5 2.0 %collective-permute-start.18 = (bf16[640,128]{1,0:T(8,128)(2,1)S(1)}, bf16[640,128]{1,0:T(8,128)(2,1)S(1)}, u32[]{:S(2)}, u32[]{:S(2)}) collective-permute-start(bf16[640,128]{1,0:T(8,128)(2,1)S(1)} %get-tuple-element.84), channel_id=1, source_target_pairs={{0,192},{32,224},{64,0},{96,32},{128,64},{160,96},{192,128},{224,1... | collective-permute-start | bytes 491528 | tf_op jit(solution)/shard_map/ppermute | solution.py:346
  83.6 2.1 %collective-permute-start.14 = (bf16[320,128]{1,0:T(8,128)(2,1)S(1)}, bf16[320,128]{1,0:T(8,128)(2,1)S(1)}, u32[]{:S(2)}, u32[]{:S(2)}) collective-permute-start(bf16[320,128]{1,0:T(8,128)(2,1)S(1)} %get-tuple-element.77), channel_id=1, source_target_pairs={{0,192},{32,224},{64,0},{96,32},{128,64},{160,96},{192,128},{224,1... | collective-permute-start | bytes 245768 | tf_op jit(solution)/shard_map/ppermute | solution.py:346
  85.7 1.3 %collective-permute-start.15 = (bf16[320,128]{1,0:T(8,128)(2,1)S(1)}, bf16[320,128]{1,0:T(8,128)(2,1)S(1)}, u32[]{:S(2)}, u32[]{:S(2)}) collective-permute-start(bf16[320,128]{1,0:T(8,128)(2,1)S(1)} %get-tuple-element.78), channel_id=1, source_target_pairs={{0,128},{32,160},{64,192},{96,224},{128,0},{160,32},{192,64},{224,... | collective-permute-start | bytes 245768 | tf_op jit(solution)/shard_map/ppermute | solution.py:346
  87.0 4.1 %collective-permute-done.14.rest_1_ = bf16[320,128]{1,0:T(8,128)(2,1)S(1)} collective-permute-done((bf16[320,128]{1,0:T(8,128)(2,1)S(1)}, bf16[320,128]{1,0:T(8,128)(2,1)S(1)}, u32[]{:S(2)}, u32[]{:S(2)}) %collective-permute-start.14) | collective-permute-done | bytes 81952 | tf_op jit(solution)/shard_map/ppermute | solution.py:346
  91.1 2.5 %collective-permute-done.15.rest_2_ = bf16[320,128]{1,0:T(8,128)(2,1)S(1)} collective-permute-done((bf16[320,128]{1,0:T(8,128)(2,1)S(1)}, bf16[320,128]{1,0:T(8,128)(2,1)S(1)}, u32[]{:S(2)}, u32[]{:S(2)}) %collective-permute-start.15) | collective-permute-done | bytes 81952 | tf_op jit(solution)/shard_map/ppermute | solution.py:346
  93.6 0.9 collective-permute-done.20.rest_7_
  94.5 1.6 %unpack.1 = (bf16[320,448]{1,0:T(8,128)(2,1)}, bf16[320,448]{1,0:T(8,128)(2,1)}, bf16[320,448]{1,0:T(8,128)(2,1)}) custom-call(bf16[320,128]{1,0:T(8,128)(2,1)S(1)} %get-tuple-element.73.rest_0_, bf16[320,128]{1,0:T(8,128)(2,1)S(1)} %collective-permute-done.14.rest_1_, bf16[320,128]{1,0:T(8,128)(2,1)S(1)} %collective-permute-done.15.rest_2_, ...), custom_call_target="tpu_custom_call" | custom-call | tf_op jit(solution)/shard_map/unpack/pallas_call | solution.py:42
  (41 shorter events, 5.0 us)
Async XLA Ops:
  0.6 10.9 %copy-start = (bf16[20,7168]{1,0:T(8,128)(2,1)S(1)}, bf16[20,7168]{1,0:T(8,128)(2,1)}, u32[]{:S(2)}) copy-start(bf16[20,7168]{1,0:T(8,128)(2,1)} %d_ref) | copy-start | bytes 860164
  0.6 1.0 %copy-start.1 = (bf16[320,448]{1,0:T(8,128)(2,1)S(1)}, bf16[320,448]{1,0:T(8,128)(2,1)}, u32[]{:S(2)}) copy-start(bf16[320,448]{1,0:T(8,128)(2,1)} %a_ref.2) | copy-start | bytes 860164
  1.7 1.0 %copy-start.2 = (bf16[320,448]{1,0:T(8,128)(2,1)S(1)}, bf16[320,448]{1,0:T(8,128)(2,1)}, u32[]{:S(2)}) copy-start(bf16[320,448]{1,0:T(8,128)(2,1)} %b_ref.2) | copy-start | bytes 860164
  2.6 0.7 copy-start.5
  4.5 19.6 %collective-permute-start = (bf16[640,128]{1,0:T(8,128)(2,1)S(1)}, bf16[640,128]{1,0:T(8,128)(2,1)S(1)}, u32[]{:S(2)}, u32[]{:S(2)}) collective-permute-start(bf16[640,128]{1,0:T(8,128)(2,1)S(1)} %get-tuple-element.50), channel_id=1, source_target_pairs={{0,64},{32,96},{64,128},{96,160},{128,192},{160,224},{192,0},{224,... | collective-permute-start | bytes 491528 | tf_op jit(solution)/shard_map/ppermute | solution.py:346
  6.6 17.6 %collective-permute-start.1 = (bf16[640,128]{1,0:T(8,128)(2,1)S(1)}, bf16[640,128]{1,0:T(8,128)(2,1)S(1)}, u32[]{:S(2)}, u32[]{:S(2)}) collective-permute-start(bf16[640,128]{1,0:T(8,128)(2,1)S(1)} %get-tuple-element.51), channel_id=1, source_target_pairs={{0,128},{32,160},{64,192},{96,224},{128,0},{160,32},{192,64},{224,... | collective-permute-start | bytes 491528 | tf_op jit(solution)/shard_map/ppermute | solution.py:346
  9.0 15.2 %collective-permute-start.2 = (bf16[640,128]{1,0:T(8,128)(2,1)S(1)}, bf16[640,128]{1,0:T(8,128)(2,1)S(1)}, u32[]{:S(2)}, u32[]{:S(2)}) collective-permute-start(bf16[640,128]{1,0:T(8,128)(2,1)S(1)} %get-tuple-element.52), channel_id=1, source_target_pairs={{0,192},{32,224},{64,0},{96,32},{128,64},{160,96},{192,128},{224,1... | collective-permute-start | bytes 491528 | tf_op jit(solution)/shard_map/ppermute | solution.py:346
  10.2 20.9 %collective-permute-start.5 = (bf16[640,128]{1,0:T(8,128)(2,1)S(1)}, bf16[640,128]{1,0:T(8,128)(2,1)S(1)}, u32[]{:S(2)}, u32[]{:S(2)}) collective-permute-start(bf16[640,128]{1,0:T(8,128)(2,1)S(1)} %get-tuple-element.49.rest_4_.rest_0_), channel_id=1, source_target_pairs={{0,32},{32,0},{64,96},{96,64},{128,160},{160,128},{192,224},{224,1... | collective-permute-start | bytes 491528 | tf_op jit(solution)/shard_map/ppermute | solution.py:346
  12.5 26.8 %all-to-all-start = ((bf16[64,20,128]{2,1,0:T(8,128)(2,1)}), bf16[64,20,128]{2,1,0:T(8,128)(2,1)S(1)}, u32[]{:S(2)}, u32[]{:S(2)}) async-start(bf16[64,20,128]{2,1,0:T(8,128)(2,1)} %cotangent_pack.1), calls=%async_computation | async-start | bytes 786432 | tf_op jit(solution)/shard_map/all_to_all | solution.py:384
  24.1 1.1 %copy-start.3 = (bf16[320,448]{1,0:T(8,128)(2,1)S(1)}, bf16[320,448]{1,0:T(8,128)(2,1)}, u32[]{:S(2)}) copy-start(bf16[320,448]{1,0:T(8,128)(2,1)} %a_ref.3) | copy-start | bytes 860164
  24.1 1.1 %copy-start.4 = (bf16[320,448]{1,0:T(8,128)(2,1)S(1)}, bf16[320,448]{1,0:T(8,128)(2,1)}, u32[]{:S(2)}) copy-start(bf16[320,448]{1,0:T(8,128)(2,1)} %b_ref.3) | copy-start | bytes 860164
  24.2 15.4 %collective-permute-start.6 = (bf16[1920,128]{1,0:T(8,128)(2,1)S(1)}, bf16[1920,128]{1,0:T(8,128)(2,1)S(1)}, u32[]{:S(2)}, u32[]{:S(2)}) collective-permute-start(bf16[1920,128]{1,0:T(8,128)(2,1)S(1)} %constant_dynamic-update-slice_fusion.rest_0_.rest_5_.rest_1_), channel_id=1, source_target_pairs={{0,32},{32,0},{64,96},{96,64},{128,160},{160,128},{192,224},{224,1... | collective-permute-start | bytes 1474568 | tf_op jit(solution)/shard_map/ppermute | solution.py:346
  24.4 0.7 copy-start.6
  26.3 8.6 %collective-permute-start.7 = (bf16[640,128]{1,0:T(8,128)(2,1)S(1)}, bf16[640,128]{1,0:T(8,128)(2,1)S(1)}, u32[]{:S(2)}, u32[]{:S(2)}) collective-permute-start(bf16[640,128]{1,0:T(8,128)(2,1)S(1)} %get-tuple-element.54), channel_id=1, source_target_pairs={{0,64},{32,96},{64,128},{96,160},{128,192},{160,224},{192,0},{224,... | collective-permute-start | bytes 491528 | tf_op jit(solution)/shard_map/ppermute | solution.py:346
  27.4 12.0 %collective-permute-start.8 = (bf16[640,128]{1,0:T(8,128)(2,1)S(1)}, bf16[640,128]{1,0:T(8,128)(2,1)S(1)}, u32[]{:S(2)}, u32[]{:S(2)}) collective-permute-start(bf16[640,128]{1,0:T(8,128)(2,1)S(1)} %get-tuple-element.55), channel_id=1, source_target_pairs={{0,128},{32,160},{64,192},{96,224},{128,0},{160,32},{192,64},{224,... | collective-permute-start | bytes 491528 | tf_op jit(solution)/shard_map/ppermute | solution.py:346
  30.0 9.4 %collective-permute-start.9 = (bf16[640,128]{1,0:T(8,128)(2,1)S(1)}, bf16[640,128]{1,0:T(8,128)(2,1)S(1)}, u32[]{:S(2)}, u32[]{:S(2)}) collective-permute-start(bf16[640,128]{1,0:T(8,128)(2,1)S(1)} %get-tuple-element.56), channel_id=1, source_target_pairs={{0,192},{32,224},{64,0},{96,32},{128,64},{160,96},{192,128},{224,1... | collective-permute-start | bytes 491528 | tf_op jit(solution)/shard_map/ppermute | solution.py:346
  31.1 13.5 %collective-permute-start.4 = (bf16[1920,128]{1,0:T(8,128)(2,1)S(1)}, bf16[1920,128]{1,0:T(8,128)(2,1)S(1)}, u32[]{:S(2)}, u32[]{:S(2)}) collective-permute-start(bf16[1920,128]{1,0:T(8,128)(2,1)S(1)} %constant_dynamic-update-slice_fusion.rest_0_.rest_5_.rest_1_), channel_id=1, source_target_pairs={{0,16},{16,0},{1,17},{17,1},{2,18},{18,2},{3,19},{19,3},{4,20},{20... | collective-permute-start | bytes 1474568 | tf_op jit(solution)/shard_map/ppermute | solution.py:350
  39.6 5.1 %collective-permute-start.11 = (bf16[1920,128]{1,0:T(8,128)(2,1)S(1)}, bf16[1920,128]{1,0:T(8,128)(2,1)S(1)}, u32[]{:S(2)}, u32[]{:S(2)}) collective-permute-start(bf16[1920,128]{1,0:T(8,128)(2,1)S(1)} %collective-permute-done.6.rest_9_.rest_5_), channel_id=1, source_target_pairs={{0,16},{16,0},{1,17},{17,1},{2,18},{18,2},{3,19},{19,3},{4,20},{20... | collective-permute-start | bytes 1474568 | tf_op jit(solution)/shard_map/ppermute | solution.py:350
  42.6 2.0 %collective-permute-start.3 = (bf16[640,128]{1,0:T(8,128)(2,1)S(1)}, bf16[640,128]{1,0:T(8,128)(2,1)S(1)}, u32[]{:S(2)}, u32[]{:S(2)}) collective-permute-start(bf16[640,128]{1,0:T(8,128)(2,1)S(1)} %get-tuple-element.49.rest_4_.rest_0_), channel_id=1, source_target_pairs={{0,16},{16,0},{1,17},{17,1},{2,18},{18,2},{3,19},{19,3},{4,20},{20... | collective-permute-start | bytes 491528 | tf_op jit(solution)/shard_map/ppermute | solution.py:350
  42.6 2.1 %collective-permute-start.10 = (bf16[640,128]{1,0:T(8,128)(2,1)S(1)}, bf16[640,128]{1,0:T(8,128)(2,1)}, u32[]{:S(2)}, u32[]{:S(2)}) collective-permute-start(bf16[640,128]{1,0:T(8,128)(2,1)S(1)} %collective-permute-done.5.rest_8_.rest_4_), channel_id=1, source_target_pairs={{0,16},{16,0},{1,17},{17,1},{2,18},{18,2},{3,19},{19,3},{4,20},{20... | collective-permute-start | bytes 491528 | tf_op jit(solution)/shard_map/ppermute | solution.py:350
  60.6 2.2 %collective-permute-start.12 = (bf16[2560,128]{1,0:T(8,128)(2,1)S(1)}, bf16[2560,128]{1,0:T(8,128)(2,1)S(1)}, u32[]{:S(2)}, u32[]{:S(2)}) collective-permute-start(bf16[2560,128]{1,0:T(8,128)(2,1)S(1)} %get-tuple-element.71), channel_id=1, source_target_pairs={{0,16},{16,0},{1,17},{17,1},{2,18},{18,2},{3,19},{19,3},{4,20},{20... | collective-permute-start | bytes 1966088 | tf_op jit(solution)/shard_map/ppermute | solution.py:350
  62.9 17.3 %collective-permute-start.13 = (bf16[2560,128]{1,0:T(8,128)(2,1)S(1)}, bf16[2560,128]{1,0:T(8,128)(2,1)S(1)}, u32[]{:S(2)}, u32[]{:S(2)}) collective-permute-start(bf16[2560,128]{1,0:T(8,128)(2,1)S(1)} %add_other.1), channel_id=1, source_target_pairs={{0,32},{32,0},{64,96},{96,64},{128,160},{160,128},{192,224},{224,1... | collective-permute-start | bytes 1966088 | tf_op jit(solution)/shard_map/ppermute | solution.py:346
  74.7 5.5 %collective-permute-start.17 = (bf16[2560,128]{1,0:T(8,128)(2,1)S(1)}, bf16[2560,128]{1,0:T(8,128)(2,1)S(1)}, u32[]{:S(2)}, u32[]{:S(2)}) collective-permute-start(bf16[2560,128]{1,0:T(8,128)(2,1)S(1)} %get-tuple-element.81), channel_id=1, source_target_pairs={{0,16},{16,0},{1,17},{17,1},{2,18},{18,2},{3,19},{19,3},{4,20},{20... | collective-permute-start | bytes 1966088 | tf_op jit(solution)/shard_map/ppermute | solution.py:350
  75.4 10.2 %collective-permute-start.16 = (bf16[320,128]{1,0:T(8,128)(2,1)S(1)}, bf16[320,128]{1,0:T(8,128)(2,1)S(1)}, u32[]{:S(2)}, u32[]{:S(2)}) collective-permute-start(bf16[320,128]{1,0:T(8,128)(2,1)S(1)} %get-tuple-element.79), channel_id=1, source_target_pairs={{0,64},{32,96},{64,128},{96,160},{128,192},{160,224},{192,0},{224,... | collective-permute-start | bytes 245768 | tf_op jit(solution)/shard_map/ppermute | solution.py:346
  80.5 13.0 %collective-permute-start.18 = (bf16[640,128]{1,0:T(8,128)(2,1)S(1)}, bf16[640,128]{1,0:T(8,128)(2,1)S(1)}, u32[]{:S(2)}, u32[]{:S(2)}) collective-permute-start(bf16[640,128]{1,0:T(8,128)(2,1)S(1)} %get-tuple-element.84), channel_id=1, source_target_pairs={{0,192},{32,224},{64,0},{96,32},{128,64},{160,96},{192,128},{224,1... | collective-permute-start | bytes 491528 | tf_op jit(solution)/shard_map/ppermute | solution.py:346
  82.5 11.0 %collective-permute-start.19 = (bf16[640,128]{1,0:T(8,128)(2,1)S(1)}, bf16[640,128]{1,0:T(8,128)(2,1)S(1)}, u32[]{:S(2)}, u32[]{:S(2)}) collective-permute-start(bf16[640,128]{1,0:T(8,128)(2,1)S(1)} %get-tuple-element.85), channel_id=1, source_target_pairs={{0,128},{32,160},{64,192},{96,224},{128,0},{160,32},{192,64},{224,... | collective-permute-start | bytes 491528 | tf_op jit(solution)/shard_map/ppermute | solution.py:346
  83.0 11.5 %collective-permute-start.20 = (bf16[640,128]{1,0:T(8,128)(2,1)S(1)}, bf16[640,128]{1,0:T(8,128)(2,1)S(1)}, u32[]{:S(2)}, u32[]{:S(2)}) collective-permute-start(bf16[640,128]{1,0:T(8,128)(2,1)S(1)} %get-tuple-element.86), channel_id=1, source_target_pairs={{0,64},{32,96},{64,128},{96,160},{128,192},{160,224},{192,0},{224,... | collective-permute-start | bytes 491528 | tf_op jit(solution)/shard_map/ppermute | solution.py:346
  83.6 7.5 %collective-permute-start.14 = (bf16[320,128]{1,0:T(8,128)(2,1)S(1)}, bf16[320,128]{1,0:T(8,128)(2,1)S(1)}, u32[]{:S(2)}, u32[]{:S(2)}) collective-permute-start(bf16[320,128]{1,0:T(8,128)(2,1)S(1)} %get-tuple-element.77), channel_id=1, source_target_pairs={{0,192},{32,224},{64,0},{96,32},{128,64},{160,96},{192,128},{224,1... | collective-permute-start | bytes 245768 | tf_op jit(solution)/shard_map/ppermute | solution.py:346
  85.7 7.9 %collective-permute-start.15 = (bf16[320,128]{1,0:T(8,128)(2,1)S(1)}, bf16[320,128]{1,0:T(8,128)(2,1)S(1)}, u32[]{:S(2)}, u32[]{:S(2)}) collective-permute-start(bf16[320,128]{1,0:T(8,128)(2,1)S(1)} %get-tuple-element.78), channel_id=1, source_target_pairs={{0,128},{32,160},{64,192},{96,224},{128,0},{160,32},{192,64},{224,... | collective-permute-start | bytes 245768 | tf_op jit(solution)/shard_map/ppermute | solution.py:346

commit v5 on v4

--- a/solution.py
+++ b/solution.py
@@ -315,15 +315,32 @@
             dqo[s][h * BLK : (h + 1) * BLK, :] = (dq[rows, :] * SCALE).astype(BF16)
 
 
+def fold(total, out):
+    rows = total.shape[0] // 8
+    out[...] = total[: 7 * rows, :]
+    for i in range(7):
+        out[i * rows : (i + 1) * rows, HD:] = total[7 * rows :, i * 16 : (i + 1) * 16]
+
+
+def unfold(folded, out):
+    rows = folded.shape[0] // 7
+    out[: 7 * rows, :] = folded[...]
+    for i in range(7):
+        out[7 * rows :, i * 16 : (i + 1) * 16] = folded[i * rows : (i + 1) * rows, HD:]
+
+
 def add_kernel(a, b, out):
-    out[...] = (a[...].astype(F32) + b[...].astype(F32)).astype(BF16)
-
-
-def add_own_kernel(a, b, c, *outs):
+    fold((a[...].astype(F32) + b[...].astype(F32)).astype(BF16), out)
+
+
+def add_own_kernel(a, b, folded, *rest):
+    outs, c = rest[0:4], rest[4]
+    c[:, HD:] = jnp.zeros((NX * 2 * OWN, W - HD), BF16)
+    unfold(folded, c)
     for s in range(NX):
         rows = slice(s * 2 * OWN, (s + 1) * 2 * OWN)
         total = a[rows, :].astype(F32) + b[rows, :].astype(F32) + c[rows, :].astype(F32)
-        outs[s][...] = total.astype(BF16)
+        fold(total.astype(BF16), outs[s])
 
 
 def unpack_kernel(*rest):
@@ -332,7 +349,7 @@
     for s in range(NX):
         head = lax.rem(x + s, NX)
         buf[head, :OWN, :] = dqs[s][...]
-        buf[head, OWN:, :] = dkvs[s][...]
+        unfold(dkvs[s], buf.at[head, OWN:, :])
     for n in range(NX):
         for i in range(3):
             outs[i][:, n * HD : (n + 1) * HD] = buf[n, i * OWN : (i + 1) * OWN, :HD]
@@ -409,7 +426,7 @@
         accs + [pltpu.VMEM((QROWS, W), BF16)] * 2 + [limits],
         "grads_other",
     )(tables, *qo, *kv_y, *kv_yc, d_rows, qs, qt)
-    (dkv_y,) = call(add_kernel, [stack], [], "add_other")(keep, swap_core(send))
+    (dkv_y,) = call(add_kernel, [((NX * 2 * OWN // 8 * 7, W), BF16)], [], "add_other")(keep, swap_core(send))
     dq, dkv_y = lax.optimization_barrier((dq, dkv_y))
     dkv_y = shift(dkv_y, 0, True)
 
@@ -422,7 +439,12 @@
     dqs[1], dqs[2], dkv_y = lax.optimization_barrier((dqs[1], dqs[2], dkv_y))
     swapped = swap_core(send)
     dqs = [dqs[0]] + [shift(dqs[s], -s) for s in (1, 2, 3)]
-    dkvs = call(add_own_kernel, [piece] * 4, [], "add_own")(keep, swapped, dkv_y)
+    dkvs = call(
+        add_own_kernel,
+        [((2 * OWN // 8 * 7, W), BF16)] * 4,
+        [pltpu.VMEM((NX * 2 * OWN, W), BF16)],
+        "add_own",
+    )(keep, swapped, dkv_y)
     dkvs = [dkvs[0]] + [shift(dkvs[s], -s) for s in (1, 2, 3)]
     return tuple(
         call(

time: 97.2 us -> 106 us (1.091); the launches traced: 96.1 us -> 107 us
  waiting for transfers between devices: 20.3 us -> 27.8 us
  starting transfers between devices: 41 us -> 47.4 us
  Pallas kernels: 30.3 us -> 27 us
    ppermute x15, waiting for transfers between devices: 17 us -> 24.5 us  [shift(): return lax.ppermute(value, ('x', 'yl'), pairs)]
    ppermute x6, starting transfers between devices: 8.03 us -> 12.9 us  [swap_core(): return lax.ppermute(value, 'c', [(0, 1), (1, 0)])]
    pallas_call x9, Pallas kernels: 30.3 us -> 27 us  [run(): pl.pallas_call(kernel, out_shape=[jax.ShapeDtypeStruct(s, d) for s, d in...]
    ppermute x15, starting transfers between devices: 21.4 us -> 22.9 us  [shift(): return lax.ppermute(value, ('x', 'yl'), pairs)]
  transfers between devices with their start and end apart: 22 -> 22, of which waited for: 10 -> 10; matrix products, arithmetic and copies ran while one was open for 0% -> 0% of each run, Pallas kernels for 12% -> 3%
where the time goes in v5:
time: 106 us; the launch traced here: 107 us
  starting transfers between devices  47.4 us (45%)
  waiting for transfers between devices  27.8 us (26%)
  Pallas kernels  27 us (25%)
  local copies, waits for them, and re-layouts  3.37 us (3%)
    pallas_call x9, Pallas kernels, run(): pl.pallas_call(kernel, out_shape=[jax.ShapeDtypeStruct(s, d) for s, d in...  27 us
    ppermute x15, waiting for transfers between devices, shift(): return lax.ppermute(value, ('x', 'yl'), pairs)  24.5 us
    ppermute x15, starting transfers between devices, shift(): return lax.ppermute(value, ('x', 'yl'), pairs)  22.9 us
    ppermute x6, starting transfers between devices, swap_core(): return lax.ppermute(value, 'c', [(0, 1), (1, 0)])  12.9 us
    all_to_all x1, starting transfers between devices, on_device(): d_rows = lax.all_to_all(d_pack, ('x', 'yh', 'z'), 0, 0)  11.6 us
    unnamed x16, local copies, waits for them, and re-layouts  3.34 us
    ppermute x6, waiting for transfers between devices, swap_core(): return lax.ppermute(value, 'c', [(0, 1), (1, 0)])  3.26 us
  transfers between devices with their start and end apart: 22, of which 10 were waited for; matrix products, arithmetic and copies ran while one was open for 0% of the time, Pallas kernels for 3%

profile of v5, /device:TPU:1, one launch (start us, length us, event | category | flops | bytes accessed | tf_op | source)
XLA Modules:
  0.0 106.7 jit_solution(11034198103302419758)
XLA Ops:
  0.7 1.0 copy-done.1
  1.7 1.0 copy-done.2
  3.3 1.2 %pack_kv.1 = (bf16[640,128]{1,0:T(8,128)(2,1)S(1)}, bf16[640,128]{1,0:T(8,128)(2,1)S(1)}, bf16[640,128]{1,0:T(8,128)(2,1)S(1)}, bf16[640,128]{1,0:T(8,128)(2,1)S(1)}) custom-call(s32[32]{0:T(128)S(1)} %copy-done.5, bf16[320,448]{1,0:T(8,128)(2,1)S(1)} %copy-done.1, bf16[320,448]{1,0:T(8,128)(2,1)S(1)} %copy-done.2), custom_call_target="tpu_custom_call" | custom-call | tf_op jit(solution)/shard_map/pack_kv/pallas_call | solution.py:42
  4.5 2.1 %collective-permute-start = (bf16[640,128]{1,0:T(8,128)(2,1)S(1)}, bf16[640,128]{1,0:T(8,128)(2,1)S(1)}, u32[]{:S(2)}, u32[]{:S(2)}) collective-permute-start(bf16[640,128]{1,0:T(8,128)(2,1)S(1)} %get-tuple-element.50), channel_id=1, source_target_pairs={{0,64},{32,96},{64,128},{96,160},{128,192},{160,224},{192,0},{224,... | collective-permute-start | bytes 491528 | tf_op jit(solution)/shard_map/ppermute | solution.py:363
  6.6 2.5 %collective-permute-start.1 = (bf16[640,128]{1,0:T(8,128)(2,1)S(1)}, bf16[640,128]{1,0:T(8,128)(2,1)S(1)}, u32[]{:S(2)}, u32[]{:S(2)}) collective-permute-start(bf16[640,128]{1,0:T(8,128)(2,1)S(1)} %get-tuple-element.51), channel_id=1, source_target_pairs={{0,128},{32,160},{64,192},{96,224},{128,0},{160,32},{192,64},{224,... | collective-permute-start | bytes 491528 | tf_op jit(solution)/shard_map/ppermute | solution.py:363
  9.0 1.2 %collective-permute-start.2 = (bf16[640,128]{1,0:T(8,128)(2,1)S(1)}, bf16[640,128]{1,0:T(8,128)(2,1)S(1)}, u32[]{:S(2)}, u32[]{:S(2)}) collective-permute-start(bf16[640,128]{1,0:T(8,128)(2,1)S(1)} %get-tuple-element.52), channel_id=1, source_target_pairs={{0,192},{32,224},{64,0},{96,32},{128,64},{160,96},{192,128},{224,1... | collective-permute-start | bytes 491528 | tf_op jit(solution)/shard_map/ppermute | solution.py:363
  10.2 1.3 %collective-permute-start.5 = (bf16[640,128]{1,0:T(8,128)(2,1)S(1)}, bf16[640,128]{1,0:T(8,128)(2,1)S(1)}, u32[]{:S(2)}, u32[]{:S(2)}) collective-permute-start(bf16[640,128]{1,0:T(8,128)(2,1)S(1)} %get-tuple-element.49.rest_4_.rest_0_), channel_id=1, source_target_pairs={{0,32},{32,0},{64,96},{96,64},{128,160},{160,128},{192,224},{224,1... | collective-permute-start | bytes 491528 | tf_op jit(solution)/shard_map/ppermute | solution.py:363
  11.5 1.0 cotangent_pack.1
  12.5 11.6 %all-to-all-start = ((bf16[64,20,128]{2,1,0:T(8,128)(2,1)}), bf16[64,20,128]{2,1,0:T(8,128)(2,1)S(1)}, u32[]{:S(2)}, u32[]{:S(2)}) async-start(bf16[64,20,128]{2,1,0:T(8,128)(2,1)} %cotangent_pack.1), calls=%async_computation | async-start | bytes 786432 | tf_op jit(solution)/shard_map/all_to_all | solution.py:401
  25.3 1.0 pack_qo.1
  26.3 1.1 %collective-permute-start.7 = (bf16[640,128]{1,0:T(8,128)(2,1)S(1)}, bf16[640,128]{1,0:T(8,128)(2,1)S(1)}, u32[]{:S(2)}, u32[]{:S(2)}) collective-permute-start(bf16[640,128]{1,0:T(8,128)(2,1)S(1)} %get-tuple-element.54), channel_id=1, source_target_pairs={{0,64},{32,96},{64,128},{96,160},{128,192},{160,224},{192,0},{224,... | collective-permute-start | bytes 491528 | tf_op jit(solution)/shard_map/ppermute | solution.py:363
  27.4 2.6 %collective-permute-start.8 = (bf16[640,128]{1,0:T(8,128)(2,1)S(1)}, bf16[640,128]{1,0:T(8,128)(2,1)S(1)}, u32[]{:S(2)}, u32[]{:S(2)}) collective-permute-start(bf16[640,128]{1,0:T(8,128)(2,1)S(1)} %get-tuple-element.55), channel_id=1, source_target_pairs={{0,128},{32,160},{64,192},{96,224},{128,0},{160,32},{192,64},{224,... | collective-permute-start | bytes 491528 | tf_op jit(solution)/shard_map/ppermute | solution.py:363
  30.0 1.1 %collective-permute-start.9 = (bf16[640,128]{1,0:T(8,128)(2,1)S(1)}, bf16[640,128]{1,0:T(8,128)(2,1)S(1)}, u32[]{:S(2)}, u32[]{:S(2)}) collective-permute-start(bf16[640,128]{1,0:T(8,128)(2,1)S(1)} %get-tuple-element.56), channel_id=1, source_target_pairs={{0,192},{32,224},{64,0},{96,32},{128,64},{160,96},{192,128},{224,1... | collective-permute-start | bytes 491528 | tf_op jit(solution)/shard_map/ppermute | solution.py:363
  31.1 3.3 %collective-permute-start.4 = (bf16[1920,128]{1,0:T(8,128)(2,1)S(1)}, bf16[1920,128]{1,0:T(8,128)(2,1)S(1)}, u32[]{:S(2)}, u32[]{:S(2)}) collective-permute-start(bf16[1920,128]{1,0:T(8,128)(2,1)S(1)} %constant_dynamic-update-slice_fusion.rest_0_.rest_5_.rest_1_), channel_id=1, source_target_pairs={{0,16},{16,0},{1,17},{17,1},{2,18},{18,2},{3,19},{19,3},{4,20},{20... | collective-permute-start | bytes 1474568 | tf_op jit(solution)/shard_map/ppermute | solution.py:367
  34.9 4.4 %collective-permute-done.8.rest_2_ = bf16[640,128]{1,0:T(8,128)(2,1)S(1)} collective-permute-done((bf16[640,128]{1,0:T(8,128)(2,1)S(1)}, bf16[640,128]{1,0:T(8,128)(2,1)S(1)}, u32[]{:S(2)}, u32[]{:S(2)}) %collective-permute-start.8) | collective-permute-done | bytes 163872 | tf_op jit(solution)/shard_map/ppermute | solution.py:363
  39.6 3.0 %collective-permute-start.11 = (bf16[1920,128]{1,0:T(8,128)(2,1)S(1)}, bf16[1920,128]{1,0:T(8,128)(2,1)S(1)}, u32[]{:S(2)}, u32[]{:S(2)}) collective-permute-start(bf16[1920,128]{1,0:T(8,128)(2,1)S(1)} %collective-permute-done.6.rest_9_.rest_5_), channel_id=1, source_target_pairs={{0,16},{16,0},{1,17},{17,1},{2,18},{18,2},{3,19},{19,3},{4,20},{20... | collective-permute-start | bytes 1474568 | tf_op jit(solution)/shard_map/ppermute | solution.py:367
  43.2 1.4 %collective-permute-done.3.rest_6_.rest_2_ = bf16[640,128]{1,0:T(8,128)(2,1)S(1)} collective-permute-done((bf16[640,128]{1,0:T(8,128)(2,1)S(1)}, bf16[640,128]{1,0:T(8,128)(2,1)S(1)}, u32[]{:S(2)}, u32[]{:S(2)}) %collective-permute-start.3) | collective-permute-done | bytes 163872 | tf_op jit(solution)/shard_map/ppermute | solution.py:367
  44.7 6.5 %stats.1 = (bf16[1536,128]{1,0:T(8,128)(2,1)S(1)}, bf16[6,128,256]{2,1,0:T(8,128)(2,1)S(1)}) custom-call(s32[4,32]{1,0:T(4,128)S(1)} %pad_add_fusion.rest_1_.tables, f32[1]{0:T(128)} %bitcast.4.slope, bf16[640,128]{1,0:T(8,128)(2,1)S(1)} %get-tuple-element.58.rest_0_, bf16[640,128]{1,0:T(8,128)(2,1)S(1)} %collective-permute-done.7.rest_1_, ...), custom_call_target="tpu_custom_call" | custom-call | tf_op jit(solution)/shard_map/stats/pallas_call | solution.py:42
  51.2 6.8 %grads_other.1 = (bf16[1536,128]{1,0:T(8,128)(2,1)S(1)}, bf16[6,128,256]{2,1,0:T(8,128)(2,1)S(1)}, f32[1536,128]{1,0:T(8,128)S(1)}, bf16[2560,128]{1,0:T(8,128)(2,1)S(1)}, bf16[2560,128]{1,0:T(8,128)(2,1)S(1)}) custom-call(s32[4,32]{1,0:T(4,128)S(1)} %pad_add_fusion.rest_1_.tables, bf16[640,128]{1,0:T(8,128)(2,1)S(1)} %get-tuple-element.58.rest_0_, ...), custom_call_target="tpu_custom_call" | custom-call | tf_op jit(solution)/shard_map/grads_other/pallas_call | solution.py:42
  58.0 4.0 %collective-permute-start.12 = (bf16[2560,128]{1,0:T(8,128)(2,1)S(1)}, bf16[2560,128]{1,0:T(8,128)(2,1)S(1)}, u32[]{:S(2)}, u32[]{:S(2)}) collective-permute-start(bf16[2560,128]{1,0:T(8,128)(2,1)S(1)} %get-tuple-element.71), channel_id=1, source_target_pairs={{0,16},{16,0},{1,17},{17,1},{2,18},{18,2},{3,19},{19,3},{4,20},{20... | collective-permute-start | bytes 1966088 | tf_op jit(solution)/shard_map/ppermute | solution.py:367
  62.0 1.7 %collective-permute-done.12.b = bf16[2560,128]{1,0:T(8,128)(2,1)S(1)} collective-permute-done((bf16[2560,128]{1,0:T(8,128)(2,1)S(1)}, bf16[2560,128]{1,0:T(8,128)(2,1)S(1)}, u32[]{:S(2)}, u32[]{:S(2)}) %collective-permute-start.12) | collective-permute-done | bytes 655392 | tf_op jit(solution)/shard_map/ppermute | solution.py:367
  64.1 7.6 %grads_own.1 = (bf16[320,128]{1,0:T(8,128)(2,1)S(1)}, bf16[320,128]{1,0:T(8,128)(2,1)S(1)}, bf16[320,128]{1,0:T(8,128)(2,1)S(1)}, bf16[320,128]{1,0:T(8,128)(2,1...) custom-call(s32[4,32]{1,0:T(4,128)S(1)} %pad_add_fusion.rest_1_.tables, ...), custom_call_target="tpu_custom_call" | custom-call | tf_op jit(solution)/shard_map/grads_own/pallas_call | solution.py:42
  71.8 2.1 %collective-permute-start.17 = (bf16[2560,128]{1,0:T(8,128)(2,1)S(1)}, bf16[2560,128]{1,0:T(8,128)(2,1)S(1)}, u32[]{:S(2)}, u32[]{:S(2)}) collective-permute-start(bf16[2560,128]{1,0:T(8,128)(2,1)S(1)} %get-tuple-element.81), channel_id=1, source_target_pairs={{0,16},{16,0},{1,17},{17,1},{2,18},{18,2},{3,19},{19,3},{4,20},{20... | collective-permute-start | bytes 1966088 | tf_op jit(solution)/shard_map/ppermute | solution.py:367
  73.9 4.0 %collective-permute-start.13 = (bf16[2240,128]{1,0:T(8,128)(2,1)S(1)}, bf16[2240,128]{1,0:T(8,128)(2,1)S(1)}, u32[]{:S(2)}, u32[]{:S(2)}) collective-permute-start(bf16[2240,128]{1,0:T(8,128)(2,1)S(1)} %add_other.1), channel_id=1, source_target_pairs={{0,32},{32,0},{64,96},{96,64},{128,160},{160,128},{192,224},{224,1... | collective-permute-start | bytes 1720328 | tf_op jit(solution)/shard_map/ppermute | solution.py:363
  78.5 12.6 %collective-permute-done.13.folded = bf16[2240,128]{1,0:T(8,128)(2,1)S(1)} collective-permute-done((bf16[2240,128]{1,0:T(8,128)(2,1)S(1)}, bf16[2240,128]{1,0:T(8,128)(2,1)S(1)}, u32[]{:S(2)}, u32[]{:S(2)}) %collective-permute-start.13) | collective-permute-done | bytes 573472 | tf_op jit(solution)/shard_map/ppermute | solution.py:363
  91.9 2.0 %collective-permute-start.18 = (bf16[560,128]{1,0:T(8,128)(2,1)S(1)}, bf16[560,128]{1,0:T(8,128)(2,1)S(1)}, u32[]{:S(2)}, u32[]{:S(2)}) collective-permute-start(bf16[560,128]{1,0:T(8,128)(2,1)S(1)} %get-tuple-element.84), channel_id=1, source_target_pairs={{0,192},{32,224},{64,0},{96,32},{128,64},{160,96},{192,128},{224,1... | collective-permute-start | bytes 430088 | tf_op jit(solution)/shard_map/ppermute | solution.py:363
  94.9 2.1 %collective-permute-start.14 = (bf16[320,128]{1,0:T(8,128)(2,1)S(1)}, bf16[320,128]{1,0:T(8,128)(2,1)S(1)}, u32[]{:S(2)}, u32[]{:S(2)}) collective-permute-start(bf16[320,128]{1,0:T(8,128)(2,1)S(1)} %get-tuple-element.77), channel_id=1, source_target_pairs={{0,192},{32,224},{64,0},{96,32},{128,64},{160,96},{192,128},{224,1... | collective-permute-start | bytes 245768 | tf_op jit(solution)/shard_map/ppermute | solution.py:363
  97.0 1.3 %collective-permute-start.15 = (bf16[320,128]{1,0:T(8,128)(2,1)S(1)}, bf16[320,128]{1,0:T(8,128)(2,1)S(1)}, u32[]{:S(2)}, u32[]{:S(2)}) collective-permute-start(bf16[320,128]{1,0:T(8,128)(2,1)S(1)} %get-tuple-element.78), channel_id=1, source_target_pairs={{0,128},{32,160},{64,192},{96,224},{128,0},{160,32},{192,64},{224,... | collective-permute-start | bytes 245768 | tf_op jit(solution)/shard_map/ppermute | solution.py:363
  98.3 4.0 %collective-permute-done.14.rest_1_ = bf16[320,128]{1,0:T(8,128)(2,1)S(1)} collective-permute-done((bf16[320,128]{1,0:T(8,128)(2,1)S(1)}, bf16[320,128]{1,0:T(8,128)(2,1)S(1)}, u32[]{:S(2)}, u32[]{:S(2)}) %collective-permute-start.14) | collective-permute-done | bytes 81952 | tf_op jit(solution)/shard_map/ppermute | solution.py:363
  102.3 1.9 %collective-permute-done.15.rest_2_ = bf16[320,128]{1,0:T(8,128)(2,1)S(1)} collective-permute-done((bf16[320,128]{1,0:T(8,128)(2,1)S(1)}, bf16[320,128]{1,0:T(8,128)(2,1)S(1)}, u32[]{:S(2)}, u32[]{:S(2)}) %collective-permute-start.15) | collective-permute-done | bytes 81952 | tf_op jit(solution)/shard_map/ppermute | solution.py:363
  104.2 0.8 collective-permute-done.20.rest_7_
  105.0 1.8 %unpack.1 = (bf16[320,448]{1,0:T(8,128)(2,1)}, bf16[320,448]{1,0:T(8,128)(2,1)}, bf16[320,448]{1,0:T(8,128)(2,1)}) custom-call(bf16[320,128]{1,0:T(8,128)(2,1)S(1)} %get-tuple-element.73.rest_0_, bf16[320,128]{1,0:T(8,128)(2,1)S(1)} %collective-permute-done.14.rest_1_, bf16[320,128]{1,0:T(8,128)(2,1)S(1)} %collective-permute-done.15.rest_2_, ...), custom_call_target="tpu_custom_call" | custom-call | tf_op jit(solution)/shard_map/unpack/pallas_call | solution.py:42
  (41 shorter events, 5.9 us)
Async XLA Ops:
  0.6 10.9 %copy-start = (bf16[20,7168]{1,0:T(8,128)(2,1)S(1)}, bf16[20,7168]{1,0:T(8,128)(2,1)}, u32[]{:S(2)}) copy-start(bf16[20,7168]{1,0:T(8,128)(2,1)} %d_ref) | copy-start | bytes 860164
  0.6 1.0 copy-start.1
  1.7 1.0 copy-start.2
  2.6 0.7 copy-start.5
  4.5 19.6 %collective-permute-start = (bf16[640,128]{1,0:T(8,128)(2,1)S(1)}, bf16[640,128]{1,0:T(8,128)(2,1)S(1)}, u32[]{:S(2)}, u32[]{:S(2)}) collective-permute-start(bf16[640,128]{1,0:T(8,128)(2,1)S(1)} %get-tuple-element.50), channel_id=1, source_target_pairs={{0,64},{32,96},{64,128},{96,160},{128,192},{160,224},{192,0},{224,... | collective-permute-start | bytes 491528 | tf_op jit(solution)/shard_map/ppermute | solution.py:363
  6.6 17.6 %collective-permute-start.1 = (bf16[640,128]{1,0:T(8,128)(2,1)S(1)}, bf16[640,128]{1,0:T(8,128)(2,1)S(1)}, u32[]{:S(2)}, u32[]{:S(2)}) collective-permute-start(bf16[640,128]{1,0:T(8,128)(2,1)S(1)} %get-tuple-element.51), channel_id=1, source_target_pairs={{0,128},{32,160},{64,192},{96,224},{128,0},{160,32},{192,64},{224,... | collective-permute-start | bytes 491528 | tf_op jit(solution)/shard_map/ppermute | solution.py:363
  9.0 15.2 %collective-permute-start.2 = (bf16[640,128]{1,0:T(8,128)(2,1)S(1)}, bf16[640,128]{1,0:T(8,128)(2,1)S(1)}, u32[]{:S(2)}, u32[]{:S(2)}) collective-permute-start(bf16[640,128]{1,0:T(8,128)(2,1)S(1)} %get-tuple-element.52), channel_id=1, source_target_pairs={{0,192},{32,224},{64,0},{96,32},{128,64},{160,96},{192,128},{224,1... | collective-permute-start | bytes 491528 | tf_op jit(solution)/shard_map/ppermute | solution.py:363
  10.2 20.9 %collective-permute-start.5 = (bf16[640,128]{1,0:T(8,128)(2,1)S(1)}, bf16[640,128]{1,0:T(8,128)(2,1)S(1)}, u32[]{:S(2)}, u32[]{:S(2)}) collective-permute-start(bf16[640,128]{1,0:T(8,128)(2,1)S(1)} %get-tuple-element.49.rest_4_.rest_0_), channel_id=1, source_target_pairs={{0,32},{32,0},{64,96},{96,64},{128,160},{160,128},{192,224},{224,1... | collective-permute-start | bytes 491528 | tf_op jit(solution)/shard_map/ppermute | solution.py:363
  12.5 26.8 %all-to-all-start = ((bf16[64,20,128]{2,1,0:T(8,128)(2,1)}), bf16[64,20,128]{2,1,0:T(8,128)(2,1)S(1)}, u32[]{:S(2)}, u32[]{:S(2)}) async-start(bf16[64,20,128]{2,1,0:T(8,128)(2,1)} %cotangent_pack.1), calls=%async_computation | async-start | bytes 786432 | tf_op jit(solution)/shard_map/all_to_all | solution.py:401
  24.1 1.1 %copy-start.3 = (bf16[320,448]{1,0:T(8,128)(2,1)S(1)}, bf16[320,448]{1,0:T(8,128)(2,1)}, u32[]{:S(2)}) copy-start(bf16[320,448]{1,0:T(8,128)(2,1)} %a_ref.3) | copy-start | bytes 860164
  24.1 1.1 %copy-start.4 = (bf16[320,448]{1,0:T(8,128)(2,1)S(1)}, bf16[320,448]{1,0:T(8,128)(2,1)}, u32[]{:S(2)}) copy-start(bf16[320,448]{1,0:T(8,128)(2,1)} %b_ref.3) | copy-start | bytes 860164
  24.2 15.4 %collective-permute-start.6 = (bf16[1920,128]{1,0:T(8,128)(2,1)S(1)}, bf16[1920,128]{1,0:T(8,128)(2,1)S(1)}, u32[]{:S(2)}, u32[]{:S(2)}) collective-permute-start(bf16[1920,128]{1,0:T(8,128)(2,1)S(1)} %constant_dynamic-update-slice_fusion.rest_0_.rest_5_.rest_1_), channel_id=1, source_target_pairs={{0,32},{32,0},{64,96},{96,64},{128,160},{160,128},{192,224},{224,1... | collective-permute-start | bytes 1474568 | tf_op jit(solution)/shard_map/ppermute | solution.py:363
  24.4 0.7 copy-start.6
  26.3 8.6 %collective-permute-start.7 = (bf16[640,128]{1,0:T(8,128)(2,1)S(1)}, bf16[640,128]{1,0:T(8,128)(2,1)S(1)}, u32[]{:S(2)}, u32[]{:S(2)}) collective-permute-start(bf16[640,128]{1,0:T(8,128)(2,1)S(1)} %get-tuple-element.54), channel_id=1, source_target_pairs={{0,64},{32,96},{64,128},{96,160},{128,192},{160,224},{192,0},{224,... | collective-permute-start | bytes 491528 | tf_op jit(solution)/shard_map/ppermute | solution.py:363
  27.4 12.0 %collective-permute-start.8 = (bf16[640,128]{1,0:T(8,128)(2,1)S(1)}, bf16[640,128]{1,0:T(8,128)(2,1)S(1)}, u32[]{:S(2)}, u32[]{:S(2)}) collective-permute-start(bf16[640,128]{1,0:T(8,128)(2,1)S(1)} %get-tuple-element.55), channel_id=1, source_target_pairs={{0,128},{32,160},{64,192},{96,224},{128,0},{160,32},{192,64},{224,... | collective-permute-start | bytes 491528 | tf_op jit(solution)/shard_map/ppermute | solution.py:363
  30.0 9.4 %collective-permute-start.9 = (bf16[640,128]{1,0:T(8,128)(2,1)S(1)}, bf16[640,128]{1,0:T(8,128)(2,1)S(1)}, u32[]{:S(2)}, u32[]{:S(2)}) collective-permute-start(bf16[640,128]{1,0:T(8,128)(2,1)S(1)} %get-tuple-element.56), channel_id=1, source_target_pairs={{0,192},{32,224},{64,0},{96,32},{128,64},{160,96},{192,128},{224,1... | collective-permute-start | bytes 491528 | tf_op jit(solution)/shard_map/ppermute | solution.py:363
  31.1 13.5 %collective-permute-start.4 = (bf16[1920,128]{1,0:T(8,128)(2,1)S(1)}, bf16[1920,128]{1,0:T(8,128)(2,1)S(1)}, u32[]{:S(2)}, u32[]{:S(2)}) collective-permute-start(bf16[1920,128]{1,0:T(8,128)(2,1)S(1)} %constant_dynamic-update-slice_fusion.rest_0_.rest_5_.rest_1_), channel_id=1, source_target_pairs={{0,16},{16,0},{1,17},{17,1},{2,18},{18,2},{3,19},{19,3},{4,20},{20... | collective-permute-start | bytes 1474568 | tf_op jit(solution)/shard_map/ppermute | solution.py:367
  39.6 5.1 %collective-permute-start.11 = (bf16[1920,128]{1,0:T(8,128)(2,1)S(1)}, bf16[1920,128]{1,0:T(8,128)(2,1)S(1)}, u32[]{:S(2)}, u32[]{:S(2)}) collective-permute-start(bf16[1920,128]{1,0:T(8,128)(2,1)S(1)} %collective-permute-done.6.rest_9_.rest_5_), channel_id=1, source_target_pairs={{0,16},{16,0},{1,17},{17,1},{2,18},{18,2},{3,19},{19,3},{4,20},{20... | collective-permute-start | bytes 1474568 | tf_op jit(solution)/shard_map/ppermute | solution.py:367
  42.6 2.0 %collective-permute-start.3 = (bf16[640,128]{1,0:T(8,128)(2,1)S(1)}, bf16[640,128]{1,0:T(8,128)(2,1)S(1)}, u32[]{:S(2)}, u32[]{:S(2)}) collective-permute-start(bf16[640,128]{1,0:T(8,128)(2,1)S(1)} %get-tuple-element.49.rest_4_.rest_0_), channel_id=1, source_target_pairs={{0,16},{16,0},{1,17},{17,1},{2,18},{18,2},{3,19},{19,3},{4,20},{20... | collective-permute-start | bytes 491528 | tf_op jit(solution)/shard_map/ppermute | solution.py:367
  42.6 2.1 %collective-permute-start.10 = (bf16[640,128]{1,0:T(8,128)(2,1)S(1)}, bf16[640,128]{1,0:T(8,128)(2,1)}, u32[]{:S(2)}, u32[]{:S(2)}) collective-permute-start(bf16[640,128]{1,0:T(8,128)(2,1)S(1)} %collective-permute-done.5.rest_8_.rest_4_), channel_id=1, source_target_pairs={{0,16},{16,0},{1,17},{17,1},{2,18},{18,2},{3,19},{19,3},{4,20},{20... | collective-permute-start | bytes 491528 | tf_op jit(solution)/shard_map/ppermute | solution.py:367
  58.0 5.7 %collective-permute-start.12 = (bf16[2560,128]{1,0:T(8,128)(2,1)S(1)}, bf16[2560,128]{1,0:T(8,128)(2,1)S(1)}, u32[]{:S(2)}, u32[]{:S(2)}) collective-permute-start(bf16[2560,128]{1,0:T(8,128)(2,1)S(1)} %get-tuple-element.71), channel_id=1, source_target_pairs={{0,16},{16,0},{1,17},{17,1},{2,18},{18,2},{3,19},{19,3},{4,20},{20... | collective-permute-start | bytes 1966088 | tf_op jit(solution)/shard_map/ppermute | solution.py:367
  71.8 19.3 %collective-permute-start.17 = (bf16[2560,128]{1,0:T(8,128)(2,1)S(1)}, bf16[2560,128]{1,0:T(8,128)(2,1)S(1)}, u32[]{:S(2)}, u32[]{:S(2)}) collective-permute-start(bf16[2560,128]{1,0:T(8,128)(2,1)S(1)} %get-tuple-element.81), channel_id=1, source_target_pairs={{0,16},{16,0},{1,17},{17,1},{2,18},{18,2},{3,19},{19,3},{4,20},{20... | collective-permute-start | bytes 1966088 | tf_op jit(solution)/shard_map/ppermute | solution.py:367
  73.9 17.2 %collective-permute-start.13 = (bf16[2240,128]{1,0:T(8,128)(2,1)S(1)}, bf16[2240,128]{1,0:T(8,128)(2,1)S(1)}, u32[]{:S(2)}, u32[]{:S(2)}) collective-permute-start(bf16[2240,128]{1,0:T(8,128)(2,1)S(1)} %add_other.1), channel_id=1, source_target_pairs={{0,32},{32,0},{64,96},{96,64},{128,160},{160,128},{192,224},{224,1... | collective-permute-start | bytes 1720328 | tf_op jit(solution)/shard_map/ppermute | solution.py:363
  77.9 19.1 %collective-permute-start.16 = (bf16[320,128]{1,0:T(8,128)(2,1)S(1)}, bf16[320,128]{1,0:T(8,128)(2,1)S(1)}, u32[]{:S(2)}, u32[]{:S(2)}) collective-permute-start(bf16[320,128]{1,0:T(8,128)(2,1)S(1)} %get-tuple-element.79), channel_id=1, source_target_pairs={{0,64},{32,96},{64,128},{96,160},{128,192},{160,224},{192,0},{224,... | collective-permute-start | bytes 245768 | tf_op jit(solution)/shard_map/ppermute | solution.py:363
  91.9 12.3 %collective-permute-start.18 = (bf16[560,128]{1,0:T(8,128)(2,1)S(1)}, bf16[560,128]{1,0:T(8,128)(2,1)S(1)}, u32[]{:S(2)}, u32[]{:S(2)}) collective-permute-start(bf16[560,128]{1,0:T(8,128)(2,1)S(1)} %get-tuple-element.84), channel_id=1, source_target_pairs={{0,192},{32,224},{64,0},{96,32},{128,64},{160,96},{192,128},{224,1... | collective-permute-start | bytes 430088 | tf_op jit(solution)/shard_map/ppermute | solution.py:363
  93.9 10.3 %collective-permute-start.19 = (bf16[560,128]{1,0:T(8,128)(2,1)S(1)}, bf16[560,128]{1,0:T(8,128)(2,1)S(1)}, u32[]{:S(2)}, u32[]{:S(2)}) collective-permute-start(bf16[560,128]{1,0:T(8,128)(2,1)S(1)} %get-tuple-element.85), channel_id=1, source_target_pairs={{0,128},{32,160},{64,192},{96,224},{128,0},{160,32},{192,64},{224,... | collective-permute-start | bytes 430088 | tf_op jit(solution)/shard_map/ppermute | solution.py:363
  94.3 10.6 %collective-permute-start.20 = (bf16[560,128]{1,0:T(8,128)(2,1)S(1)}, bf16[560,128]{1,0:T(8,128)(2,1)S(1)}, u32[]{:S(2)}, u32[]{:S(2)}) collective-permute-start(bf16[560,128]{1,0:T(8,128)(2,1)S(1)} %get-tuple-element.86), channel_id=1, source_target_pairs={{0,64},{32,96},{64,128},{96,160},{128,192},{160,224},{192,0},{224,... | collective-permute-start | bytes 430088 | tf_op jit(solution)/shard_map/ppermute | solution.py:363
  94.9 7.4 %collective-permute-start.14 = (bf16[320,128]{1,0:T(8,128)(2,1)S(1)}, bf16[320,128]{1,0:T(8,128)(2,1)S(1)}, u32[]{:S(2)}, u32[]{:S(2)}) collective-permute-start(bf16[320,128]{1,0:T(8,128)(2,1)S(1)} %get-tuple-element.77), channel_id=1, source_target_pairs={{0,192},{32,224},{64,0},{96,32},{128,64},{160,96},{192,128},{224,1... | collective-permute-start | bytes 245768 | tf_op jit(solution)/shard_map/ppermute | solution.py:363
  97.0 7.2 %collective-permute-start.15 = (bf16[320,128]{1,0:T(8,128)(2,1)S(1)}, bf16[320,128]{1,0:T(8,128)(2,1)S(1)}, u32[]{:S(2)}, u32[]{:S(2)}) collective-permute-start(bf16[320,128]{1,0:T(8,128)(2,1)S(1)} %get-tuple-element.78), channel_id=1, source_target_pairs={{0,128},{32,160},{64,192},{96,224},{128,0},{160,32},{192,64},{224,... | collective-permute-start | bytes 245768 | tf_op jit(solution)/shard_map/ppermute | solution.py:363
